TPU v7x, 32 devices: a whole 2x2x4 slice. The times are simulated.
32 devices in a mesh: ens: 2 (over y), gx: 4 (over z), gy: 2 (over x), gz: 2 (over core).
Axes of the slice: x: 2, y: 2, z: 4, core: 2. Of those that a mesh axis runs over, the one named last changes fastest.
Arguments:
- ocean_temp: float32 [128, 128, 512], P(('ens', 'gz'), 'gx', 'gy'), parts along dimension 0, may hold values from -6 to 6
- bathy_levels: int32 [256, 512], P(('ens', 'gx'), 'gy'), parts along dimension 0, may hold values from 0 to 64
- mixing: float32 [256, 512], P(('ens', 'gx'), 'gy'), parts along dimension 0, may hold values from 0.02 to 0.3
- atm_flux: bfloat16 [128, 2, 128], P(('ens', 'gx', 'gy')), parts along dimension 0, may hold values from -6 to 6
- send_tiles: int32 [8, 8, 1], replicated, may hold values from -1 to 7, as said below
- regrid_slots: int32 [2, 1024], P(None, ('gx', 'gy', 'gz')), may hold values from 0 to 63, as said below
- regrid_weights: bfloat16 [1024, 128, 128], P(('gx', 'gy', 'gz'))
Outputs:
- ocean_final: float32 [128, 128, 512], P(('ens', 'gz'), 'gx', 'gy'), parts along dimension 0
- atm_surface: float32 [128, 128], P(('ens', 'gx', 'gy')), parts along dimension 0
There are 2 independent parts, one for each index of `ens`. A program takes and returns all parts, laid end to end along the dimension named above; an argument that names none is the same for every part. Nothing has to cross between parts.
Inputs may be any that keep to these rules, and one draw needn't show every extreme that they name: send_tiles[b, d, c] is the atmosphere tile of block b sent to block d in slot c, -1 where nothing is sent; a block sends at most 1 tiles to one destination, and each block receives 4 tiles. `regrid_slots`: row 0 holds the received position b * 1 + c of each slot, always a sent position, and every position sent to a block is named by some slot of it; row 1 the destination ocean tile.
All inputs are finite; a program needn't handle non-finite values.
Results may differ from a plain program's by a relative error of at most 0.00044.
Values may be sent and summed in bfloat16 or wider, within the bound.
No kernel may reach another device: no remote copies, remote signals or barrier semaphores. Data moves between devices by JAX's collectives and lax.ppermute only.
A program may use at most 64 MiB of HBM per device.

v0:
```python
import jax
import jax.numpy as jnp
from jax import lax
from jax.sharding import PartitionSpec as P

STEPS = 4


def extended(block, sides, width):
    for axis, dim in sides:
        count = lax.axis_size(axis)
        forward = [(i, i + 1) for i in range(count - 1)]
        backward = [(target, source) for source, target in forward]
        low = lax.ppermute(
            lax.slice_in_dim(block, block.shape[dim] - width, None, axis=dim), axis, forward
        )
        high = lax.ppermute(lax.slice_in_dim(block, 0, width, axis=dim), axis, backward)
        block = jnp.concatenate([low, block, high], axis=dim)
    return block


def broadcast(block, axis, holder):
    block = jnp.where(lax.axis_index(axis) == holder, block, jnp.zeros_like(block))
    return lax.psum(block, axis)


def wet_levels(levels_float, first_level, level_count):
    level_index = (first_level + jnp.arange(level_count)).astype(jnp.float32)[:, None, None]
    inside = (level_index >= 0.0) & (level_index < levels_float[None])
    return jnp.where(inside, 1.0, 0.0).astype(jnp.float32)


def level_forcing(surface, first_level, level_count, total_levels):
    level_index = (first_level + jnp.arange(level_count)).astype(jnp.float32)[:, None, None]
    top_only = jnp.where(level_index == 0.0, 1.0, 0.0).astype(jnp.float32)
    depth_share = jnp.exp(-4.0 * level_index / total_levels)
    return top_only * surface[0][None] + depth_share * surface[1][None]


def advance(padded_temp, padded_wet, mixing, forcing):
    center = padded_temp[1:-1, 1:-1, 1:-1]
    water_indicator = padded_wet[1:-1, 1:-1, 1:-1]
    lateral = (padded_temp[1:-1, 2:, 1:-1] - center) * padded_wet[1:-1, 2:, 1:-1]
    lateral = lateral + (padded_temp[1:-1, :-2, 1:-1] - center) * padded_wet[1:-1, :-2, 1:-1]
    lateral = lateral + (padded_temp[1:-1, 1:-1, 2:] - center) * padded_wet[1:-1, 1:-1, 2:]
    lateral = lateral + (padded_temp[1:-1, 1:-1, :-2] - center) * padded_wet[1:-1, 1:-1, :-2]
    vertical = (padded_temp[2:, 1:-1, 1:-1] - center) * padded_wet[2:, 1:-1, 1:-1]
    vertical = vertical + (padded_temp[:-2, 1:-1, 1:-1] - center) * padded_wet[:-2, 1:-1, 1:-1]
    return center + water_indicator * (0.1 * lateral + mixing * vertical + 0.1 * forcing)


def outgoing_tiles(my_sends, atm_flux):
    own_tiles = atm_flux.shape[0]
    chooser = (my_sends.reshape(-1)[:, None] == jnp.arange(own_tiles)[None, :]).astype(jnp.bfloat16)
    flat_flux = atm_flux.reshape(own_tiles, atm_flux.shape[1] * atm_flux.shape[2])
    return jnp.dot(chooser, flat_flux, preferred_element_type=jnp.float32).astype(jnp.bfloat16)


def per_device(
    ocean_temp, bathy_levels, mixing, atm_flux, send_tiles, regrid_slots, regrid_weights
):
    layers, row_count, columns = ocean_temp.shape
    total_levels = layers * lax.axis_size("gz")
    first_level = lax.axis_index("gz") * layers
    gx_count = lax.axis_size("gx")
    gy_count = lax.axis_size("gy")
    number_partitions = gx_count * gy_count
    self_block = lax.axis_index("gx") * gy_count + lax.axis_index("gy")
    own_tiles, fields, tile_atm = atm_flux.shape
    caps = send_tiles.shape[2]
    slot_count, unused_rows, patch_marine = regrid_weights.shape
    number_patches = row_count * columns // patch_marine
    position = regrid_slots[0]
    target_patch = regrid_slots[1]
    my_sends = send_tiles[self_block]
    outgoing = outgoing_tiles(my_sends, atm_flux).reshape(
        number_partitions, caps, fields * tile_atm
    )
    incoming = lax.all_to_all(outgoing, ("gx", "gy"), split_axis=0, concat_axis=0, tiled=True)
    picked = incoming.reshape(number_partitions * caps, fields, tile_atm)[position]
    contrib = jnp.einsum("kfa,kao->kfo", picked, regrid_weights, preferred_element_type=jnp.float32)
    collect = (target_patch[None, :] == jnp.arange(number_patches)[:, None]).astype(jnp.float32)
    summed = jnp.dot(
        collect, contrib.reshape(slot_count, fields * patch_marine), precision=lax.Precision.HIGHEST
    )
    partial_surface = (
        summed.reshape(number_patches, fields, patch_marine)
        .transpose(1, 0, 2)
        .reshape(fields, row_count, columns)
    )
    surface = lax.psum(partial_surface, "gz")
    levels_float = bathy_levels.astype(jnp.float32)
    coast = extended(levels_float.astype(jnp.bfloat16), (("gx", 0), ("gy", 1)), 1).astype(
        levels_float.dtype
    )
    padded_wet = wet_levels(coast, first_level - 1, layers + 2)
    forcing = level_forcing(surface, first_level, layers, total_levels)
    current_reading = ocean_temp
    for section in range(STEPS):
        padded = extended(current_reading, (("gx", 1), ("gy", 2), ("gz", 0)), 1)
        current_reading = advance(padded, padded_wet, mixing, forcing)
    topmost_water_points = jnp.where(levels_float > 0.0, 1.0, 0.0).astype(jnp.float32)
    mine_skin_heat = (current_reading[0] * topmost_water_points).astype(jnp.bfloat16)
    skin_heat_grid = broadcast(mine_skin_heat, "gz", 0)
    chosen_patch = skin_heat_grid.reshape(number_patches, patch_marine)[target_patch]
    back = jnp.einsum(
        "kao,ko->ka", regrid_weights, chosen_patch, preferred_element_type=jnp.float32
    )
    placer = (jnp.arange(number_partitions * caps)[:, None] == position[None, :]).astype(
        jnp.float32
    )
    buffer = jnp.dot(placer, back, precision=lax.Precision.HIGHEST).reshape(
        number_partitions, caps, tile_atm
    )
    returned = lax.all_to_all(buffer, ("gx", "gy"), split_axis=0, concat_axis=0, tiled=True)
    gatherer = (jnp.arange(own_tiles)[:, None] == my_sends.reshape(-1)[None, :]).astype(jnp.float32)
    mine = jnp.dot(
        gatherer,
        returned.reshape(number_partitions * caps, tile_atm),
        precision=lax.Precision.HIGHEST,
    )
    atm_surface = lax.psum(mine, "gz")
    return (current_reading, atm_surface)


def solution(mesh):
    return jax.shard_map(
        per_device,
        mesh=mesh,
        in_specs=(
            P(("ens", "gz"), "gx", "gy"),
            P(("ens", "gx"), "gy"),
            P(("ens", "gx"), "gy"),
            P(("ens", "gx", "gy"), None, None),
            P(),
            P(None, ("gx", "gy", "gz")),
            P(("gx", "gy", "gz"), None, None),
        ),
        out_specs=(P(("ens", "gz"), "gx", "gy"), P(("ens", "gx", "gy"), None)),
        check_vma=False,
    )
```

profile of v0, /device:TPU:1, one launch (start us, length us, event | category | flops | bytes accessed | tf_op | source)
XLA Modules:
  0.0 227.3 jit_solution(3960870352798912044)
XLA Ops:
  8.1 4.0 %collective-permute-start = (bf16[1,256]{1,0:T(2,128)(2,1)S(1)}, bf16[1,256]{1,0:T(2,128)(2,1)S(1)}, u32[]{:S(2)}, u32[]{:S(2)}) collective-permute-start(bf16[1,256]{1,0:T(2,128)(2,1)S(1)} %get-tuple-element.36), channel_id=1, source_target_pairs={{0,4},{4,8},{8,12},{1,5},{5,9},{9,13},{2,6},{6,10},{10,14},{3,7},{... | collective-permute-start | bytes 1544 | tf_op jit(solution)/shard_map/ppermute | solution.py:14
  12.1 1.3 collective-permute-start.1
  16.8 6.3 %all-to-all-start = ((bf16[8,2,128]{2,1,0:T(2,128)(2,1)}), bf16[8,2,128]{2,1,0:T(2,128)(2,1)S(1)}, u32[]{:S(2)}, u32[]{:S(2)}) async-start(bf16[8,2,128]{2,1,0:T(2,128)(2,1)} %reshape.163), calls=%async_computation | async-start | bytes 8192 | tf_op jit(solution)/shard_map/all_to_all | solution.py:79
  24.2 1.3 collective-permute-start.4
  25.5 4.0 %collective-permute-start.5 = (f32[32,1,256]{2,0,1:T(8,128)S(1)}, f32[32,1,256]{2,0,1:T(8,128)S(1)}, u32[]{:S(2)}, u32[]{:S(2)}) collective-permute-start(f32[32,1,256]{2,0,1:T(8,128)S(1)} %copy.258), channel_id=1, source_target_pairs={{0,4},{4,8},{8,12},{1,5},{5,9},{9,13},{2,6},{6,10},{10,14},{3,7},{... | collective-permute-start | bytes 98312 | tf_op jit(solution)/shard_map/ppermute | solution.py:14
  30.8 1.3 slice_bitcast_fusion.3
  32.8 3.3 %collective-permute-start.2 = (bf16[34,1]{1,0:T(8,128)(2,1)S(1)}, bf16[34,1]{1,0:T(8,128)(2,1)S(1)}, u32[]{:S(2)}, u32[]{:S(2)}) collective-permute-start(bf16[34,1]{1,0:T(8,128)(2,1)S(1)} %get-tuple-element.34), channel_id=1, source_target_pairs={{0,2},{1,3},{4,6},{5,7},{8,10},{9,11},{12,14},{13,15},{16,18},{17,... | collective-permute-start | bytes 212 | tf_op jit(solution)/shard_map/ppermute | solution.py:14
  36.1 1.3 collective-permute-start.3
  37.5 3.1 %collective-permute-done.3 = bf16[34,1]{1,0:T(8,128)(2,1)S(1)} collective-permute-done((bf16[34,1]{1,0:T(8,128)(2,1)S(1)}, bf16[34,1]{1,0:T(8,128)(2,1)S(1)}, u32[]{:S(2)}, u32[]{:S(2)}) %collective-permute-start.3) | collective-permute-done | bytes 100 | tf_op jit(solution)/shard_map/ppermute | solution.py:17
  40.7 1.7 and_select_fusion
  45.3 1.4 copy.208
  46.7 1.3 collective-permute-start.6
  48.0 1.4 copy.210
  49.4 4.0 %collective-permute-start.7 = (f32[32,34,1]{1,0,2:T(8,128)S(1)}, f32[32,34,1]{1,0,2:T(8,128)S(1)}, u32[]{:S(2)}, u32[]{:S(2)}) collective-permute-start(f32[32,34,1]{1,0,2:T(8,128)S(1)} %copy.210), channel_id=1, source_target_pairs={{0,2},{1,3},{4,6},{5,7},{8,10},{9,11},{12,14},{13,15},{16,18},{17,... | collective-permute-start | bytes 13064 | tf_op jit(solution)/shard_map/ppermute | solution.py:14
  57.5 6.3 %collective-permute-start.8 = (f32[1,34,258]{2,1,0:T(8,128)S(1)}, f32[1,34,258]{2,1,0:T(8,128)S(1)}, u32[]{:S(2)}, u32[]{:S(2)}) collective-permute-start(f32[1,34,258]{2,1,0:T(8,128)S(1)} %get-tuple-element.14), channel_id=1, source_target_pairs={{1,0},{3,2},{5,4},{7,6},{9,8},{11,10},{13,12},{15,14},{17,16},{19,... | collective-permute-start | bytes 105272 | tf_op jit(solution)/shard_map/ppermute | solution.py:17
  63.7 1.3 collective-permute-start.9
  65.0 10.2 %all-reduce.2.cloned.1.call-done = f32[2,32,256]{2,1,0:T(8,128)} async-done(((f32[2,32,256]{2,1,0:T(8,128)}), f32[2,32,256]{2,1,0:T(8,128)}) %all-reduce.2.cloned.1.call-update) | async-done | bytes 65552 | tf_op jit(solution)/shard_map/psum | solution.py:91
  76.0 12.8 %fusion.74 = f32[32,32,256]{2,1,0:T(8,128)S(1)} fusion(f32[32,32,256]{2,1,0:T(8,128)} %param.7, f32[1,34,258]{2,1,0:T(8,128)S(1)} %collective-permute-done.9, f32[32,34,1]{2,1,0:T(8,128)} %copy.209, f32[32,34,1]{2,1,0:T(8,128)} %copy.211, f32[32,1,256]{2,1,0:T(1,128)S(1)} %copy.203, f32[32,1,256]{2,1,0:T(1,128)S(1)} %copy.205, ...), kind=kLoop, calls=%fused_computation.138 | loop fusion | flops 11534336 | bytes 9680160 | tf_op jit(solution)/shard_map/add | solution.py:49
  88.9 1.3 collective-permute-start.10
  90.2 4.1 %collective-permute-start.11 = (f32[32,1,256]{2,0,1:T(8,128)S(1)}, f32[32,1,256]{2,0,1:T(8,128)S(1)}, u32[]{:S(2)}, u32[]{:S(2)}) collective-permute-start(f32[32,1,256]{2,0,1:T(8,128)S(1)} %copy.220), channel_id=1, source_target_pairs={{0,4},{4,8},{8,12},{1,5},{5,9},{9,13},{2,6},{6,10},{10,14},{3,7},{... | collective-permute-start | bytes 98312 | tf_op jit(solution)/shard_map/ppermute | solution.py:14
  96.8 1.4 copy.224
  98.2 1.3 collective-permute-start.12
  99.5 1.4 copy.226
  100.9 4.0 %collective-permute-start.13 = (f32[32,34,1]{1,0,2:T(8,128)S(1)}, f32[32,34,1]{1,0,2:T(8,128)S(1)}, u32[]{:S(2)}, u32[]{:S(2)}) collective-permute-start(f32[32,34,1]{1,0,2:T(8,128)S(1)} %copy.226), channel_id=1, source_target_pairs={{0,2},{1,3},{4,6},{5,7},{8,10},{9,11},{12,14},{13,15},{16,18},{17,... | collective-permute-start | bytes 13064 | tf_op jit(solution)/shard_map/ppermute | solution.py:14
  108.3 4.0 %collective-permute-start.14 = (f32[1,34,258]{2,1,0:T(8,128)S(1)}, f32[1,34,258]{2,1,0:T(8,128)S(1)}, u32[]{:S(2)}, u32[]{:S(2)}) collective-permute-start(f32[1,34,258]{2,1,0:T(8,128)S(1)} %get-tuple-element.12), channel_id=1, source_target_pairs={{1,0},{3,2},{5,4},{7,6},{9,8},{11,10},{13,12},{15,14},{17,16},{19,... | collective-permute-start | bytes 105272 | tf_op jit(solution)/shard_map/ppermute | solution.py:17
  112.3 1.3 collective-permute-start.15
  113.6 1.8 collective-permute-done.15
  115.5 9.1 %fusion.52 = f32[32,32,256]{2,1,0:T(8,128)S(1)} fusion(f32[32,32,256]{2,1,0:T(8,128)} %copy-done.4, f32[1,34,258]{2,1,0:T(8,128)S(1)} %collective-permute-done.15, f32[32,34,1]{2,1,0:T(8,128)} %copy.225, f32[32,34,1]{2,1,0:T(8,128)} %copy.227, f32[32,1,256]{2,1,0:T(1,128)S(1)} %copy.219, f32[32,1,256]{2,1,0:T(1,128)S(1)} %copy.221, ...), kind=kLoop, calls=%fused_computation.98 | loop fusion | flops 11534336 | bytes 9680160 | tf_op jit(solution)/shard_map/add | solution.py:49
  124.7 1.3 collective-permute-start.16
  126.0 4.6 %collective-permute-start.17 = (f32[32,1,256]{2,0,1:T(8,128)S(1)}, f32[32,1,256]{2,0,1:T(8,128)S(1)}, u32[]{:S(2)}, u32[]{:S(2)}) collective-permute-start(f32[32,1,256]{2,0,1:T(8,128)S(1)} %copy.232), channel_id=1, source_target_pairs={{0,4},{4,8},{8,12},{1,5},{5,9},{9,13},{2,6},{6,10},{10,14},{3,7},{... | collective-permute-start | bytes 98312 | tf_op jit(solution)/shard_map/ppermute | solution.py:14
  133.0 1.4 copy.236
  135.7 1.4 copy.238
  137.1 4.0 %collective-permute-start.19 = (f32[32,34,1]{1,0,2:T(8,128)S(1)}, f32[32,34,1]{1,0,2:T(8,128)S(1)}, u32[]{:S(2)}, u32[]{:S(2)}) collective-permute-start(f32[32,34,1]{1,0,2:T(8,128)S(1)} %copy.238), channel_id=1, source_target_pairs={{0,2},{1,3},{4,6},{5,7},{8,10},{9,11},{12,14},{13,15},{16,18},{17,... | collective-permute-start | bytes 13064 | tf_op jit(solution)/shard_map/ppermute | solution.py:14
  144.5 3.7 %collective-permute-start.20 = (f32[1,34,258]{2,1,0:T(8,128)S(1)}, f32[1,34,258]{2,1,0:T(8,128)S(1)}, u32[]{:S(2)}, u32[]{:S(2)}) collective-permute-start(f32[1,34,258]{2,1,0:T(8,128)S(1)} %get-tuple-element.10), channel_id=1, source_target_pairs={{1,0},{3,2},{5,4},{7,6},{9,8},{11,10},{13,12},{15,14},{17,16},{19,... | collective-permute-start | bytes 105272 | tf_op jit(solution)/shard_map/ppermute | solution.py:17
  148.2 1.5 collective-permute-start.21
  149.7 1.7 collective-permute-done.21
  151.4 9.1 %fusion.30 = f32[32,32,256]{2,1,0:T(8,128)S(1)} fusion(f32[32,32,256]{2,1,0:T(8,128)} %copy-done.3, f32[1,34,258]{2,1,0:T(8,128)S(1)} %collective-permute-done.21, f32[32,34,1]{2,1,0:T(8,128)} %copy.237, f32[32,34,1]{2,1,0:T(8,128)} %copy.239, f32[32,1,256]{2,1,0:T(1,128)S(1)} %copy.231, f32[32,1,256]{2,1,0:T(1,128)S(1)} %copy.233, ...), kind=kLoop, calls=%fused_computation.58 | loop fusion | flops 11534336 | bytes 9680160 | tf_op jit(solution)/shard_map/add | solution.py:49
  160.6 1.3 collective-permute-start.22
  161.9 4.6 %collective-permute-start.23 = (f32[32,1,256]{2,0,1:T(8,128)S(1)}, f32[32,1,256]{2,0,1:T(8,128)S(1)}, u32[]{:S(2)}, u32[]{:S(2)}) collective-permute-start(f32[32,1,256]{2,0,1:T(8,128)S(1)} %copy.244), channel_id=1, source_target_pairs={{0,4},{4,8},{8,12},{1,5},{5,9},{9,13},{2,6},{6,10},{10,14},{3,7},{... | collective-permute-start | bytes 98312 | tf_op jit(solution)/shard_map/ppermute | solution.py:14
  168.9 1.4 copy.248
  171.6 1.4 copy.250
  173.0 4.0 %collective-permute-start.25 = (f32[32,34,1]{1,0,2:T(8,128)S(1)}, f32[32,34,1]{1,0,2:T(8,128)S(1)}, u32[]{:S(2)}, u32[]{:S(2)}) collective-permute-start(f32[32,34,1]{1,0,2:T(8,128)S(1)} %copy.250), channel_id=1, source_target_pairs={{0,2},{1,3},{4,6},{5,7},{8,10},{9,11},{12,14},{13,15},{16,18},{17,... | collective-permute-start | bytes 13064 | tf_op jit(solution)/shard_map/ppermute | solution.py:14
  180.3 3.7 %collective-permute-start.26 = (f32[1,34,258]{2,1,0:T(8,128)S(1)}, f32[1,34,258]{2,1,0:T(8,128)S(1)}, u32[]{:S(2)}, u32[]{:S(2)}) collective-permute-start(f32[1,34,258]{2,1,0:T(8,128)S(1)} %get-tuple-element.8), channel_id=1, source_target_pairs={{1,0},{3,2},{5,4},{7,6},{9,8},{11,10},{13,12},{15,14},{17,16},{19,... | collective-permute-start | bytes 105272 | tf_op jit(solution)/shard_map/ppermute | solution.py:17
  184.0 1.3 collective-permute-start.27
  187.1 9.2 %fusion.8 = f32[32,32,256]{2,1,0:T(8,128)S(1)} fusion(f32[32,32,256]{2,1,0:T(8,128)S(1)} %fusion.30, f32[1,34,258]{2,1,0:T(8,128)S(1)} %collective-permute-done.27, f32[32,34,1]{2,1,0:T(8,128)} %copy.249, f32[32,34,1]{2,1,0:T(8,128)} %copy.251, f32[32,1,256]{2,1,0:T(1,128)S(1)} %copy.243, f32[32,1,256]{2,1,0:T(1,128)S(1)} %copy.245, ...), kind=kLoop, calls=%fused_computation.18 | loop fusion | flops 11534336 | bytes 9680160 | tf_op jit(solution)/shard_map/add | solution.py:49
  197.4 3.4 %psum.22 = bf16[64,128]{1,0:T(8,128)(2,1)S(1)} all-reduce(bf16[64,128]{1,0:T(8,128)(2,1)S(1)} %reshape.141), channel_id=1, replica_groups=mesh['ens'=2,'gx'=4,'gy'=2,'gz'=2] {'gz'}, use_global_device_ids=true, to_apply=%region_1.2 | all-reduce | flops 8192 | bytes 32768 | tf_op jit(solution)/shard_map/psum | solution.py:24
  202.8 13.1 %all_to_all.10 = f32[8,1,128]{2,1,0:T(1,128)S(1)} all-to-all(f32[8,1,128]{2,1,0:T(1,128)S(1)} %bitcast.68), channel_id=1, replica_groups=mesh['ens'=2,'gx'=4,'gy'=2,'gz'=2] {'gx','gy'}, dimensions={0} | all-to-all | bytes 8192 | tf_op jit(solution)/shard_map/all_to_all | solution.py:115
  216.0 4.5 %psum.23 = f32[8,128]{1,0:T(8,128)} all-reduce(f32[8,128]{1,0:T(8,128)S(1)} %fusion.101), channel_id=1, replica_groups=mesh['ens'=2,'gx'=4,'gy'=2,'gz'=2] {'gz'}, use_global_device_ids=true, to_apply=%region_2.3 | all-reduce | flops 1024 | bytes 8192 | tf_op jit(solution)/shard_map/psum | solution.py:122
  (130 shorter events, 40.3 us)
Async XLA Ops:
  7.2 35.9 %copy-start = (bf16[64,128,128]{2,1,0:T(8,128)(2,1)S(1)}, bf16[64,128,128]{2,1,0:T(8,128)(2,1)}, u32[]{:S(2)}) copy-start(bf16[64,128,128]{2,1,0:T(8,128)(2,1)} %param.13) | copy-start | bytes 6291460
  8.1 24.6 %collective-permute-start = (bf16[1,256]{1,0:T(2,128)(2,1)S(1)}, bf16[1,256]{1,0:T(2,128)(2,1)S(1)}, u32[]{:S(2)}, u32[]{:S(2)}) collective-permute-start(bf16[1,256]{1,0:T(2,128)(2,1)S(1)} %get-tuple-element.36), channel_id=1, source_target_pairs={{0,4},{4,8},{8,12},{1,5},{5,9},{9,13},{2,6},{6,10},{10,14},{3,7},{... | collective-permute-start | bytes 1544 | tf_op jit(solution)/shard_map/ppermute | solution.py:14
  12.1 20.6 %collective-permute-start.1 = (bf16[1,256]{1,0:T(2,128)(2,1)S(1)}, bf16[1,256]{1,0:T(2,128)(2,1)S(1)}, u32[]{:S(2)}, u32[]{:S(2)}) collective-permute-start(bf16[1,256]{1,0:T(2,128)(2,1)S(1)} %get-tuple-element.37), channel_id=1, source_target_pairs={{4,0},{8,4},{12,8},{5,1},{9,5},{13,9},{6,2},{10,6},{14,10},{7,3},{... | collective-permute-start | bytes 1544 | tf_op jit(solution)/shard_map/ppermute | solution.py:17
  14.1 0.9 copy-start.13
  16.8 25.6 %all-to-all-start = ((bf16[8,2,128]{2,1,0:T(2,128)(2,1)}), bf16[8,2,128]{2,1,0:T(2,128)(2,1)S(1)}, u32[]{:S(2)}, u32[]{:S(2)}) async-start(bf16[8,2,128]{2,1,0:T(2,128)(2,1)} %reshape.163), calls=%async_computation | async-start | bytes 8192 | tf_op jit(solution)/shard_map/all_to_all | solution.py:79
  23.1 52.1 %all-reduce.2.cloned.1.call-start = ((), (), s32[]{:S(2)}) async-start(), calls=%async_computation.2 | async-start | bytes 131072 | tf_op jit(solution)/shard_map/psum | solution.py:91
  24.2 19.5 %collective-permute-start.4 = (f32[32,1,256]{2,0,1:T(8,128)S(1)}, f32[32,1,256]{2,0,1:T(8,128)S(1)}, u32[]{:S(2)}, u32[]{:S(2)}) collective-permute-start(f32[32,1,256]{2,0,1:T(8,128)S(1)} %copy.257), channel_id=1, source_target_pairs={{4,0},{8,4},{12,8},{5,1},{9,5},{13,9},{6,2},{10,6},{14,10},{7,3},{... | collective-permute-start | bytes 98312 | tf_op jit(solution)/shard_map/ppermute | solution.py:17
  25.5 18.3 %collective-permute-start.5 = (f32[32,1,256]{2,0,1:T(8,128)S(1)}, f32[32,1,256]{2,0,1:T(8,128)S(1)}, u32[]{:S(2)}, u32[]{:S(2)}) collective-permute-start(f32[32,1,256]{2,0,1:T(8,128)S(1)} %copy.258), channel_id=1, source_target_pairs={{0,4},{4,8},{8,12},{1,5},{5,9},{9,13},{2,6},{6,10},{10,14},{3,7},{... | collective-permute-start | bytes 98312 | tf_op jit(solution)/shard_map/ppermute | solution.py:14
  32.8 4.6 %collective-permute-start.2 = (bf16[34,1]{1,0:T(8,128)(2,1)S(1)}, bf16[34,1]{1,0:T(8,128)(2,1)S(1)}, u32[]{:S(2)}, u32[]{:S(2)}) collective-permute-start(bf16[34,1]{1,0:T(8,128)(2,1)S(1)} %get-tuple-element.34), channel_id=1, source_target_pairs={{0,2},{1,3},{4,6},{5,7},{8,10},{9,11},{12,14},{13,15},{16,18},{17,... | collective-permute-start | bytes 212 | tf_op jit(solution)/shard_map/ppermute | solution.py:14
  36.1 4.4 %collective-permute-start.3 = (bf16[34,1]{1,0:T(8,128)(2,1)S(1)}, bf16[34,1]{1,0:T(8,128)(2,1)S(1)}, u32[]{:S(2)}, u32[]{:S(2)}) collective-permute-start(bf16[34,1]{1,0:T(8,128)(2,1)S(1)} %get-tuple-element.35), channel_id=1, source_target_pairs={{2,0},{3,1},{6,4},{7,5},{10,8},{11,9},{14,12},{15,13},{18,16},{19,... | collective-permute-start | bytes 212 | tf_op jit(solution)/shard_map/ppermute | solution.py:17
  42.4 1.4 copy-start.5
  46.7 7.5 %collective-permute-start.6 = (f32[32,34,1]{1,0,2:T(8,128)S(1)}, f32[32,34,1]{1,0,2:T(8,128)S(1)}, u32[]{:S(2)}, u32[]{:S(2)}) collective-permute-start(f32[32,34,1]{1,0,2:T(8,128)S(1)} %copy.208), channel_id=1, source_target_pairs={{2,0},{3,1},{6,4},{7,5},{10,8},{11,9},{14,12},{15,13},{18,16},{19,... | collective-permute-start | bytes 13064 | tf_op jit(solution)/shard_map/ppermute | solution.py:17
  49.4 6.0 %collective-permute-start.7 = (f32[32,34,1]{1,0,2:T(8,128)S(1)}, f32[32,34,1]{1,0,2:T(8,128)S(1)}, u32[]{:S(2)}, u32[]{:S(2)}) collective-permute-start(f32[32,34,1]{1,0,2:T(8,128)S(1)} %copy.210), channel_id=1, source_target_pairs={{0,2},{1,3},{4,6},{5,7},{8,10},{9,11},{12,14},{13,15},{16,18},{17,... | collective-permute-start | bytes 13064 | tf_op jit(solution)/shard_map/ppermute | solution.py:14
  56.6 19.4 %copy-start.7 = (f32[32,256]{1,0:T(8,128)S(1)}, f32[32,256]{1,0:T(8,128)}, u32[]{:S(2)}) copy-start(f32[32,256]{1,0:T(8,128)} %param.9) | copy-start | bytes 98308
  57.5 18.5 %collective-permute-start.8 = (f32[1,34,258]{2,1,0:T(8,128)S(1)}, f32[1,34,258]{2,1,0:T(8,128)S(1)}, u32[]{:S(2)}, u32[]{:S(2)}) collective-permute-start(f32[1,34,258]{2,1,0:T(8,128)S(1)} %get-tuple-element.14), channel_id=1, source_target_pairs={{1,0},{3,2},{5,4},{7,6},{9,8},{11,10},{13,12},{15,14},{17,16},{19,... | collective-permute-start | bytes 105272 | tf_op jit(solution)/shard_map/ppermute | solution.py:17
  63.7 12.2 %collective-permute-start.9 = (f32[1,34,258]{2,1,0:T(8,128)S(1)}, f32[1,34,258]{2,1,0:T(8,128)S(1)}, u32[]{:S(2)}, u32[]{:S(2)}) collective-permute-start(f32[1,34,258]{2,1,0:T(8,128)S(1)} %get-tuple-element.15), channel_id=1, source_target_pairs={{0,1},{2,3},{4,5},{6,7},{8,9},{10,11},{12,13},{14,15},{16,17},{18,... | collective-permute-start | bytes 105272 | tf_op jit(solution)/shard_map/ppermute | solution.py:14
  88.8 18.4 %copy-start.4 = (f32[32,32,256]{2,1,0:T(8,128)}, f32[32,32,256]{2,1,0:T(8,128)S(1)}, u32[]{:S(2)}) copy-start(f32[32,32,256]{2,1,0:T(8,128)S(1)} %fusion.74) | copy-start | bytes 3145732
  88.9 5.4 %collective-permute-start.10 = (f32[32,1,256]{2,0,1:T(8,128)S(1)}, f32[32,1,256]{2,0,1:T(8,128)S(1)}, u32[]{:S(2)}, u32[]{:S(2)}) collective-permute-start(f32[32,1,256]{2,0,1:T(8,128)S(1)} %copy.218), channel_id=1, source_target_pairs={{4,0},{8,4},{12,8},{5,1},{9,5},{13,9},{6,2},{10,6},{14,10},{7,3},{... | collective-permute-start | bytes 98312 | tf_op jit(solution)/shard_map/ppermute | solution.py:17
  90.2 5.1 %collective-permute-start.11 = (f32[32,1,256]{2,0,1:T(8,128)S(1)}, f32[32,1,256]{2,0,1:T(8,128)S(1)}, u32[]{:S(2)}, u32[]{:S(2)}) collective-permute-start(f32[32,1,256]{2,0,1:T(8,128)S(1)} %copy.220), channel_id=1, source_target_pairs={{0,4},{4,8},{8,12},{1,5},{5,9},{9,13},{2,6},{6,10},{10,14},{3,7},{... | collective-permute-start | bytes 98312 | tf_op jit(solution)/shard_map/ppermute | solution.py:14
  98.2 6.7 %collective-permute-start.12 = (f32[32,34,1]{1,0,2:T(8,128)S(1)}, f32[32,34,1]{1,0,2:T(8,128)S(1)}, u32[]{:S(2)}, u32[]{:S(2)}) collective-permute-start(f32[32,34,1]{1,0,2:T(8,128)S(1)} %copy.224), channel_id=1, source_target_pairs={{2,0},{3,1},{6,4},{7,5},{10,8},{11,9},{14,12},{15,13},{18,16},{19,... | collective-permute-start | bytes 13064 | tf_op jit(solution)/shard_map/ppermute | solution.py:17
  100.9 5.2 %collective-permute-start.13 = (f32[32,34,1]{1,0,2:T(8,128)S(1)}, f32[32,34,1]{1,0,2:T(8,128)S(1)}, u32[]{:S(2)}, u32[]{:S(2)}) collective-permute-start(f32[32,34,1]{1,0,2:T(8,128)S(1)} %copy.226), channel_id=1, source_target_pairs={{0,2},{1,3},{4,6},{5,7},{8,10},{9,11},{12,14},{13,15},{16,18},{17,... | collective-permute-start | bytes 13064 | tf_op jit(solution)/shard_map/ppermute | solution.py:14
  107.2 8.2 %copy-start.1 = (f32[34,34,258]{2,1,0:T(8,128)S(1)}, f32[34,34,258]{2,1,0:T(8,128)}, u32[]{:S(2)}) copy-start(f32[34,34,258]{2,1,0:T(8,128)} %and_select_fusion) | copy-start | bytes 3578980
  107.2 8.2 %copy-start.9 = (f32[32]{0:T(128)S(1)}, f32[32]{0:T(128)}, u32[]{:S(2)}) copy-start(f32[32]{0:T(128)} %get-tuple-element.42) | copy-start | bytes 388
  107.2 8.2 %copy-start.10 = (f32[32]{0:T(128)S(1)}, f32[32]{0:T(128)}, u32[]{:S(2)}) copy-start(f32[32]{0:T(128)} %get-tuple-element.43) | copy-start | bytes 388
  108.3 5.3 %collective-permute-start.14 = (f32[1,34,258]{2,1,0:T(8,128)S(1)}, f32[1,34,258]{2,1,0:T(8,128)S(1)}, u32[]{:S(2)}, u32[]{:S(2)}) collective-permute-start(f32[1,34,258]{2,1,0:T(8,128)S(1)} %get-tuple-element.12), channel_id=1, source_target_pairs={{1,0},{3,2},{5,4},{7,6},{9,8},{11,10},{13,12},{15,14},{17,16},{19,... | collective-permute-start | bytes 105272 | tf_op jit(solution)/shard_map/ppermute | solution.py:17
  112.3 3.1 %collective-permute-start.15 = (f32[1,34,258]{2,1,0:T(8,128)S(1)}, f32[1,34,258]{2,1,0:T(8,128)S(1)}, u32[]{:S(2)}, u32[]{:S(2)}) collective-permute-start(f32[1,34,258]{2,1,0:T(8,128)S(1)} %get-tuple-element.13), channel_id=1, source_target_pairs={{0,1},{2,3},{4,5},{6,7},{8,9},{10,11},{12,13},{14,15},{16,17},{18,... | collective-permute-start | bytes 105272 | tf_op jit(solution)/shard_map/ppermute | solution.py:14
  124.6 18.9 %copy-start.3 = (f32[32,32,256]{2,1,0:T(8,128)}, f32[32,32,256]{2,1,0:T(8,128)S(1)}, u32[]{:S(2)}) copy-start(f32[32,32,256]{2,1,0:T(8,128)S(1)} %fusion.52) | copy-start | bytes 3145732
  124.7 5.9 %collective-permute-start.16 = (f32[32,1,256]{2,0,1:T(8,128)S(1)}, f32[32,1,256]{2,0,1:T(8,128)S(1)}, u32[]{:S(2)}, u32[]{:S(2)}) collective-permute-start(f32[32,1,256]{2,0,1:T(8,128)S(1)} %copy.230), channel_id=1, source_target_pairs={{4,0},{8,4},{12,8},{5,1},{9,5},{13,9},{6,2},{10,6},{14,10},{7,3},{... | collective-permute-start | bytes 98312 | tf_op jit(solution)/shard_map/ppermute | solution.py:17
  126.0 5.6 %collective-permute-start.17 = (f32[32,1,256]{2,0,1:T(8,128)S(1)}, f32[32,1,256]{2,0,1:T(8,128)S(1)}, u32[]{:S(2)}, u32[]{:S(2)}) collective-permute-start(f32[32,1,256]{2,0,1:T(8,128)S(1)} %copy.232), channel_id=1, source_target_pairs={{0,4},{4,8},{8,12},{1,5},{5,9},{9,13},{2,6},{6,10},{10,14},{3,7},{... | collective-permute-start | bytes 98312 | tf_op jit(solution)/shard_map/ppermute | solution.py:14
  134.4 6.7 %collective-permute-start.18 = (f32[32,34,1]{1,0,2:T(8,128)S(1)}, f32[32,34,1]{1,0,2:T(8,128)S(1)}, u32[]{:S(2)}, u32[]{:S(2)}) collective-permute-start(f32[32,34,1]{1,0,2:T(8,128)S(1)} %copy.236), channel_id=1, source_target_pairs={{2,0},{3,1},{6,4},{7,5},{10,8},{11,9},{14,12},{15,13},{18,16},{19,... | collective-permute-start | bytes 13064 | tf_op jit(solution)/shard_map/ppermute | solution.py:17
  137.1 5.2 %collective-permute-start.19 = (f32[32,34,1]{1,0,2:T(8,128)S(1)}, f32[32,34,1]{1,0,2:T(8,128)S(1)}, u32[]{:S(2)}, u32[]{:S(2)}) collective-permute-start(f32[32,34,1]{1,0,2:T(8,128)S(1)} %copy.238), channel_id=1, source_target_pairs={{0,2},{1,3},{4,6},{5,7},{8,10},{9,11},{12,14},{13,15},{16,18},{17,... | collective-permute-start | bytes 13064 | tf_op jit(solution)/shard_map/ppermute | solution.py:14
  143.5 7.9 %copy-start.2 = (f32[34,34,258]{2,1,0:T(8,128)S(1)}, f32[34,34,258]{2,1,0:T(8,128)}, u32[]{:S(2)}) copy-start(f32[34,34,258]{2,1,0:T(8,128)} %and_select_fusion) | copy-start | bytes 3578980
  144.5 5.2 %collective-permute-start.20 = (f32[1,34,258]{2,1,0:T(8,128)S(1)}, f32[1,34,258]{2,1,0:T(8,128)S(1)}, u32[]{:S(2)}, u32[]{:S(2)}) collective-permute-start(f32[1,34,258]{2,1,0:T(8,128)S(1)} %get-tuple-element.10), channel_id=1, source_target_pairs={{1,0},{3,2},{5,4},{7,6},{9,8},{11,10},{13,12},{15,14},{17,16},{19,... | collective-permute-start | bytes 105272 | tf_op jit(solution)/shard_map/ppermute | solution.py:17
  148.2 3.1 %collective-permute-start.21 = (f32[1,34,258]{2,1,0:T(8,128)S(1)}, f32[1,34,258]{2,1,0:T(8,128)S(1)}, u32[]{:S(2)}, u32[]{:S(2)}) collective-permute-start(f32[1,34,258]{2,1,0:T(8,128)S(1)} %get-tuple-element.11), channel_id=1, source_target_pairs={{0,1},{2,3},{4,5},{6,7},{8,9},{10,11},{12,13},{14,15},{16,17},{18,... | collective-permute-start | bytes 105272 | tf_op jit(solution)/shard_map/ppermute | solution.py:14
  160.6 5.9 %collective-permute-start.22 = (f32[32,1,256]{2,0,1:T(8,128)S(1)}, f32[32,1,256]{2,0,1:T(8,128)S(1)}, u32[]{:S(2)}, u32[]{:S(2)}) collective-permute-start(f32[32,1,256]{2,0,1:T(8,128)S(1)} %copy.242), channel_id=1, source_target_pairs={{4,0},{8,4},{12,8},{5,1},{9,5},{13,9},{6,2},{10,6},{14,10},{7,3},{... | collective-permute-start | bytes 98312 | tf_op jit(solution)/shard_map/ppermute | solution.py:17
  161.9 5.6 %collective-permute-start.23 = (f32[32,1,256]{2,0,1:T(8,128)S(1)}, f32[32,1,256]{2,0,1:T(8,128)S(1)}, u32[]{:S(2)}, u32[]{:S(2)}) collective-permute-start(f32[32,1,256]{2,0,1:T(8,128)S(1)} %copy.244), channel_id=1, source_target_pairs={{0,4},{4,8},{8,12},{1,5},{5,9},{9,13},{2,6},{6,10},{10,14},{3,7},{... | collective-permute-start | bytes 98312 | tf_op jit(solution)/shard_map/ppermute | solution.py:14
  170.3 6.7 %collective-permute-start.24 = (f32[32,34,1]{1,0,2:T(8,128)S(1)}, f32[32,34,1]{1,0,2:T(8,128)S(1)}, u32[]{:S(2)}, u32[]{:S(2)}) collective-permute-start(f32[32,34,1]{1,0,2:T(8,128)S(1)} %copy.248), channel_id=1, source_target_pairs={{2,0},{3,1},{6,4},{7,5},{10,8},{11,9},{14,12},{15,13},{18,16},{19,... | collective-permute-start | bytes 13064 | tf_op jit(solution)/shard_map/ppermute | solution.py:17
  173.0 5.2 %collective-permute-start.25 = (f32[32,34,1]{1,0,2:T(8,128)S(1)}, f32[32,34,1]{1,0,2:T(8,128)S(1)}, u32[]{:S(2)}, u32[]{:S(2)}) collective-permute-start(f32[32,34,1]{1,0,2:T(8,128)S(1)} %copy.250), channel_id=1, source_target_pairs={{0,2},{1,3},{4,6},{5,7},{8,10},{9,11},{12,14},{13,15},{16,18},{17,... | collective-permute-start | bytes 13064 | tf_op jit(solution)/shard_map/ppermute | solution.py:14
  179.4 5.9 %copy-start.12 = (s32[64]{0:T(128)S(1)}, s32[64]{0:T(128)}, u32[]{:S(2)}) copy-start(s32[64]{0:T(128)} %get-tuple-element.40) | copy-start | bytes 772
  180.3 5.6 %collective-permute-start.26 = (f32[1,34,258]{2,1,0:T(8,128)S(1)}, f32[1,34,258]{2,1,0:T(8,128)S(1)}, u32[]{:S(2)}, u32[]{:S(2)}) collective-permute-start(f32[1,34,258]{2,1,0:T(8,128)S(1)} %get-tuple-element.8), channel_id=1, source_target_pairs={{1,0},{3,2},{5,4},{7,6},{9,8},{11,10},{13,12},{15,14},{17,16},{19,... | collective-permute-start | bytes 105272 | tf_op jit(solution)/shard_map/ppermute | solution.py:17
  184.0 3.1 %collective-permute-start.27 = (f32[1,34,258]{2,1,0:T(8,128)S(1)}, f32[1,34,258]{2,1,0:T(8,128)S(1)}, u32[]{:S(2)}, u32[]{:S(2)}) collective-permute-start(f32[1,34,258]{2,1,0:T(8,128)S(1)} %get-tuple-element.9), channel_id=1, source_target_pairs={{0,1},{2,3},{4,5},{6,7},{8,9},{10,11},{12,13},{14,15},{16,17},{18,... | collective-permute-start | bytes 105272 | tf_op jit(solution)/shard_map/ppermute | solution.py:14
  185.9 11.4 %copy-start.8 = (s32[32,256]{1,0:T(8,128)S(1)}, s32[32,256]{1,0:T(8,128)}, u32[]{:S(2)}) copy-start(s32[32,256]{1,0:T(8,128)} %param.8) | copy-start | bytes 98308
  196.4 1.0 copy-start.6
  197.3 5.3 %copy-start.11 = (s32[64]{0:T(128)S(1)}, s32[64]{0:T(128)}, u32[]{:S(2)}) copy-start(s32[64]{0:T(128)} %get-tuple-element.38) | copy-start | bytes 772
  197.3 18.5 %copy-start.14 = (s32[8]{0:T(128)S(1)}, s32[8]{0:T(128)}, u32[]{:S(2)}) copy-start(s32[8]{0:T(128)} %copy-done.13) | copy-start | bytes 100
Sparse Core Ops, SparseCore 0:
  54.3 20.8 all-reduce.1
where the time goes:
time: 229 us; the launch traced here: 227 us
  starting transfers between devices  82.7 us (36%)
  other arithmetic  50.7 us (22%)
  local copies, waits for them, and re-layouts  34.2 us (15%)
  waiting for transfers between devices  20.9 us (9%)
  blocking collectives  20.9 us (9%)
  between operations  14.8 us (6%)
  matrix products  3.12 us (1%)
    ppermute x14, starting transfers between devices, extended(): lax.ppermute(lax.slice_in_dim(block, block.shape[dim] - width, None, axis...  45.8 us
    add x4, other arithmetic, advance(): center + water_indicator * (0.1 * lateral + mixing * vertical + 0.1 * for...  40.2 us
    ppermute x14, starting transfers between devices, extended(): lax.ppermute(lax.slice_in_dim(block, 0, width, axis=dim), axis, backward)  30.6 us
    all_to_all x1, blocking collectives, per_device(): lax.all_to_all(buffer, ('gx', 'gy'), split_axis=0, concat_axis=0, tiled=T...  13.1 us
    slice x17, local copies, waits for them, and re-layouts, extended(): lax.slice_in_dim(block, block.shape[dim] - width, None, axis=dim)  11.9 us
    psum x1, waiting for transfers between devices, per_device(): surface = lax.psum(partial_surface, 'gz')  10.2 us
    ppermute x14, waiting for transfers between devices, extended(): lax.ppermute(lax.slice_in_dim(block, block.shape[dim] - width, None, axis...  7.59 us
    all_to_all x1, starting transfers between devices, per_device(): lax.all_to_all(outgoing, ('gx', 'gy'), split_axis=0, concat_axis=0, tiled...  6.31 us
  transfers between devices with their start and end apart: 30, of which 8 were waited for; matrix products, arithmetic and copies ran while one was open for 11% of the time, Pallas kernels for 0%

commit v1 on v0

v1 whole, which is shorter than its diff:
```python
import functools

import jax
import jax.numpy as jnp
from jax import lax
from jax.experimental import pallas as pl
from jax.experimental.pallas import tpu as pltpu
from jax.sharding import PartitionSpec as P

STEPS = 4
HALO = STEPS
TOP = STEPS + 1
LANES = 128
GROUP = LANES // HALO
FEW = 16
BLOCKS_AXES = ("gx", "gy")
ALL_AXES = ("gx", "gy", "gz")
VMEM_LIMIT = 48 * 1024 * 1024


def side_tile(left, right, index):
    lane = lax.broadcasted_iota(jnp.int32, left.shape, 1)
    from_right = pltpu.roll(right, lax.rem(LANES - HALO * index, LANES), 1)
    from_left = pltpu.roll(left, lax.rem(2 * LANES - HALO - HALO * index, LANES), 1)
    zero = jnp.zeros_like(left)
    return jnp.where(lane < HALO, from_right, jnp.where(lane >= LANES - HALO, from_left, zero))


def put_slab(ref, own, after, before, tile):
    rows, columns = own.shape
    ref[0:rows, 0:columns] = own
    ref[rows : rows + HALO, 0:columns] = after
    ref[rows + HALO : rows + 2 * HALO, 0:columns] = before
    ref[:, columns:] = tile


def neighbour_levels(levels):
    rows, lanes = levels.shape
    return (
        pltpu.roll(levels, 1, 0),
        pltpu.roll(levels, rows - 1, 0),
        pltpu.roll(levels, 1, 1),
        pltpu.roll(levels, lanes - 1, 1),
    )


def keep_share(levels_ref, around_ref, mixing_ref, level):
    wet_around = jnp.where(around_ref[0] > level, 0.1, 0.0)
    for side in range(1, 4):
        wet_around = wet_around + jnp.where(around_ref[side] > level, 0.1, 0.0)
    above = jnp.where(level > 0.0, 1.0, 0.0)
    vertical = above + jnp.where(levels_ref[...] > level + 1.0, 1.0, 0.0)
    return 1.0 - wet_around - mixing_ref[...] * vertical


def step_slab(center, over, under, keep, mixing, levels, level, forcing):
    rows, lanes = center.shape
    lateral = pltpu.roll(center, 1, 0) + pltpu.roll(center, rows - 1, 0)
    lateral = lateral + (pltpu.roll(center, 1, 1) + pltpu.roll(center, lanes - 1, 1))
    new = center * keep + 0.1 * (lateral + forcing) + mixing * (over + under)
    return jnp.where(levels > level, new, 0.0)


def prepare(bathy_ref, mixing_ref, next_ref, prev_ref, left_ref, right_ref, info_ref, fields, levels_ref, mix_ref, around_ref):
    rows, columns = bathy_ref.shape
    size = rows + 2 * HALO
    lane = lax.broadcasted_iota(jnp.int32, (size, LANES), 1)
    tile = side_tile(left_ref[1], right_ref[1], fields % GROUP)
    tile = jnp.where((lane < HALO) & (info_ref[2] == 0), 0.0, tile)
    tile = jnp.where((lane >= LANES - HALO) & (info_ref[1] == 0), 0.0, tile)
    put_slab(levels_ref, bathy_ref[...].astype(jnp.float32), next_ref[fields], prev_ref[fields], tile)
    tile = side_tile(left_ref[1], right_ref[1], (fields + 1) % GROUP)
    put_slab(mix_ref, mixing_ref[...], next_ref[fields + 1], prev_ref[fields + 1], tile)
    for side, values in enumerate(neighbour_levels(levels_ref[...])):
        around_ref[side] = values


def skin_kernel(
    info_ref, temp_ref, shared_ref, bathy_ref, mixing_ref, next_ref, prev_ref, left_ref, right_ref, surface_ref,
    skin_ref, first_ref, second_ref, keep_ref, levels_ref, mix_ref, around_ref, *, total_levels,
):
    layers = temp_ref.shape[0]
    fields = layers + shared_ref.shape[0]
    prepare(bathy_ref, mixing_ref, next_ref, prev_ref, left_ref, right_ref, info_ref, fields, levels_ref, mix_ref, around_ref)
    gz = info_ref[0]
    shift = gz * layers
    levels = levels_ref[...]
    for level in range(TOP):
        slot = level + shift
        own = jnp.where(gz == 0, temp_ref[level], shared_ref[level])
        tile = side_tile(left_ref[gz], right_ref[gz], level)
        put_slab(first_ref.at[level], own, next_ref[slot], prev_ref[slot], tile)
        first_ref[level] = jnp.where(levels > float(level), first_ref[level], 0.0)
        if level < STEPS:
            keep_ref[level] = keep_share(levels_ref, around_ref, mix_ref, jnp.float32(level))
    zero = jnp.zeros_like(levels)
    source, target = first_ref, second_ref
    for step in range(1, STEPS + 1):
        for level in range(TOP - step):
            depth_share = jnp.exp(jnp.full((1, 1), -4.0 * level / total_levels, jnp.float32))
            forcing = depth_share * surface_ref[1]
            if level == 0:
                forcing = forcing + surface_ref[0]
            over = source[level - 1] if level else zero
            target[level] = step_slab(
                source[level], over, source[level + 1], keep_ref[level], mix_ref[...], levels, float(level), forcing
            )
        source, target = target, source
    rows, columns = bathy_ref.shape
    skin_ref[...] = source[0, 0:rows, 0:columns].astype(jnp.bfloat16)


def ocean_kernel(
    info_ref, temp_ref, shared_ref, bathy_ref, mixing_ref, next_ref, prev_ref, left_ref, right_ref, surface_ref,
    ocean_ref, first_ref, second_ref, keep_ref, levels_ref, mix_ref, around_ref, *, total_levels,
):
    layers, rows, columns = temp_ref.shape
    fields = layers + shared_ref.shape[0]
    prepare(bathy_ref, mixing_ref, next_ref, prev_ref, left_ref, right_ref, info_ref, fields, levels_ref, mix_ref, around_ref)
    gz = info_ref[0]
    first_level = gz * layers - HALO

    def level_of(place):
        return (first_level + place).astype(jnp.float32)

    def settle(place):
        level = level_of(place)
        first_ref[place] = jnp.where(levels_ref[...] > level, first_ref[place], 0.0)
        keep_ref[place] = keep_share(levels_ref, around_ref, mix_ref, level)

    def own_level(index, carry):
        tile = side_tile(left_ref[0], right_ref[0], index)
        put_slab(first_ref.at[index + HALO], temp_ref[index], next_ref[index], prev_ref[index], tile)
        settle(index + HALO)
        return carry

    lax.fori_loop(0, layers, own_level, 0)

    def shared_level(index, carry):
        slot = jnp.where(gz == 0, index, TOP + index)
        place = jnp.where(gz == 0, HALO + layers + index, index)
        tile = side_tile(left_ref[1], right_ref[1], slot)
        put_slab(first_ref.at[place], shared_ref[slot], next_ref[layers + slot], prev_ref[layers + slot], tile)
        settle(place)
        return carry

    lax.fori_loop(0, HALO, shared_level, 0)
    edge = jnp.where(gz == 0, HALO - 1, HALO + layers)
    first_ref[edge] = jnp.zeros_like(first_ref[0])
    second_ref[edge] = jnp.zeros_like(first_ref[0])
    source, target = first_ref, second_ref
    for step in range(1, STEPS + 1):
        base = jnp.where(gz == 0, HALO, step)

        def one(index, carry, source=source, target=target, base=base):
            place = base + index
            level = level_of(place)
            depth_share = jnp.exp(jnp.full((1, 1), -4.0 / total_levels, jnp.float32) * level)
            target[place] = step_slab(
                source[place], source[place - 1], source[place + 1], keep_ref[place], mix_ref[...], levels_ref[...],
                level, depth_share * surface_ref[1],
            )
            return carry

        lax.fori_loop(0, layers + HALO - step, one, 0)

        @pl.when(gz == 0)
        def _(target=target):
            target[HALO] = target[HALO] + jnp.where(levels_ref[...] > 0.0, 0.1 * surface_ref[0], 0.0)

        source, target = target, source

    def write(index, carry):
        wet = levels_ref[0:rows, 0:columns] > level_of(index + HALO)
        ocean_ref[index] = jnp.where(wet, source[index + HALO, 0:rows, 0:columns], temp_ref[index])
        return carry

    lax.fori_loop(0, layers, write, 0)


def pack_kernel(side_ref, temp_ref, shared_ref, bathy_ref, mixing_ref, next_ref, prev_ref, packed_ref):
    layers, rows, columns = temp_ref.shape
    shared = shared_ref.shape[0]
    right = side_ref[0]
    start = pl.multiple_of(right * (columns - LANES), LANES)
    base = jnp.where(right == 1, HALO, 0)
    window = pl.ds(start, LANES)
    lane = lax.broadcasted_iota(jnp.int32, (rows + 2 * HALO, LANES), 1)

    def add(carry, index, own, slot):
        slab = jnp.concatenate([own, next_ref[slot, :, window], prev_ref[slot, :, window]], axis=0)
        place = index * HALO
        moved = pltpu.roll(slab, lax.rem(place + base, LANES), 1)
        return jnp.where((lane >= place) & (lane < place + HALO), moved, carry)

    packed_ref[0] = lax.fori_loop(
        0, layers, lambda i, c: add(c, i, temp_ref[i, :, window], i), jnp.zeros(lane.shape, jnp.float32)
    )
    second = lax.fori_loop(
        0, shared, lambda i, c: add(c, i, shared_ref[i, :, window], layers + i), jnp.zeros(lane.shape, jnp.float32)
    )
    second = add(second, shared, bathy_ref[:, window].astype(jnp.float32), layers + shared)
    packed_ref[1] = add(second, shared + 1, mixing_ref[:, window], layers + shared + 1)


def vmem_call(body, out_shape, scratch=(), arguments=1, **options):
    vmem = pl.BlockSpec(memory_space=pltpu.VMEM)
    return pl.pallas_call(
        body,
        out_shape=out_shape,
        in_specs=[pl.BlockSpec(memory_space=pltpu.SMEM)] + [vmem] * arguments,
        out_specs=vmem,
        scratch_shapes=list(scratch),
        compiler_params=pltpu.CompilerParams(vmem_limit_bytes=VMEM_LIMIT),
        **options,
    )


def line(count):
    forward = [(i, i + 1) for i in range(count - 1)]
    return forward, [(target, source) for source, target in forward]


def outgoing_tiles(my_sends, atm_flux):
    own_tiles = atm_flux.shape[0]
    chooser = (my_sends.reshape(-1)[:, None] == jnp.arange(own_tiles)[None, :]).astype(jnp.bfloat16)
    flat_flux = atm_flux.reshape(own_tiles, atm_flux.shape[1] * atm_flux.shape[2])
    return jnp.dot(chooser, flat_flux, preferred_element_type=jnp.float32).astype(jnp.bfloat16)


def edge_frame(surface, after, before, left, right):
    fields, rows, columns = surface.shape
    width = STEPS - 1
    gap = jnp.zeros((fields, HALO - width, columns), jnp.float32)
    body = jnp.concatenate([surface, after, gap, gap, before], axis=1)
    middle = jnp.zeros((fields, rows + 2 * HALO, LANES - 2 * width), jnp.float32)
    return jnp.concatenate([body, right, middle, left], axis=2)


def frame_rows(own, after, before):
    gap = jnp.zeros(own.shape[:1] + (HALO - after.shape[1],) + own.shape[2:], jnp.float32)
    return jnp.concatenate([own, after, gap, gap, before], axis=1)


def surface_frame_few(surface, gx_count, gy_count):
    fields, rows, columns = surface.shape
    width = STEPS - 1
    gx, gy = lax.axis_index("gx"), lax.axis_index("gy")
    block = jnp.arange(gx_count * gy_count)
    dx, dy = block // gy_count - gx, block % gy_count - gy
    columns_low = jnp.pad(surface[:, :, :width].transpose(0, 2, 1), ((0, 0), (0, 0), (0, columns - rows)))
    columns_high = jnp.pad(surface[:, :, -width:].transpose(0, 2, 1), ((0, 0), (0, 0), (0, columns - rows)))
    strips = jnp.stack([surface[:, :width], surface[:, -width:], columns_low, columns_high])
    choice = jnp.where(dx < 0, 0, jnp.where(dx > 0, 1, jnp.where(dy < 0, 2, 3)))
    message = strips[choice]
    got = lax.all_to_all(message, BLOCKS_AXES, split_axis=0, concat_axis=0, tiled=True)

    def of(x, y):
        index = jnp.clip(x, 0, gx_count - 1) * gy_count + jnp.clip(y, 0, gy_count - 1)
        return lax.dynamic_index_in_dim(got, index, 0, keepdims=False)

    after, before = of(gx + 1, gy), of(gx - 1, gy)
    right = frame_rows(
        of(gx, gy + 1)[:, :, :rows].transpose(0, 2, 1),
        of(gx + 1, gy + 1)[:, :, :width],
        of(gx - 1, gy + 1)[:, :, :width],
    )
    left = frame_rows(
        of(gx, gy - 1)[:, :, :rows].transpose(0, 2, 1),
        of(gx + 1, gy - 1)[:, :, -width:],
        of(gx - 1, gy - 1)[:, :, -width:],
    )
    return edge_frame(surface, after, before, left, right)


def surface_frame_many(surface, gx_count, gy_count):
    width = STEPS - 1
    forward, backward = line(gx_count)
    before = lax.ppermute(surface[:, -width:], "gx", forward)
    after = lax.ppermute(surface[:, :width], "gx", backward)
    forward, backward = line(gy_count)
    low, high = surface[:, :, :width], surface[:, :, -width:]
    left = lax.ppermute(
        frame_rows(high, after[:, :, -width:], before[:, :, -width:]).transpose(0, 2, 1), "gy", forward
    )
    right = lax.ppermute(
        frame_rows(low, after[:, :, :width], before[:, :, :width]).transpose(0, 2, 1), "gy", backward
    )
    return edge_frame(surface, after, before, left.transpose(0, 2, 1), right.transpose(0, 2, 1))


def per_device(
    ocean_temp, bathy_levels, mixing, atm_flux, send_tiles, regrid_slots, regrid_weights
):
    layers, row_count, columns = ocean_temp.shape
    gx_count, gy_count, gz_count = (lax.axis_size(axis) for axis in ALL_AXES)
    assert gz_count == 2 and layers == GROUP
    total_levels = layers * gz_count
    number_partitions = gx_count * gy_count
    gx, gy, gz = (lax.axis_index(axis) for axis in ALL_AXES)
    self_block = gx * gy_count + gy
    own_tiles, fields, tile_atm = atm_flux.shape
    caps = send_tiles.shape[2]
    slot_count, unused_rows, patch_marine = regrid_weights.shape
    number_patches = row_count * columns // patch_marine
    position = regrid_slots[0]
    target_patch = regrid_slots[1]
    my_sends = send_tiles[self_block]

    edge_levels = jnp.concatenate([ocean_temp[:TOP], ocean_temp[layers - HALO :]])
    shared = lax.ppermute(edge_levels, "gz", [(0, 1), (1, 0)])
    levels_float = bathy_levels.astype(jnp.float32)

    def strip(low):
        part = slice(0, HALO) if low else slice(row_count - HALO, row_count)
        return jnp.concatenate(
            [ocean_temp[:, part], shared[:, part], levels_float[None, part], mixing[None, part]]
        )

    forward, backward = line(gx_count)
    before_rows = lax.ppermute(strip(False), "gx", forward)
    after_rows = lax.ppermute(strip(True), "gx", backward)
    padded_rows = row_count + 2 * HALO
    lanes = columns + LANES

    def packed(right_side):
        return vmem_call(
            pack_kernel, jax.ShapeDtypeStruct((2, padded_rows, LANES), jnp.float32), arguments=6
        )(right_side.reshape(1), ocean_temp, shared, bathy_levels, mixing, after_rows, before_rows)

    if gy_count == 2 and FEW:
        from_left = from_right = lax.ppermute(packed(1 - gy), "gy", [(0, 1), (1, 0)])
    else:
        forward, backward = line(gy_count)
        one = jnp.int32(1)
        from_left = lax.ppermute(packed(one), "gy", forward)
        from_right = lax.ppermute(packed(one - 1), "gy", backward)

    outgoing = outgoing_tiles(my_sends, atm_flux).reshape(
        number_partitions, caps, fields * tile_atm
    )
    incoming = lax.all_to_all(outgoing, BLOCKS_AXES, split_axis=0, concat_axis=0, tiled=True)
    picked = incoming.reshape(number_partitions * caps, fields, tile_atm)[position]
    contrib = jnp.einsum("kfa,kao->kfo", picked, regrid_weights, preferred_element_type=jnp.float32)
    collect = (target_patch[None, :] == jnp.arange(number_patches)[:, None]).astype(jnp.float32)
    summed = jnp.dot(
        collect, contrib.reshape(slot_count, fields * patch_marine), precision=lax.Precision.HIGHEST
    )
    partial_surface = (
        summed.reshape(number_patches, fields, patch_marine)
        .transpose(1, 0, 2)
        .reshape(fields, row_count, columns)
    )
    surface = partial_surface + lax.ppermute(partial_surface, "gz", [(0, 1), (1, 0)])
    few = number_partitions <= FEW
    surface = (surface_frame_few if few else surface_frame_many)(surface, gx_count, gy_count)

    info = jnp.stack([gz, (gy > 0).astype(jnp.int32), (gy < gy_count - 1).astype(jnp.int32)])
    operands = (
        info, ocean_temp, shared, bathy_levels, mixing, after_rows, before_rows, from_left, from_right, surface,
    )
    slab = (padded_rows, lanes)
    flat = [pltpu.VMEM(slab, jnp.float32), pltpu.VMEM(slab, jnp.float32), pltpu.VMEM((4,) + slab, jnp.float32)]
    top_scratch = [pltpu.VMEM((TOP,) + slab, jnp.float32)] * 3 + flat
    skin = vmem_call(
        functools.partial(skin_kernel, total_levels=total_levels),
        jax.ShapeDtypeStruct((row_count, columns), jnp.bfloat16), top_scratch, arguments=9,
        cost_estimate=pl.CostEstimate(flops=10 * 20 * padded_rows * lanes, bytes_accessed=1 << 21, transcendentals=0),
    )(*operands)
    full_scratch = [pltpu.VMEM((layers + 2 * HALO,) + slab, jnp.float32)] * 3 + flat
    ocean = vmem_call(
        functools.partial(ocean_kernel, total_levels=total_levels),
        jax.ShapeDtypeStruct(ocean_temp.shape, jnp.float32), full_scratch, arguments=9,
        cost_estimate=pl.CostEstimate(
            flops=140 * 20 * padded_rows * lanes, bytes_accessed=1 << 24, transcendentals=0
        ),
    )(*operands)

    chosen_patch = skin.reshape(number_patches, patch_marine)[target_patch]
    back = jnp.einsum(
        "kao,ko->ka", regrid_weights, chosen_patch, preferred_element_type=jnp.float32
    )
    placer = (jnp.arange(number_partitions * caps)[:, None] == position[None, :]).astype(
        jnp.float32
    )
    buffer = jnp.dot(placer, back, precision=lax.Precision.HIGHEST).reshape(
        number_partitions, 1, caps * tile_atm
    )
    buffer = jnp.broadcast_to(buffer, (number_partitions, gz_count, caps * tile_atm)).reshape(
        number_partitions * gz_count, caps * tile_atm
    )
    returned = lax.all_to_all(buffer, ALL_AXES, split_axis=0, concat_axis=0, tiled=True)
    sends = jnp.broadcast_to(my_sends[:, None], (number_partitions, gz_count, caps)).reshape(-1)
    gatherer = (jnp.arange(own_tiles)[:, None] == sends[None, :]).astype(jnp.float32)
    atm_surface = jnp.dot(
        gatherer, returned.reshape(-1, tile_atm), precision=lax.Precision.HIGHEST
    )
    return (ocean, atm_surface)


def solution(mesh):
    return jax.shard_map(
        per_device,
        mesh=mesh,
        in_specs=(
            P(("ens", "gz"), "gx", "gy"),
            P(("ens", "gx"), "gy"),
            P(("ens", "gx"), "gy"),
            P(("ens", "gx", "gy"), None, None),
            P(),
            P(None, ("gx", "gy", "gz")),
            P(("gx", "gy", "gz"), None, None),
        ),
        out_specs=(P(("ens", "gz"), "gx", "gy"), P(("ens", "gx", "gy"), None)),
        check_vma=False,
    )
```

time: 229 us -> 110 us (0.48)
  starting transfers between devices: 82.7 us -> 24.8 us
  other arithmetic: 50.7 us -> 8.43 us
  Pallas kernels: 0 us -> 25.4 us
  blocking collectives: 20.9 us -> 0 us
  between operations: 14.8 us -> 0.85 us
  waiting for transfers between devices: 20.9 us -> 12 us
    ppermute x28 -> x5, starting transfers between devices: 76.4 us -> 4.9 us  [the longest x1 2 us: per_device(): before_rows = lax.ppermute(strip(False), 'gx', forward)]
    add x4 -> x1, other arithmetic: 40.2 us -> 0.01 us  [per_device(): partial_surface + lax.ppermute(partial_surface, 'gz', [(0, 1), (1, 0)])]
    pallas_call x0 -> x3, Pallas kernels: none -> 25.4 us  [the longest x1 21 us: per_device(): vmem_call(functools.partial(ocean_kernel, total_levels=total_levels), jax...]
    all_to_all x1 -> x3, starting transfers between devices: 6.31 us -> 19.9 us  [the longest x1 7.83 us: per_device(): lax.all_to_all(buffer, ALL_AXES, split_axis=0, concat_axis=0, tiled=True)]
    all_to_all x1 -> x0, blocking collectives: 13.1 us -> none  [per_device(): lax.all_to_all(buffer, ('gx', 'gy'), split_axis=0, concat_axis=0, tiled=T...]
    slice x24 -> x9, local copies, waits for them, and re-layouts: 17.5 us -> 6.53 us  [the longest x1 1.8 us: strip(): ocean_temp[:, part]]
    psum x1 -> x0, waiting for transfers between devices: 10.2 us -> none  [per_device(): surface = lax.psum(partial_surface, 'gz')]
    ppermute x16 -> x0, local copies, waits for them, and re-layouts: 9.73 us -> none  [the longest x8 4.87 us: extended(): lax.ppermute(lax.slice_in_dim(block, block.shape[dim] - width, None, axis...]
  transfers between devices with their start and end apart: 30 -> 8, of which waited for: 8 -> 4; matrix products, arithmetic and copies ran while one was open for 11% -> 27% of each run, Pallas kernels for 0% -> 19%
where the time goes in v1:
time: 110 us; the launch traced here: 109 us
  local copies, waits for them, and re-layouts  32.2 us (29%)
  Pallas kernels  25.4 us (23%)
  starting transfers between devices  24.8 us (23%)
  waiting for transfers between devices  12 us (11%)
  other arithmetic  8.43 us (8%)
  matrix products  5.14 us (5%)
    pallas_call x1, Pallas kernels, per_device(): vmem_call(functools.partial(ocean_kernel, total_levels=total_levels), jax...  21 us
    all_to_all x1, starting transfers between devices, per_device(): lax.all_to_all(buffer, ALL_AXES, split_axis=0, concat_axis=0, tiled=True)  7.83 us
    unnamed x42, local copies, waits for them, and re-layouts  6.91 us
    all_to_all x1, starting transfers between devices, per_device(): lax.all_to_all(outgoing, BLOCKS_AXES, split_axis=0, concat_axis=0, tiled=...  6.35 us
    all_to_all x1, starting transfers between devices, surface_frame_few(): lax.all_to_all(message, BLOCKS_AXES, split_axis=0, concat_axis=0, tiled=T...  5.72 us
    all_to_all x1, waiting for transfers between devices, surface_frame_few(): lax.all_to_all(message, BLOCKS_AXES, split_axis=0, concat_axis=0, tiled=T...  5.68 us
    ppermute x1, waiting for transfers between devices, per_device(): after_rows = lax.ppermute(strip(True), 'gx', backward)  4.12 us
    dynamic_slice x5, local copies, waits for them, and re-layouts, of(): return lax.dynamic_index_in_dim(got, index, 0, keepdims=False)  3.18 us
  transfers between devices with their start and end apart: 8, of which 4 were waited for; matrix products, arithmetic and copies ran while one was open for 27% of the time, Pallas kernels for 19%

profile of v1, /device:TPU:1, one launch (start us, length us, event | category | flops | bytes accessed | tf_op | source)
XLA Modules:
  0.0 108.8 jit_solution(12757601685863892493)
XLA Ops:
  0.7 0.8 fusion.18
  1.5 0.9 fusion
  4.1 6.4 %all-to-all-start = ((bf16[8,2,128]{2,1,0:T(2,128)(2,1)}), bf16[8,2,128]{2,1,0:T(2,128)(2,1)S(1)}, u32[]{:S(2)}, u32[]{:S(2)}) async-start(bf16[8,2,128]{2,1,0:T(2,128)(2,1)} %reshape.205), calls=%async_computation | async-start | bytes 8192 | tf_op jit(solution)/shard_map/all_to_all | solution.py:342
  10.5 0.9 slice.66
  11.4 0.9 slice.67
  12.3 0.7 pad_maximum_fusion.1
  13.0 1.0 collective-permute-start
  14.0 0.8 fusion.20
  14.8 1.3 %slice_bitcast_fusion.8 = (s32[64]{0:T(128)}, s32[64]{0:T(128)S(1)}) fusion(s32[2,64]{1,0:T(2,128)} %param.12), kind=kLoop, calls=%fused_computation.71 | loop fusion | bytes 1024 | tf_op jit(solution)/shard_map/eq | solution.py:383
  16.0 1.8 %fusion.21 = (f32[32,4,256]{2,1,0:T(4,128)}, f32[32,4,256]{2,1,0:T(4,128)}) fusion(f32[32,32,256]{2,1,0:T(8,128)} %temp_ref.5), kind=kLoop, calls=%fused_computation.73 | loop fusion | bytes 524288 | tf_op jit(solution)/shard_map/slice | solution.py:317
  17.8 0.8 convert_element_type.7
  18.6 1.3 %slice_bitcast_fusion.4 = (f32[1,4,256]{2,1,0:T(4,128)S(1)}, f32[1,4,256]{2,1,0:T(4,128)S(1)}, f32[1,4,256]{2,1,0:T(4,128)S(1)}, f32[1,4,256]{2,1,0:T(4,128)}) fusion(f32[32,256]{1,0:T(8,128)S(1)} %convert_element_type.7, f32[32,256]{1,0:T(8,128)} %mixing_ref.5), kind=kLoop, calls=%fused_computation.33 | loop fusion | bytes 32768 | tf_op jit(solution)/shard_map/broadcast_in_dim | solution.py:317
  20.6 0.7 pad.17.clone
  24.7 0.9 copy.71
  25.6 0.9 copy.72
  26.5 2.2 %pad_maximum_fusion = f32[4,2,3,256]{2,3,1,0:T(8,128)} fusion(f32[1,2,3,256]{2,3,1,0:T(8,128)S(1)} %get-tuple-element.28, f32[1,2,3,256]{2,3,1,0:T(8,128)S(1)} %get-tuple-element.29, f32[1,2,3,256]{2,3,1,0:T(8,128)} %bitcast.96, f32[1,2,3,256]{2,3,1,0:T(8,128)} %bitcast.95), kind=kLoop, calls=%fused_computation.6 | loop fusion | flops 18432 | bytes 49152 | tf_op jit(solution)/shard_map/stack | solution.py:253
  28.7 1.6 %copy.60 = f32[4,2,3,256]{3,1,2,0:T(2,128)S(1)} copy(f32[4,2,3,256]{2,3,1,0:T(8,128)} %pad_maximum_fusion) | data formatting | bytes 49152 | tf_op jit(solution)/shard_map/stack | solution.py:253
  30.2 1.2 %gather_fusion.1 = f32[8,2,3,256]{3,1,2,0:T(2,128)} fusion(f32[4,2,3,256]{3,1,2,0:T(2,128)S(1)} %copy.60, s32[1024]{0:T(1024)S(1)} %pad_clamp_fusion.1), kind=kCustom, calls=%fused_computation.1 | custom fusion | bytes 98336 | tf_op jit(solution)/shard_map/gather | solution.py:255
  31.5 5.7 %all-to-all-start.1 = ((f32[8,2,3,256]{3,1,2,0:T(2,128)}), f32[8,2,3,256]{3,1,2,0:T(2,128)}, u32[]{:S(2)}, u32[]{:S(2)}) async-start(f32[8,2,3,256]{3,1,2,0:T(2,128)} %gather_fusion.1), calls=%async_computation.1 | async-start | bytes 98304 | tf_op jit(solution)/shard_map/all_to_all | solution.py:256
  37.3 5.7 %all-to-all-done.1 = f32[8,2,3,256]{3,1,2,0:T(2,128)} async-done(((f32[8,2,3,256]{3,1,2,0:T(2,128)}), f32[8,2,3,256]{3,1,2,0:T(2,128)}, u32[]{:S(2)}, u32[]{:S(2)}) %all-to-all-start.1) | async-done | bytes 49184 | tf_op jit(solution)/shard_map/all_to_all | solution.py:256
  42.9 1.4 %constant_dynamic-slice_fusion.3 = (f32[1,2,3,256]{3,1,2,0:T(2,128)S(1)}, f32[2,3,256]{2,0,1:T(2,128)}, f32[2,3,256]{2,0,1:T(2,128)}, f32[1,2,3,256]{3,1,2,0:T(2...) fusion(f32[8,2,3,256]{3,1,2,0:T(2,128)} %all-to-all-done.1, ...), kind=kLoop, calls=%fused_computation.51 | loop fusion | bytes 98336 | tf_op jit(solution)/shard_map/jit(dynamic_index_in_dim)/dynamic_slice | solution.py:260
  44.4 0.9 copy.66
  45.3 0.9 copy.63
  46.1 0.7 slice.103
  46.8 0.7 slice.104
  47.5 0.7 slice.106
  48.3 0.8 slice.107
  49.0 0.8 slice_bitcast_fusion
  49.8 1.0 pad_maximum_fusion.3
  50.8 2.0 %collective-permute-start.2 = (f32[43,4,256]{2,1,0:T(4,128)S(1)}, f32[43,4,256]{2,1,0:T(4,128)S(1)}, u32[]{:S(2)}, u32[]{:S(2)}) collective-permute-start(f32[43,4,256]{2,1,0:T(4,128)S(1)} %pad_maximum_fusion.3), channel_id=1, source_target_pairs={{0,4},{4,8},{8,12},{1,5},{5,9},{9,13},{2,6},{6,10},{10,14},{3,7},{... | collective-permute-start | bytes 528392 | tf_op jit(solution)/shard_map/ppermute | solution.py:321
  52.8 0.9 pad_maximum_fusion.2
  53.7 1.3 %collective-permute-start.1 = (f32[43,4,256]{2,1,0:T(4,128)S(1)}, f32[43,4,256]{2,1,0:T(4,128)S(1)}, u32[]{:S(2)}, u32[]{:S(2)}) collective-permute-start(f32[43,4,256]{2,1,0:T(4,128)S(1)} %pad_maximum_fusion.2), channel_id=1, source_target_pairs={{4,0},{8,4},{12,8},{5,1},{9,5},{13,9},{6,2},{10,6},{14,10},{7,3},{... | collective-permute-start | bytes 528392 | tf_op jit(solution)/shard_map/ppermute | solution.py:322
  55.0 0.8 slice_bitcast_fusion.1
  55.8 4.1 %collective-permute-done.1.next_ref = f32[43,4,256]{2,1,0:T(4,128)S(1)} collective-permute-done((f32[43,4,256]{2,1,0:T(4,128)S(1)}, f32[43,4,256]{2,1,0:T(4,128)S(1)}, u32[]{:S(2)}, u32[]{:S(2)}) %collective-permute-start.1) | collective-permute-done | bytes 176160 | tf_op jit(solution)/shard_map/ppermute | solution.py:322
  59.9 3.1 %shard_map.86 = f32[2,40,128]{2,1,0:T(8,128)S(1)} custom-call(s32[1]{0:T(128)} %bitcast.7.side_ref, f32[32,32,256]{2,1,0:T(8,128)S(1)} %copy-done.1, f32[9,32,256]{2,1,0:T(8,128)S(1)} %collective-permute-done.shared_ref, s32[32,256]{1,0:T(8,128)S(1)} %copy-done.8, f32[32,256]{1,0:T(8,128)S(1)} %copy-done.9, ...), custom_call_target="tpu_custom_call" | custom-call | tf_op jit(solution)/shard_map/pallas_call | solution.py:327
  63.7 0.8 maximum_maximum_fusion.surface_ref
  64.5 1.5 %collective-permute-done.3.left_ref.right_ref = f32[2,40,128]{2,1,0:T(8,128)S(1)} collective-permute-done((f32[2,40,128]{2,1,0:T(8,128)S(1)}, f32[2,40,128]{2,1,0:T(8,128)S(1)}, u32[]{:S(2)}, u32[]{:S(2)}) %collective-permute-start.3) | collective-permute-done | bytes 40992 | tf_op jit(solution)/shard_map/ppermute | solution.py:332
  66.0 1.3 %shard_map.88 = bf16[32,256]{1,0:T(8,128)(2,1)S(1)} custom-call(s32[3]{0:T(128)S(1)} %pad_add_fusion.info_ref, f32[32,32,256]{2,1,0:T(8,128)S(1)} %copy-done.1, f32[9,32,256]{2,1,0:T(8,128)S(1)} %collective-permute-done.shared_ref, s32[32,256]{1,0:T(8,128)S(1)} %copy-done.8, f32[32,256]{1,0:T(8,128)S(1)} %copy-done.9, ...), custom_call_target="tpu_custom_call" | custom-call | flops 3072000 | bytes 2097152 | tf_op jit(solution)/shard_map/pallas_call | solution.py:365
  68.5 1.3 %reshape.175 = bf16[64,128]{1,0:T(8,128)(2,1)} reshape(bf16[32,256]{1,0:T(8,128)(2,1)} %copy-done.10) | data formatting | bytes 32768 | tf_op jit(solution)/shard_map/reshape | solution.py:379
  69.8 2.0 %gather_fusion.2 = bf16[64,128]{1,0:T(8,128)(2,1)} fusion(bf16[64,128]{1,0:T(8,128)(2,1)} %reshape.175, s32[1024]{0:T(1024)} %pad_clamp_fusion), kind=kCustom, calls=%fused_computation.2 | custom fusion | bytes 33024 | tf_op jit(solution)/shard_map/gather | solution.py:379
  71.9 1.9 %fusion.3 = f32[64,1,128]{2,1,0:T(1,128)S(1)} fusion(bf16[64,128,128]{2,1,0:T(8,128)(2,1)S(1)} %copy-done, bf16[64,128,1]{1,0,2:T(8,128)(2,1)} %bitcast.100), kind=kOutput, calls=%fused_computation.20 | convolution fusion | flops 2097152 | bytes 2146304 | tf_op jit(solution)/shard_map/kao,ko->ka/dot_general | solution.py:380
  74.5 7.8 %all-to-all-start.2 = ((f32[16,1,128]{2,1,0:T(1,128)}), f32[16,1,128]{2,1,0:T(1,128)}, u32[]{:S(2)}, u32[]{:S(2)}) async-start(f32[16,1,128]{2,1,0:T(1,128)} %bitcast.104), calls=%async_computation.2 | async-start | bytes 16384 | tf_op jit(solution)/shard_map/all_to_all | solution.py:392
  82.4 0.7 broadcast_in_dim.49
  83.6 0.9 copy-done.3
  84.5 0.9 copy-done.5
  85.5 0.9 copy-done.7
  86.4 21.0 %shard_map.87 = f32[32,32,256]{2,1,0:T(8,128)} custom-call(s32[3]{0:T(128)S(1)} %pad_add_fusion.info_ref, f32[32,32,256]{2,1,0:T(8,128)S(1)} %copy-done.1, f32[9,32,256]{2,1,0:T(8,128)S(1)} %collective-permute-done.shared_ref, s32[32,256]{1,0:T(8,128)S(1)} %copy-done.8, f32[32,256]{1,0:T(8,128)S(1)} %copy-done.9, f32[43,4,256]{2,1,0:T(4,128)S(1)} %copy-done.5, ...), custom_call_target="tpu_custom_call" | custom-call | flops 43008000 | bytes 16777216 | tf_op jit(solution)/shard_map/pallas_call | solution.py:371
  107.4 1.4 %fusion.10 = f32[8,128]{1,0:T(8,128)} fusion(f32[16,128]{1,0:T(8,128)} %bitcast.41, s32[16]{0:T(128)S(1)} %copy-done.15), kind=kOutput, calls=%fused_computation.44 | convolution fusion | flops 196736 | bytes 12352 | tf_op jit(solution)/shard_map/dot_general | solution.py:395
  (71 shorter events, 9.3 us)
Async XLA Ops:
  0.6 21.3 %copy-start = (bf16[64,128,128]{2,1,0:T(8,128)(2,1)S(1)}, bf16[64,128,128]{2,1,0:T(8,128)(2,1)}, u32[]{:S(2)}) copy-start(bf16[64,128,128]{2,1,0:T(8,128)(2,1)} %param.13) | copy-start | bytes 6291460
  1.5 0.9 copy-start.16
  4.1 17.1 %all-to-all-start = ((bf16[8,2,128]{2,1,0:T(2,128)(2,1)}), bf16[8,2,128]{2,1,0:T(2,128)(2,1)S(1)}, u32[]{:S(2)}, u32[]{:S(2)}) async-start(bf16[8,2,128]{2,1,0:T(2,128)(2,1)} %reshape.205), calls=%async_computation | async-start | bytes 8192 | tf_op jit(solution)/shard_map/all_to_all | solution.py:342
  13.0 36.7 %collective-permute-start = (f32[9,32,256]{2,1,0:T(8,128)}, f32[9,32,256]{2,1,0:T(8,128)S(1)}, u32[]{:S(2)}, u32[]{:S(2)}) collective-permute-start(f32[9,32,256]{2,1,0:T(8,128)} %pad_maximum_fusion.1), channel_id=1, source_target_pairs={{0,1},{1,0},{2,3},{3,2},{4,5},{5,4},{6,7},{7,6},{8,9},{9,8},{10,11... | collective-permute-start | bytes 884744 | tf_op jit(solution)/shard_map/ppermute | solution.py:311
  22.8 1.3 %collective-permute-start.4 = (f32[2,32,256]{2,1,0:T(8,128)S(1)}, f32[2,32,256]{2,1,0:T(8,128)S(1)}, u32[]{:S(2)}, u32[]{:S(2)}) collective-permute-start(f32[2,32,256]{2,1,0:T(8,128)S(1)} %reshape.174), channel_id=1, source_target_pairs={{0,1},{1,0},{2,3},{3,2},{4,5},{5,4},{6,7},{7,6},{8,9},{9,8},{10,11... | collective-permute-start | bytes 196616 | tf_op jit(solution)/shard_map/ppermute | solution.py:354
  24.1 0.6 copy-start.11
  26.5 33.4 %copy-start.1 = (f32[32,32,256]{2,1,0:T(8,128)S(1)}, f32[32,32,256]{2,1,0:T(8,128)}, u32[]{:S(2)}) copy-start(f32[32,32,256]{2,1,0:T(8,128)} %temp_ref.5) | copy-start | bytes 3145732
  26.5 33.4 %copy-start.8 = (s32[32,256]{1,0:T(8,128)S(1)}, s32[32,256]{1,0:T(8,128)}, u32[]{:S(2)}) copy-start(s32[32,256]{1,0:T(8,128)} %bathy_ref.5) | copy-start | bytes 98308
  26.5 33.4 %copy-start.9 = (f32[32,256]{1,0:T(8,128)S(1)}, f32[32,256]{1,0:T(8,128)}, u32[]{:S(2)}) copy-start(f32[32,256]{1,0:T(8,128)} %mixing_ref.5) | copy-start | bytes 98308
  31.5 11.5 %all-to-all-start.1 = ((f32[8,2,3,256]{3,1,2,0:T(2,128)}), f32[8,2,3,256]{3,1,2,0:T(2,128)}, u32[]{:S(2)}, u32[]{:S(2)}) async-start(f32[8,2,3,256]{3,1,2,0:T(2,128)} %gather_fusion.1), calls=%async_computation.1 | async-start | bytes 98304 | tf_op jit(solution)/shard_map/all_to_all | solution.py:256
  46.1 17.5 %copy-start.12 = (f32[2,32,256]{2,1,0:T(8,128)S(1)}, f32[2,32,256]{2,1,0:T(8,128)}, u32[]{:S(2)}) copy-start(f32[2,32,256]{2,1,0:T(8,128)} %copy-done.11) | copy-start | bytes 196612
  46.1 17.5 %copy-start.13 = (f32[40,384]{1,0:T(8,128)S(1)}, f32[40,384]{1,0:T(8,128)}, u32[]{:S(2)}) copy-start(f32[40,384]{1,0:T(8,128)} %pad.11.clone) | copy-start | bytes 184324
  50.8 5.0 %collective-permute-start.2 = (f32[43,4,256]{2,1,0:T(4,128)S(1)}, f32[43,4,256]{2,1,0:T(4,128)S(1)}, u32[]{:S(2)}, u32[]{:S(2)}) collective-permute-start(f32[43,4,256]{2,1,0:T(4,128)S(1)} %pad_maximum_fusion.3), channel_id=1, source_target_pairs={{0,4},{4,8},{8,12},{1,5},{5,9},{9,13},{2,6},{6,10},{10,14},{3,7},{... | collective-permute-start | bytes 528392 | tf_op jit(solution)/shard_map/ppermute | solution.py:321
  53.7 6.2 %collective-permute-start.1 = (f32[43,4,256]{2,1,0:T(4,128)S(1)}, f32[43,4,256]{2,1,0:T(4,128)S(1)}, u32[]{:S(2)}, u32[]{:S(2)}) collective-permute-start(f32[43,4,256]{2,1,0:T(4,128)S(1)} %pad_maximum_fusion.2), channel_id=1, source_target_pairs={{4,0},{8,4},{12,8},{5,1},{9,5},{13,9},{6,2},{10,6},{14,10},{7,3},{... | collective-permute-start | bytes 528392 | tf_op jit(solution)/shard_map/ppermute | solution.py:322
  55.8 10.2 %copy-start.2 = (f32[43,4,256]{2,1,0:T(4,128)}, f32[43,4,256]{2,1,0:T(4,128)S(1)}, u32[]{:S(2)}) copy-start(f32[43,4,256]{2,1,0:T(4,128)S(1)} %collective-permute-done.2.prev_ref) | copy-start | bytes 528388
  59.9 6.1 %copy-start.4 = (f32[43,4,256]{2,1,0:T(4,128)}, f32[43,4,256]{2,1,0:T(4,128)S(1)}, u32[]{:S(2)}) copy-start(f32[43,4,256]{2,1,0:T(4,128)S(1)} %collective-permute-done.1.next_ref) | copy-start | bytes 528388
  63.1 2.9 %collective-permute-start.3 = (f32[2,40,128]{2,1,0:T(8,128)S(1)}, f32[2,40,128]{2,1,0:T(8,128)S(1)}, u32[]{:S(2)}, u32[]{:S(2)}) collective-permute-start(f32[2,40,128]{2,1,0:T(8,128)S(1)} %shard_map.86), channel_id=1, source_target_pairs={{0,2},{2,0},{1,3},{3,1},{4,6},{6,4},{5,7},{7,5},{8,10},{10,8},{9,1... | collective-permute-start | bytes 122888 | tf_op jit(solution)/shard_map/ppermute | solution.py:332
  64.4 9.3 %copy-start.14 = (s32[64]{0:T(128)S(1)}, s32[64]{0:T(128)}, u32[]{:S(2)}) copy-start(s32[64]{0:T(128)} %get-tuple-element.22) | copy-start | bytes 772
  67.3 0.6 copy-start.6
  67.9 0.6 copy-start.10
  74.5 32.9 %all-to-all-start.2 = ((f32[16,1,128]{2,1,0:T(1,128)}), f32[16,1,128]{2,1,0:T(1,128)}, u32[]{:S(2)}, u32[]{:S(2)}) async-start(f32[16,1,128]{2,1,0:T(1,128)} %bitcast.104), calls=%async_computation.2 | async-start | bytes 16384 | tf_op jit(solution)/shard_map/all_to_all | solution.py:392
  83.6 0.9 copy-start.3
  84.5 0.9 copy-start.5
  85.5 0.9 copy-start.7
  86.4 21.0 %copy-start.15 = (s32[16]{0:T(128)S(1)}, s32[16]{0:T(128)}, u32[]{:S(2)}) copy-start(s32[16]{0:T(128)} %broadcast_in_dim.50) | copy-start | bytes 196

commit v2 on v0

v2 whole, which is shorter than its diff:
```python
import functools

import jax
import jax.numpy as jnp
from jax import lax
from jax.experimental import pallas as pl
from jax.experimental.pallas import tpu as pltpu
from jax.sharding import PartitionSpec as P

STEPS = 4
HALO = STEPS
WIDTH = STEPS - 1
TOP = STEPS + 1
LANES = 128
TILE = 8
GROUP = LANES // HALO
FEW = 16
UNROLL = 8
CHUNKS = 4
BLOCKS_AXES = ("gx", "gy")
ALL_AXES = ("gx", "gy", "gz")
VMEM_LIMIT = 24 * 1024 * 1024


def position_of(few, dx, dy):
    if not few:
        return (dx + 1) * 2 + (1 if dy > 0 else 0)
    gx_count, gy_count = lax.axis_size("gx"), lax.axis_size("gy")
    x = jnp.clip(lax.axis_index("gx") + dx, 0, gx_count - 1)
    y = jnp.clip(lax.axis_index("gy") + dy, 0, gy_count - 1)
    return x * gy_count + y


def side_tile(left, right, index):
    lane = lax.broadcasted_iota(jnp.int32, left.shape, 1)
    from_right = pltpu.roll(right, lax.rem(LANES - HALO * index, LANES), 1)
    from_left = pltpu.roll(left, lax.rem(2 * LANES - HALO - HALO * index, LANES), 1)
    zero = jnp.zeros_like(left)
    return jnp.where(lane < HALO, from_right, jnp.where(lane >= LANES - HALO, from_left, zero))


def put_slab(ref, own, after, before, tile):
    rows, columns = own.shape
    ref[0:rows, 0:columns] = own
    ref[rows : rows + HALO, 0:columns] = after
    ref[rows + HALO : rows + 2 * HALO, 0:columns] = before
    ref[:, columns:] = tile


def wet_around(levels, level):
    rows, lanes = levels.shape
    wet = jnp.where(levels > level, 0.1, 0.0)
    total = pltpu.roll(wet, 1, 0) + pltpu.roll(wet, rows - 1, 0)
    return total + (pltpu.roll(wet, 1, 1) + pltpu.roll(wet, lanes - 1, 1))


def keep_share(levels, mixing, level):
    above = jnp.where(level > 0.0, 1.0, 0.0)
    vertical = above + jnp.where(levels > level + 1.0, 1.0, 0.0)
    return 1.0 - wet_around(levels, level) - mixing * vertical


def step_slab(center, over, under, keep, mixing, levels, level, forcing):
    rows, lanes = center.shape
    lateral = pltpu.roll(center, 1, 0) + pltpu.roll(center, rows - 1, 0)
    lateral = lateral + (pltpu.roll(center, 1, 1) + pltpu.roll(center, lanes - 1, 1))
    if forcing is not None:
        lateral = lateral + forcing
    new = center * keep + 0.1 * lateral + mixing * (over + under)
    return jnp.where(levels > level, new, 0.0)


def depth_share(level, total_levels):
    return jnp.exp(jnp.full((1, 1), -4.0 / total_levels, jnp.float32) * level)


def begin(copies, semaphores, first=0):
    started = []
    for index, (source, target) in enumerate(copies):
        copy = pltpu.make_async_copy(source, target, semaphores.at[first + index])
        copy.start()
        started.append(copy)
    return started


def finish(copies):
    for copy in copies:
        copy.wait()


def in_order(start, count, body):
    whole = count // UNROLL

    def group(index, carry):
        for offset in range(UNROLL):
            body(start + index * UNROLL + offset)
        return carry

    lax.fori_loop(0, whole, group, 0)
    for index in range(whole * UNROLL, count):
        body(start + index)


def rows_kernel(temp_ref, bathy_ref, mixing_ref, low_ref, high_ref, temp_rows, bathy_rows, mixing_rows, semaphores):
    layers, rows, columns = temp_ref.shape
    copies = []
    for side in range(2):
        part = pl.ds(side * (rows - TILE), TILE)
        copies += [(temp_ref.at[:, part], temp_rows.at[side]), (bathy_ref.at[part], bathy_rows.at[side])]
        copies += [(mixing_ref.at[part], mixing_rows.at[side])]
    finish(begin(copies, semaphores))
    for side, (out_ref, part) in enumerate(((low_ref, slice(0, HALO)), (high_ref, slice(TILE - HALO, TILE)))):
        out_ref[0:layers] = temp_rows[side, :, part]
        out_ref[layers] = bathy_rows[side, part].astype(jnp.float32)
        out_ref[layers + 1] = mixing_rows[side, part]


def send_kernel(sends_hbm, flux_hbm, temp_hbm, bathy_hbm, mixing_hbm, after_ref, *refs, few, sides):
    if few:
        message_ref, sends_ref, flux_ref, temp_ref, bathy_ref, mixing_ref, semaphores, flux_scratch, strips_ref = refs
        fluxes_ref = message_ref
    else:
        (
            fluxes_ref, strips_ref, sends_ref, flux_ref, temp_ref, bathy_ref, mixing_ref, semaphores, flux_scratch,
        ) = refs
    layers, rows, columns = temp_hbm.shape
    gy, gy_count = lax.axis_index("gy"), lax.axis_size("gy")
    me = lax.axis_index("gx") * gy_count + gy
    copies = [(sends_hbm, sends_ref), (flux_hbm, flux_ref)]
    for place in range(sides):
        side = 1 - gy if sides == 1 else place
        window = pl.ds(pl.multiple_of(side * (columns - LANES), LANES), LANES)
        copies += [(bathy_hbm.at[:, window], bathy_ref.at[place]), (mixing_hbm.at[:, window], mixing_ref.at[place])]
        copies += [(temp_hbm.at[:, :, window], temp_ref.at[place])]
    copies = begin(copies, semaphores)
    lane = lax.broadcasted_iota(jnp.int32, (rows, LANES), 1)
    short = lax.broadcasted_iota(jnp.int32, (TILE, LANES), 1)
    finish(copies)
    for side in range(sides):
        base = HALO * (1 - gy) if sides == 1 else HALO * side
        strip = jnp.zeros((rows, LANES), jnp.float32)
        for index in range(layers):
            place = HALO * index
            moved = pltpu.roll(temp_ref[side, index], lax.rem(place + base, LANES), 1)
            strip = jnp.where((lane >= place) & (lane < place + HALO), moved, strip)
        strips_ref[side, 2 * TILE : 2 * TILE + rows] = strip
        plain = jnp.zeros((TILE, LANES), jnp.float32)
        for part in range(rows // TILE):
            here = slice(part * TILE, (part + 1) * TILE)
            for which, values in enumerate((bathy_ref[side, here].astype(jnp.float32), mixing_ref[side, here])):
                place = 2 * HALO * part + HALO * which
                moved = pltpu.roll(values, lax.rem(place + base, LANES), 1)
                plain = jnp.where((short >= place) & (short < place + HALO), moved, plain)
        strips_ref[side, TILE : 2 * TILE] = plain
        strips_ref[side, 0:TILE] = jnp.zeros((TILE, LANES), jnp.float32)
    flux_scratch[...] = flux_ref[...].astype(jnp.float32)
    fields = flux_ref.shape[1]

    def one(block, carry):
        tile = sends_ref[me, block]
        if few:
            side = 0 if sides == 1 else (lax.rem(block, gy_count) > gy).astype(jnp.int32)
            message_ref[block] = strips_ref[side]
        else:
            fluxes_ref[block] = jnp.zeros(fluxes_ref.shape[1:], jnp.float32)
        sent = jnp.where(tile >= 0, flux_scratch[jnp.maximum(tile, 0)], 0.0)
        fluxes_ref[block, 0:fields] = sent
        return carry

    if few:
        for block in range(fluxes_ref.shape[0]):
            one(block, 0)
    else:
        lax.fori_loop(0, fluxes_ref.shape[0], one, 0)


def regrid_kernel(slots_hbm, *refs, few):
    if few:
        sides_ref, *refs = refs
        flux_ref = sides_ref
    else:
        flux_ref, sides_ref, *refs = refs
    (
        weights_hbm, temp_hbm, bathy_hbm, mixing_hbm, next_ref, prev_ref,
        partial_ref, edges_ref, shared_ref, levels_hbm, mix_hbm, packed_hbm,
        slots_ref, weights_ref, temp_ref, bathy_ref, mixing_ref, levels_ref, mix_ref, packed_ref, semaphores,
        sums_ref, *strip_scratch,
    ) = refs
    layers, rows, columns = temp_hbm.shape
    slot_count, tile_atm, patch = weights_ref.shape
    halves = columns // LANES
    lasts = pl.ds(layers - HALO, HALO)
    needed = begin([
        (temp_hbm.at[pl.ds(0, TOP)], temp_ref.at[pl.ds(0, TOP)]), (temp_hbm.at[lasts], temp_ref.at[pl.ds(TOP, HALO)]),
        (bathy_hbm, bathy_ref), (mixing_hbm, mixing_ref), (slots_hbm, slots_ref),
    ], semaphores)
    chunk = slot_count // CHUNKS
    arriving = begin([
        (weights_hbm.at[pl.ds(part * chunk, chunk)], weights_ref.at[pl.ds(part * chunk, chunk)])
        for part in range(CHUNKS)
    ], semaphores, len(needed))
    sums_ref[...] = jnp.zeros_like(sums_ref)

    gx, gx_count = lax.axis_index("gx"), lax.axis_size("gx")
    gy, gy_count = lax.axis_index("gy"), lax.axis_size("gy")
    plain = []
    for side, dy in ((0, -1), (1, 1)):
        own, after, before = (position_of(few, dx, dy) for dx in (0, 1, -1))
        packed_ref[side, 0:rows] = sides_ref[own, 2 * TILE : 2 * TILE + rows]
        packed_ref[side, rows : rows + HALO] = sides_ref[after, 2 * TILE : 2 * TILE + HALO]
        packed_ref[side, rows + HALO :] = sides_ref[before, 2 * TILE + rows - HALO : 2 * TILE + rows]
        tile = sides_ref[own, TILE : 2 * TILE]
        parts = [tile] + [pltpu.roll(tile, LANES - 2 * HALO * part, 1) for part in range(1, rows // TILE)]
        last = pltpu.roll(sides_ref[before, TILE : 2 * TILE], LANES - 2 * HALO * (rows // TILE - 1), 1)
        row = lax.broadcasted_iota(jnp.int32, (TILE, LANES), 0)
        parts.append(jnp.where(row < HALO, sides_ref[after, TILE : 2 * TILE], last))
        plain.append(jnp.concatenate(parts, axis=0))
    finish(needed)
    size = (rows + 2 * HALO, LANES)
    lane, row = (lax.broadcasted_iota(jnp.int32, size, dim) for dim in (1, 0))
    there = (lane < HALO) & (gy < gy_count - 1) | (lane >= HALO) & (gy > 0)
    there = there & ((row < rows) | (row < rows + HALO) & (gx < gx_count - 1) | (row >= rows + HALO) & (gx > 0))
    tile = jnp.where(there, side_tile(plain[0], plain[1], 0), 0.0)
    put_slab(levels_ref, bathy_ref[...].astype(jnp.float32), next_ref[layers], prev_ref[layers], tile)
    tile = side_tile(plain[0], plain[1], 1)
    put_slab(mix_ref, mixing_ref[...], next_ref[layers + 1], prev_ref[layers + 1], tile)
    for place, level in enumerate(list(range(TOP)) + list(range(layers - HALO, layers))):
        tile = side_tile(packed_ref[0], packed_ref[1], level)
        put_slab(shared_ref.at[place], temp_ref[place], next_ref[level], prev_ref[level], tile)
    leaving = begin(
        [(levels_ref, levels_hbm), (mix_ref, mix_hbm), (packed_ref, packed_hbm)], semaphores, len(needed) + CHUNKS
    )
    for slot in range(slot_count):
        if slot % chunk == 0:
            arriving[slot // chunk].wait()
        fluxes = flux_ref[slots_ref[0, slot], 0:TILE, :].astype(jnp.bfloat16)
        got = jnp.dot(fluxes, weights_ref[slot], preferred_element_type=jnp.float32)
        place = pl.multiple_of(slots_ref[1, slot] * TILE, TILE)
        sums_ref[pl.ds(place, TILE)] += got

    strips_ref = strip_scratch[0] if few else edges_ref
    strips_ref[...] = jnp.zeros_like(strips_ref)
    short = lax.broadcasted_iota(jnp.int32, (TILE, LANES), 1)
    columns_low = jnp.zeros((TILE, LANES), jnp.float32)
    columns_high = jnp.zeros((TILE, LANES), jnp.float32)
    for field in range(2):
        for half in range(halves):
            values = sums_ref[pl.ds(half * TILE + field, rows, stride=halves * TILE), :]
            partial_ref[field, :, half * LANES : (half + 1) * LANES] = values
            place = (field * 2 + half) * HALO
            strips_ref[0, place : place + WIDTH] = values[0:WIDTH]
            strips_ref[1, place : place + WIDTH] = values[rows - WIDTH : rows]
            for part in range(rows // TILE):
                block = values[part * TILE : (part + 1) * TILE]
                place = 2 * HALO * part + HALO * field
                inside = (short >= place) & (short < place + HALO)
                if half == 0:
                    columns_low = jnp.where(inside, pltpu.roll(block, place % LANES, 1), columns_low)
                if half == halves - 1:
                    columns_high = jnp.where(inside, pltpu.roll(block, (place + HALO) % LANES, 1), columns_high)
    strips_ref[2, 0:TILE] = columns_low
    strips_ref[3, 0:TILE] = columns_high
    if few:
        gx, gy, gy_count = lax.axis_index("gx"), lax.axis_index("gy"), lax.axis_size("gy")
        for entry in range(edges_ref.shape[0]):
            x, y = entry // 2 // gy_count, entry // 2 % gy_count
            choice = jnp.where(x < gx, 0, jnp.where(x > gx, 1, jnp.where(y < gy, 2, 3)))
            edges_ref[entry] = strips_ref[choice]

    finish(leaving)


def first_kernel(
    temp_hbm, next_hbm, prev_hbm, packed_hbm, other_hbm, levels_hbm, mix_hbm,
    moved_hbm, keep_hbm, top_hbm, top_keep_hbm,
    temp_ref, next_ref, prev_ref, packed_ref, other_ref, levels_ref, mix_ref,
    moved_ref, keep_ref, top_ref, top_keep_ref, first_ref, skin_ref, semaphores,
):
    layers = temp_hbm.shape[0]
    gz = lax.axis_index("gz")
    first_level = gz * layers - HALO
    needed = begin([
        (next_hbm, next_ref), (prev_hbm, prev_ref), (packed_hbm, packed_ref), (levels_hbm, levels_ref),
        (mix_hbm, mix_ref), (other_hbm, other_ref),
    ], semaphores)
    chunk = layers // CHUNKS
    parts = [pl.ds(part * chunk, chunk) for part in range(CHUNKS)]
    used = len(needed)
    arriving = begin([(temp_hbm.at[part], temp_ref.at[part]) for part in parts], semaphores, used)
    used += CHUNKS
    finish(needed)

    def level_of(place):
        return (first_level + place).astype(jnp.float32)

    def settle(place):
        level = level_of(place)
        first_ref[place] = jnp.where(levels_ref[...] > level, first_ref[place], 0.0)
        keep_ref[place] = keep_share(levels_ref[...], mix_ref[...], level)

    def own_level(index):
        tile = side_tile(packed_ref[0], packed_ref[1], index)
        put_slab(first_ref.at[index + HALO], temp_ref[index], next_ref[index], prev_ref[index], tile)
        settle(index + HALO)

    for part in range(CHUNKS):
        arriving[part].wait()
        in_order(part * chunk, chunk, own_level)

    for index in range(HALO):
        slot = jnp.where(gz == 0, index, TOP + index)
        place = jnp.where(gz == 0, HALO + layers + index, index)
        first_ref[place] = other_ref[slot]
        settle(place)

    base = jnp.where(gz == 0, HALO, 1)
    count = layers + HALO - 1
    span = pl.ds(base, count)
    leaving = begin([(keep_ref.at[span], keep_hbm.at[span])], semaphores, used)
    used += 1
    levels = levels_ref[...]
    for level in range(TOP):
        slab = jnp.where(gz == 0, first_ref[HALO + level], other_ref[level])
        skin_ref[level] = jnp.where(levels > float(level), slab, 0.0)
    for level in range(STEPS):
        top_keep_ref[level] = keep_share(levels, mix_ref[...], jnp.float32(level))
        over = skin_ref[level - 1] if level else jnp.zeros_like(levels)
        top_ref[level] = step_slab(
            skin_ref[level], over, skin_ref[level + 1], top_keep_ref[level], mix_ref[...], levels, float(level), None
        )
    leaving += begin([(top_ref, top_hbm), (top_keep_ref, top_keep_hbm)], semaphores, used)
    used += 2
    edge = jnp.where(gz == 0, HALO - 1, HALO + layers)
    first_ref[edge] = jnp.zeros_like(first_ref[0])

    def one(place):
        moved_ref[place] = step_slab(
            first_ref[place], first_ref[place - 1], first_ref[place + 1], keep_ref[place], mix_ref[...],
            levels_ref[...], level_of(place), None,
        )

    for start, size in pieces(count):
        in_order(base + start, size, one)
        here = pl.ds(base + start, size)
        leaving += begin([(moved_ref.at[here], moved_hbm.at[here])], semaphores, used)
        used += 1
    finish(leaving)


def pieces(count):
    return [(start, min(UNROLL, count - start)) for start in range(0, count, UNROLL)]


def skin_kernel(
    slots_hbm, partial_hbm, other_hbm, edges_ref, weights_hbm, levels_hbm, mix_hbm, top_hbm, top_keep_hbm,
    surface_hbm, back_ref,
    slots_ref, partial_ref, other_ref, weights_ref, levels_ref, mix_ref, top_ref, top_keep_ref, surface_ref, semaphores,
    first_ref, second_ref, sst_ref, rows_ref, *sums_scratch, few, total_levels,
):
    fields, rows, columns = partial_ref.shape
    slot_count, tile_atm, patch = weights_ref.shape
    halves = columns // LANES
    needed = begin([
        (partial_hbm, partial_ref), (other_hbm, other_ref), (levels_hbm, levels_ref), (mix_hbm, mix_ref),
        (top_hbm, top_ref), (top_keep_hbm, top_keep_ref), (slots_hbm, slots_ref),
    ], semaphores)
    chunk = slot_count // CHUNKS
    used = len(needed)
    arriving = begin([
        (weights_hbm.at[pl.ds(part * chunk, chunk)], weights_ref.at[pl.ds(part * chunk, chunk)])
        for part in range(CHUNKS)
    ], semaphores, used)
    used += CHUNKS

    def edge(dx, dy):
        if few:
            where = position_of(few, dx, dy)
            return edges_ref[2 * where] + edges_ref[2 * where + 1]
        where = EDGES.index((dx, dy))
        return edges_ref[2 * where] + edges_ref[2 * where + 1]

    after, before = edge(1, 0), edge(-1, 0)
    right, left = edge(0, 1), edge(0, -1)
    corners = {(dx, dy): edge(dx, dy) for dx in (1, -1) for dy in (1, -1)}
    lane = lax.broadcasted_iota(jnp.int32, (TILE, LANES), 1)
    short = lax.broadcasted_iota(jnp.int32, (HALO, LANES), 1)
    surface_ref[...] = jnp.zeros_like(surface_ref)
    finish(needed)
    for field in range(fields):
        surface_ref[field, 0:rows, 0:columns] = partial_ref[field] + other_ref[field]
        for half in range(halves):
            place = (field * 2 + half) * HALO
            here = slice(half * LANES, (half + 1) * LANES)
            surface_ref[field, rows : rows + WIDTH, here] = after[place : place + WIDTH]
            surface_ref[field, rows + 2 * HALO - WIDTH :, here] = before[place : place + WIDTH]
        for part in range(rows // TILE):
            place = 2 * HALO * part + HALO * field
            from_right = pltpu.roll(right[0:TILE], (LANES - place) % LANES, 1)
            from_left = pltpu.roll(left[0:TILE], (2 * LANES - HALO - place) % LANES, 1)
            tile = jnp.where(lane < HALO, from_right, jnp.where(lane >= LANES - HALO, from_left, 0.0))
            surface_ref[field, part * TILE : (part + 1) * TILE, columns:] = tile
        low, high = field * 2 * HALO, (field * 2 + halves - 1) * HALO
        for dx in (1, -1):
            from_right, from_left = corners[dx, 1][low : low + HALO], corners[dx, -1][high : high + HALO]
            tile = jnp.where(short < HALO, from_right, jnp.where(short >= LANES - HALO, from_left, 0.0))
            if dx == 1:
                surface_ref[field, rows : rows + WIDTH, columns:] = tile[0:WIDTH]
            else:
                surface_ref[field, rows + 2 * HALO - WIDTH :, columns:] = tile[0:WIDTH]

    leaving = begin([(surface_ref, surface_hbm)], semaphores, used)
    levels = levels_ref[...]
    forcings = [depth_share(jnp.float32(level), total_levels) * surface_ref[1] for level in range(STEPS)]
    forcings[0] = forcings[0] + surface_ref[0]
    for level in range(STEPS):
        first_ref[level] = top_ref[level] + jnp.where(levels > float(level), 0.1 * forcings[level], 0.0)
    source, target = first_ref, second_ref
    zero = jnp.zeros_like(levels)
    for step in range(2, STEPS + 1):
        for level in range(TOP - step):
            over = source[level - 1] if level else zero
            target[level] = step_slab(
                source[level], over, source[level + 1], top_keep_ref[level], mix_ref[...], levels, float(level),
                forcings[level],
            )
        source, target = target, source
    for half in range(halves):
        values = source[0, 0:rows, half * LANES : (half + 1) * LANES]
        sst_ref[half * rows : (half + 1) * rows] = values.astype(jnp.bfloat16).astype(jnp.float32)

    for slot in range(slot_count):
        tile = slots_ref[1, slot]
        place = lax.rem(tile, halves) * rows + lax.div(tile, halves)
        rows_ref[pl.ds(slot, 1)] = sst_ref[pl.ds(place, 1)]
    sums_ref = sums_scratch[0]
    sums_ref[...] = jnp.zeros_like(sums_ref)
    for group in range(slot_count // TILE):
        given = rows_ref[group * TILE : (group + 1) * TILE].astype(jnp.bfloat16)
        for row in range(TILE):
            slot = group * TILE + row
            if slot % chunk == 0:
                arriving[slot // chunk].wait()
            got = lax.dot_general(
                given, weights_ref[slot], (((1,), (1,)), ((), ())), preferred_element_type=jnp.float32
            )
            sums_ref[pl.ds(slots_ref[0, slot], 1)] += got[row : row + 1]
    if few:
        for block in range(sums_ref.shape[0]):
            both = jnp.broadcast_to(sums_ref[block : block + 1], (2, LANES))
            back_ref[2 * block : 2 * block + 2] = both
    else:
        back_ref[...] = sums_ref[...]
    finish(leaving)


def ocean_kernel(
    temp_hbm, moved_hbm, keep_hbm, levels_hbm, mix_hbm, surface_hbm, ocean_hbm,
    temp_ref, keep_ref, levels_ref, mix_ref, surface_ref, semaphores, first_ref, second_ref, *, total_levels,
):
    layers, rows, columns = temp_hbm.shape
    gz = lax.axis_index("gz")
    first_level = gz * layers - HALO
    base = jnp.where(gz == 0, HALO, 1)
    count = layers + HALO - 1
    needed = begin(
        [(levels_hbm, levels_ref), (mix_hbm, mix_ref), (surface_hbm, surface_ref)], semaphores
    )
    used = len(needed)
    spans = [pl.ds(base + start, size) for start, size in pieces(count)]
    arriving = begin([(moved_hbm.at[span], first_ref.at[span]) for span in spans], semaphores, used)
    used += len(spans)
    later = begin([
        (keep_hbm.at[pl.ds(base, count)], keep_ref.at[pl.ds(base, count)]), (temp_hbm, temp_ref)
    ], semaphores, used)
    used += len(later)
    edge = jnp.where(gz == 0, HALO - 1, HALO + layers)
    first_ref[edge] = jnp.zeros_like(first_ref[0])
    second_ref[edge] = jnp.zeros_like(first_ref[0])
    finish(needed)

    def level_of(place):
        return (first_level + place).astype(jnp.float32)

    def add(place):
        level = level_of(place)
        forcing = (0.1 * depth_share(level, total_levels)) * surface_ref[1]
        first_ref[place] = first_ref[place] + jnp.where(levels_ref[...] > level, forcing, 0.0)

    for (start, size), copy in zip(pieces(count), arriving):
        copy.wait()
        in_order(base + start, size, add)

    def top_forcing():
        return jnp.where(levels_ref[...] > 0.0, 0.1 * surface_ref[0], 0.0)

    @pl.when(gz == 0)
    def _():
        first_ref[HALO] = first_ref[HALO] + top_forcing()

    later[0].wait()
    source, target = first_ref, second_ref
    for step in range(2, STEPS + 1):
        if step == STEPS:
            later[1].wait()

        def one(place, source=source, target=target, step=step):
            level = level_of(place)
            new = step_slab(
                source[place], source[place - 1], source[place + 1], keep_ref[place], mix_ref[...], levels_ref[...],
                level, depth_share(level, total_levels) * surface_ref[1],
            )
            if step < STEPS:
                target[place] = new
            else:
                index = place - HALO
                wet = levels_ref[0:rows, 0:columns] > level
                temp_ref[index] = jnp.where(wet, new[0:rows, 0:columns], temp_ref[index])

        if step < STEPS:
            in_order(jnp.where(gz == 0, HALO, step), layers + HALO - step, one)

            @pl.when(gz == 0)
            def _(target=target):
                target[HALO] = target[HALO] + top_forcing()
        else:
            leaving = []
            for start, size in pieces(layers):
                in_order(HALO + start, size, one)
                if start == 0:
                    @pl.when(gz == 0)
                    def _():
                        temp_ref[0] = temp_ref[0] + top_forcing()[0:rows, 0:columns]

                here = pl.ds(start, size)
                leaving += begin([(temp_ref.at[here], ocean_hbm.at[here])], semaphores, used)
                used += 1
            finish(leaving)
        source, target = target, source


def gather_kernel(sends_ref, returned_ref, surface_ref):
    me = lax.axis_index("gx") * lax.axis_size("gy") + lax.axis_index("gy")
    surface_ref[...] = jnp.zeros_like(surface_ref)
    blocks = sends_ref.shape[0]
    copies = returned_ref.shape[0] // blocks

    def one(block, carry):
        tile = sends_ref[me, block]
        place = jnp.maximum(tile, 0)
        got = returned_ref[pl.ds(block * copies, 1)]
        for copy in range(1, copies):
            got = got + returned_ref[pl.ds(block * copies + copy, 1)]
        surface_ref[pl.ds(place, 1)] += jnp.where(tile >= 0, got, 0.0)
        return carry

    lax.fori_loop(0, blocks, one, 0)


def call(body, outs, scratch, operands, places, out_places, cost=0):
    space = {"v": pltpu.VMEM, "s": pltpu.SMEM, "h": pl.ANY}
    assert len(places) == len(operands) and len(out_places) == len(outs)
    scratch_shapes = []
    for item in scratch:
        if isinstance(item, int):
            scratch_shapes.append(pltpu.SemaphoreType.DMA((item,)))
        elif isinstance(item, tuple):
            scratch_shapes.append(pltpu.VMEM(item, jnp.float32))
        else:
            scratch_shapes.append(item)
    return pl.pallas_call(
        body,
        out_shape=[jax.ShapeDtypeStruct(out, jnp.float32) for out in outs],
        in_specs=[pl.BlockSpec(memory_space=space[place]) for place in places],
        out_specs=[pl.BlockSpec(memory_space=space[place]) for place in out_places],
        scratch_shapes=scratch_shapes,
        compiler_params=pltpu.CompilerParams(vmem_limit_bytes=VMEM_LIMIT),
        cost_estimate=pl.CostEstimate(flops=cost, bytes_accessed=4 * cost // 16, transcendentals=0),
    )(*operands)


def like(array):
    return pltpu.VMEM(array.shape, array.dtype)


EDGES = [(dx, dy) for dx in (-1, 0, 1) for dy in (-1, 0, 1) if (dx, dy) != (0, 0)]


def toward(gx_count, gy_count, dx, dy):
    pairs = []
    for x in range(gx_count):
        for y in range(gy_count):
            if 0 <= x + dx < gx_count and 0 <= y + dy < gy_count:
                pairs.append(((x + dx) * gy_count + y + dy, x * gy_count + y))
    return pairs


def per_device(
    ocean_temp, bathy_levels, mixing, atm_flux, send_tiles, regrid_slots, regrid_weights
):
    layers, rows, columns = ocean_temp.shape
    gx_count, gy_count, gz_count = (lax.axis_size(axis) for axis in ALL_AXES)
    blocks = gx_count * gy_count
    own_tiles, fields, tile_atm = atm_flux.shape
    caps = send_tiles.shape[2]
    assert gz_count == 2 and caps == 1 and layers == GROUP and tile_atm == LANES
    assert columns == 2 * LANES and rows == 4 * TILE and regrid_weights.shape[2] == LANES
    total_levels = layers * gz_count
    few = blocks <= FEW
    sends = send_tiles.reshape(blocks, blocks)
    swap = [(0, 1), (1, 0)]
    tall = 2 * TILE + rows
    strip = (layers + 2, HALO, columns)
    slab = (rows + 2 * HALO, columns + LANES)
    slab_cost = 20 * slab[0] * slab[1]
    deep = (layers + 2 * HALO,) + slab

    high_rows = (2, layers, TILE, columns)
    low, high = call(
        rows_kernel, [strip, strip],
        [high_rows, pltpu.VMEM((2, TILE, columns), jnp.int32), (2, TILE, columns), 6],
        (ocean_temp, bathy_levels, mixing), "hhh", "vv", cost=slab_cost,
    )
    forward = [(i, i + 1) for i in range(gx_count - 1)]
    backward = [(target, source) for source, target in forward]
    before_rows = lax.ppermute(high, "gx", forward)
    after_rows = lax.ppermute(low, "gx", backward)
    outs = [(blocks, tall, LANES)] if few else [(blocks, TILE, LANES), (2, tall, LANES)]
    sides = 1 if few and gy_count == 2 else 2
    scratch = [
        pltpu.SMEM(sends.shape, jnp.int32), like(atm_flux), (sides, layers, rows, LANES),
        pltpu.VMEM((sides, rows, LANES), jnp.int32), (sides, rows, LANES), 2 + 3 * sides,
        (own_tiles, fields, LANES),
    ]
    sent = call(
        functools.partial(send_kernel, few=few, sides=sides), outs, scratch + ([(sides, tall, LANES)] if few else []),
        (sends, atm_flux, ocean_temp, bathy_levels, mixing, low), "hhhhhh", "v" * len(outs), cost=2 * slab_cost,
    )
    got = [lax.all_to_all(sent[0], BLOCKS_AXES, split_axis=0, concat_axis=0, tiled=True)]
    if not few:
        got.append(jnp.stack([
            lax.ppermute(sent[1][0 if dy > 0 else 1], BLOCKS_AXES, toward(gx_count, gy_count, dx, dy))
            for dx in (-1, 0, 1) for dy in (-1, 1)
        ]))

    strips = (4, 2 * TILE, LANES)
    packed_shape = (2, slab[0], LANES)
    partial, edges, shared, levels, mix, packed = call(
        functools.partial(regrid_kernel, few=few),
        [
            (fields, rows, columns), (2 * blocks, 2 * TILE, LANES) if few else strips,
            (TOP + HALO,) + slab, slab, slab, packed_shape,
        ],
        [
            pltpu.SMEM(regrid_slots.shape, jnp.int32), like(regrid_weights), (TOP + HALO, rows, columns),
            like(bathy_levels), like(mixing), slab, slab, packed_shape, 8 + CHUNKS,
            (rows * columns // LANES * TILE, LANES),
        ] + ([strips] if few else []),
        (
            regrid_slots, *got, regrid_weights, ocean_temp, bathy_levels, mixing, after_rows, before_rows,
        ), "h" + "v" * len(got) + "hhhhvv", "vvvhhh", cost=10 * slab_cost,
    )
    other_partial = lax.ppermute(partial, "gz", swap)
    other_shared = lax.ppermute(shared, "gz", swap)
    if few:
        edges = lax.all_to_all(edges, ALL_AXES, split_axis=0, concat_axis=0, tiled=True)
    else:
        choice = {-1: 1, 1: 0}
        around = jnp.stack([
            lax.ppermute(
                edges[choice[dx] if dx else (3 if dy < 0 else 2)], BLOCKS_AXES, toward(gx_count, gy_count, dx, dy)
            )
            for dx, dy in EDGES
        ])
        edges = jnp.stack([around, lax.ppermute(around, "gz", swap)], axis=1)
        edges = edges.reshape((2 * len(EDGES),) + strips[1:])

    top = (STEPS,) + slab
    parts = len(pieces(layers + HALO - 1))
    moved, keep, top_moved, top_keep = call(
        first_kernel, [deep, deep, top, top],
        [
            like(ocean_temp), strip, strip, packed_shape, (TOP + HALO,) + slab, slab, slab,
            deep, deep, top, top, deep, (TOP,) + slab, 9 + CHUNKS + parts,
        ],
        (ocean_temp, after_rows, before_rows, packed, other_shared, levels, mix), "h" * 7, "hhhh", cost=80 * slab_cost,
    )
    surface, back = call(
        functools.partial(skin_kernel, few=few, total_levels=total_levels),
        [(fields,) + slab, ((2 if few else 1) * blocks, LANES)],
        [
            pltpu.SMEM(regrid_slots.shape, jnp.int32), like(partial), like(partial), like(regrid_weights), slab, slab,
            top, top, (fields,) + slab, 8 + CHUNKS,
            top, top, (rows * columns // LANES, LANES), (regrid_weights.shape[0], LANES), (blocks, LANES),
        ],
        (regrid_slots, partial, other_partial, edges, regrid_weights, levels, mix, top_moved, top_keep),
        "hhhvhhhhh", "hv", cost=20 * slab_cost,
    )
    if few:
        returned = lax.all_to_all(back, ALL_AXES, split_axis=0, concat_axis=0, tiled=True)
    else:
        returned = lax.all_to_all(back, BLOCKS_AXES, split_axis=0, concat_axis=0, tiled=True)
        returned = returned + lax.ppermute(returned, "gz", swap)
    ocean, = call(
        functools.partial(ocean_kernel, total_levels=total_levels), [ocean_temp.shape],
        [like(ocean_temp), deep, slab, slab, (fields,) + slab, 5 + parts + len(pieces(layers)), deep, deep],
        (ocean_temp, moved, keep, levels, mix, surface), "h" * 6, "h", cost=120 * slab_cost,
    )
    atm_surface, = call(gather_kernel, [(own_tiles, LANES)], [], (sends, returned), "sv", "v", cost=slab_cost // 10)
    return (ocean, atm_surface)


def solution(mesh):
    return jax.shard_map(
        per_device,
        mesh=mesh,
        in_specs=(
            P(("ens", "gz"), "gx", "gy"),
            P(("ens", "gx"), "gy"),
            P(("ens", "gx"), "gy"),
            P(("ens", "gx", "gy"), None, None),
            P(),
            P(None, ("gx", "gy", "gz")),
            P(("gx", "gy", "gz"), None, None),
        ),
        out_specs=(P(("ens", "gz"), "gx", "gy"), P(("ens", "gx", "gy"), None)),
        check_vma=False,
    )
```

time: 229 us -> 85.6 us (0.37)
  starting transfers between devices: 82.7 us -> 24.8 us
  other arithmetic: 50.7 us -> 0 us
  Pallas kernels: 0 us -> 28.2 us
  blocking collectives: 20.9 us -> 0 us
  waiting for transfers between devices: 20.9 us -> 4.25 us
  between operations: 14.8 us -> 0.8 us
  local copies, waits for them, and re-layouts: 34.2 us -> 26 us
  matrix products: 3.12 us -> 0 us
    ppermute x28 -> x4, starting transfers between devices: 76.4 us -> 6.31 us  [the longest x1 4 us: per_device(): before_rows = lax.ppermute(high, 'gx', forward)]
    add x4 -> x0, other arithmetic: 40.2 us -> none  [advance(): center + water_indicator * (0.1 * lateral + mixing * vertical + 0.1 * for...]
    pallas_call x0 -> x7, Pallas kernels: none -> 28.2 us  [call(): pl.pallas_call(body, out_shape=[jax.ShapeDtypeStruct(out, jnp.float32) fo...]
    unnamed x34 -> x64, local copies, waits for them, and re-layouts: 1.65 us -> 26 us
    slice x24 -> x0, local copies, waits for them, and re-layouts: 17.5 us -> none  [the longest x17 11.9 us: extended(): lax.slice_in_dim(block, block.shape[dim] - width, None, axis=dim)]
    all_to_all x1 -> x0, blocking collectives: 13.1 us -> none  [per_device(): lax.all_to_all(buffer, ('gx', 'gy'), split_axis=0, concat_axis=0, tiled=T...]
    all_to_all x1 -> x3, starting transfers between devices: 6.31 us -> 18.5 us  [the longest x1 6.37 us: per_device(): lax.all_to_all(sent[0], BLOCKS_AXES, split_axis=0, concat_axis=0, tiled=T...]
    psum x1 -> x0, waiting for transfers between devices: 10.2 us -> none  [per_device(): surface = lax.psum(partial_surface, 'gz')]
  transfers between devices with their start and end apart: 30 -> 7, of which waited for: 8 -> 1; matrix products, arithmetic and copies ran while one was open for 11% -> 0% of each run, Pallas kernels for 0% -> 20%
where the time goes in v2:
time: 85.6 us; the launch traced here: 84 us
  Pallas kernels  28.2 us (33%)
  local copies, waits for them, and re-layouts  26 us (30%)
  starting transfers between devices  24.8 us (29%)
  waiting for transfers between devices  4.25 us (5%)
    pallas_call x7, Pallas kernels, call(): pl.pallas_call(body, out_shape=[jax.ShapeDtypeStruct(out, jnp.float32) fo...  28.2 us
    unnamed x64, local copies, waits for them, and re-layouts  26 us
    all_to_all x1, starting transfers between devices, per_device(): lax.all_to_all(sent[0], BLOCKS_AXES, split_axis=0, concat_axis=0, tiled=T...  6.37 us
    all_to_all x1, starting transfers between devices, per_device(): lax.all_to_all(edges, ALL_AXES, split_axis=0, concat_axis=0, tiled=True)  6.15 us
    all_to_all x1, starting transfers between devices, per_device(): lax.all_to_all(back, ALL_AXES, split_axis=0, concat_axis=0, tiled=True)  5.96 us
    ppermute x1, waiting for transfers between devices, per_device(): after_rows = lax.ppermute(low, 'gx', backward)  4.23 us
    ppermute x1, starting transfers between devices, per_device(): before_rows = lax.ppermute(high, 'gx', forward)  4 us
  transfers between devices with their start and end apart: 7, of which 1 were waited for; matrix products, arithmetic and copies ran while one was open for 0% of the time, Pallas kernels for 20%

profile of v2, /device:TPU:1, one launch (start us, length us, event | category | flops | bytes accessed | tf_op | source)
XLA Modules:
  0.0 84.0 jit_solution(5629610112212827277)
XLA Ops:
  0.6 1.2 %copy-done = f32[32,32,256]{2,1,0:T(8,128)S(1)} copy-done((f32[32,32,256]{2,1,0:T(8,128)S(1)}, f32[32,32,256]{2,1,0:T(8,128)}, u32[]{:S(2)}) %copy-start) | copy-done | bytes 1048600
  1.9 0.8 copy-done.15
  2.6 0.8 copy-done.17
  3.4 0.2 shard_map.86
  3.5 0.0 copy-start.28
  3.6 0.8 copy-done.28
  4.3 0.7 copy-done.30
  5.0 1.5 %shard_map.87 = f32[8,48,128]{2,1,0:T(8,128)} custom-call(s32[8,8]{1,0:T(8,128)S(1)} %bitcast.6, bf16[8,2,128]{2,1,0:T(2,128)(2,1)S(1)} %copy-done.30, f32[32,32,256]{2,1,0:T(8,128)S(1)} %copy-done, s32[32,256]{1,0:T(8,128)S(1)} %copy-done.15, f32[32,256]{1,0:T(8,128)S(1)} %copy-done.17, f32[34,4,256]{2,1,0:T(4,128)S(1)} %get-tuple-element.16.after_ref), custom_call_target="tpu_custom_call" | custom-call | flops 614400 | bytes 153600 | tf_op jit(solution)/shard_map/pallas_call | solution.py:570
  6.6 6.4 %all-to-all-start = ((f32[8,48,128]{2,1,0:T(8,128)}), f32[8,48,128]{2,1,0:T(8,128)S(1)}, u32[]{:S(2)}, u32[]{:S(2)}) async-start(f32[8,48,128]{2,1,0:T(8,128)} %shard_map.87), calls=%async_computation | async-start | bytes 393216 | tf_op jit(solution)/shard_map/all_to_all | solution.py:638
  12.9 1.3 %collective-permute-start = (f32[34,4,256]{2,1,0:T(4,128)S(1)}, f32[34,4,256]{2,1,0:T(4,128)S(1)}, u32[]{:S(2)}, u32[]{:S(2)}) collective-permute-start(f32[34,4,256]{2,1,0:T(4,128)S(1)} %get-tuple-element.16.after_ref), channel_id=1, source_target_pairs={{4,0},{8,4},{12,8},{5,1},{9,5},{13,9},{6,2},{10,6},{14,10},{7,3},{... | collective-permute-start | bytes 417800 | tf_op jit(solution)/shard_map/ppermute | solution.py:626
  14.2 4.0 %collective-permute-start.1 = (f32[34,4,256]{2,1,0:T(4,128)S(1)}, f32[34,4,256]{2,1,0:T(4,128)S(1)}, u32[]{:S(2)}, u32[]{:S(2)}) collective-permute-start(f32[34,4,256]{2,1,0:T(4,128)S(1)} %get-tuple-element.17), channel_id=1, source_target_pairs={{0,4},{4,8},{8,12},{1,5},{5,9},{9,13},{2,6},{6,10},{10,14},{3,7},{... | collective-permute-start | bytes 417800 | tf_op jit(solution)/shard_map/ppermute | solution.py:625
  18.2 4.2 %collective-permute-done.refs_5_.next_hbm = f32[34,4,256]{2,1,0:T(4,128)S(1)} collective-permute-done((f32[34,4,256]{2,1,0:T(4,128)S(1)}, f32[34,4,256]{2,1,0:T(4,128)S(1)}, u32[]{:S(2)}, u32[]{:S(2)}) %collective-permute-start) | collective-permute-done | bytes 139296 | tf_op jit(solution)/shard_map/ppermute | solution.py:626
  22.4 0.0 collective-permute-done.1.refs_6_.prev_hbm
  22.5 0.6 copy-done.8
  23.1 0.0 all-to-all-done.refs_0_
  23.1 0.0 copy-start.2
  23.1 1.6 %copy-done.2 = bf16[64,128,128]{2,1,0:T(8,128)(2,1)S(1)} copy-done((bf16[64,128,128]{2,1,0:T(8,128)(2,1)S(1)}, bf16[64,128,128]{2,1,0:T(8,128)(2,1)}, u32[]{:S(2)}) %copy-start.2) | copy-done | bytes 2097176
  24.7 0.9 %copy-done.9 = f32[34,4,256]{2,1,0:T(4,128)S(1)} copy-done((f32[34,4,256]{2,1,0:T(4,128)S(1)}, f32[34,4,256]{2,1,0:T(4,128)}, u32[]{:S(2)}) %copy-start.9) | copy-done | bytes 139288
  25.6 0.8 copy-done.16
  26.4 0.8 copy-done.18
  27.1 3.4 %shard_map.88 = (f32[2,32,256]{2,1,0:T(8,128)S(1)}, f32[16,16,128]{2,1,0:T(8,128)S(1)}, f32[9,40,384]{2,1,0:T(8,128)}, f32[40,384]{1,0:T(8,128)S(1)}, f32[40,384]{1,0:T(8,128)S(1)}, /*index=5*/f32[2,40,128]{2,1,0:T(8,128)S(1)}) custom-call(s32[2,64]{1,0:T(2,128)S(1)} %copy-done.31, f32[8,48,128]{2,1,0:T(8,128)S(1)} %all-to-all-done.refs_0_, ...), custom_call_target="tpu_custom_call" | custom-call | flops 3072000 | bytes 768000 | tf_op jit(solution)/shard_map/pallas_call | solution.py:570
  30.6 0.6 copy-done.11
  31.2 0.6 copy-done.23
  31.8 0.6 copy-done.24
  32.5 0.6 copy-done.26
  33.1 0.8 collective-permute-start.2
  33.9 6.2 %all-to-all-start.1 = ((f32[16,16,128]{2,1,0:T(8,128)}), f32[16,16,128]{2,1,0:T(8,128)}, u32[]{:S(2)}, u32[]{:S(2)}) async-start(f32[16,16,128]{2,1,0:T(8,128)} %copy-done.23), calls=%async_computation.1 | async-start | bytes 262144 | tf_op jit(solution)/shard_map/all_to_all | solution.py:665
  40.0 0.2 collective-permute-start.3
  40.3 0.0 collective-permute-done.2.other_hbm
  40.3 0.9 %copy-done.10 = f32[34,4,256]{2,1,0:T(4,128)S(1)} copy-done((f32[34,4,256]{2,1,0:T(4,128)S(1)}, f32[34,4,256]{2,1,0:T(4,128)}, u32[]{:S(2)}) %copy-start.10) | copy-done | bytes 139288
  41.2 0.8 copy-done.12
  42.0 0.8 copy-done.27
  42.8 8.5 %shard_map.89 = (f32[40,40,384]{2,1,0:T(8,128)S(1)}, f32[40,40,384]{2,1,0:T(8,128)S(1)}, f32[4,40,384]{2,1,0:T(8,128)S(1)}, f32[4,40,384]{2,1,0:T(8,128)S(1)}) custom-call(f32[32,32,256]{2,1,0:T(8,128)S(1)} %copy-done.1, f32[34,4,256]{2,1,0:T(4,128)S(1)} %collective-permute-done.refs_5_.next_hbm, f32[34,4,256]{2,1,0:T(4,128)S(1)} %copy-done.10, ...), custom_call_target="tpu_custom_call" | custom-call | flops 24576000 | bytes 6144000 | tf_op jit(solution)/shard_map/pallas_call | solution.py:570
  51.3 1.4 %copy-done.4 = f32[40,40,384]{2,1,0:T(8,128)} copy-done((f32[40,40,384]{2,1,0:T(8,128)}, f32[40,40,384]{2,1,0:T(8,128)S(1)}, u32[]{:S(2)}) %copy-start.4) | copy-done | bytes 2457624
  52.7 1.5 %copy-done.6 = f32[40,40,384]{2,1,0:T(8,128)} copy-done((f32[40,40,384]{2,1,0:T(8,128)}, f32[40,40,384]{2,1,0:T(8,128)S(1)}, u32[]{:S(2)}) %copy-start.6) | copy-done | bytes 2457624
  54.2 0.7 copy-done.19
  54.9 0.7 copy-done.21
  55.7 0.8 copy-done.13
  56.5 0.9 %copy-done.20 = f32[4,40,384]{2,1,0:T(8,128)S(1)} copy-done((f32[4,40,384]{2,1,0:T(8,128)S(1)}, f32[4,40,384]{2,1,0:T(8,128)}, u32[]{:S(2)}) %copy-start.20) | copy-done | bytes 245784
  57.4 0.9 %copy-done.22 = f32[4,40,384]{2,1,0:T(8,128)S(1)} copy-done((f32[4,40,384]{2,1,0:T(8,128)S(1)}, f32[4,40,384]{2,1,0:T(8,128)}, u32[]{:S(2)}) %copy-start.22) | copy-done | bytes 245784
  58.4 0.8 copy-done.25
  59.2 5.4 %shard_map.90 = (f32[2,40,384]{2,1,0:T(8,128)S(1)}, f32[16,128]{1,0:T(8,128)}) custom-call(s32[2,64]{1,0:T(2,128)S(1)} %copy-done.31, f32[2,32,256]{2,1,0:T(8,128)S(1)} %copy-done.25, f32[2,32,256]{2,1,0:T(8,128)S(1)} %collective-permute-done.3.other_hbm, f32[16,16,128]{2,1,0:T(8,128)} %all-to-all-done.1.edges_ref, bf16[64,128,128]{2,1,0:T(8,128)(2,1)S(1)} %copy-done.3, ...), custom_call_target="tpu_custom_call" | custom-call | flops 6144000 | bytes 1536000 | tf_op jit(solution)/shard_map/pallas_call | solution.py:570
  64.6 6.0 %all-to-all-start.2 = ((f32[16,1,128]{2,1,0:T(1,128)}), f32[16,1,128]{2,1,0:T(1,128)S(1)}, u32[]{:S(2)}, u32[]{:S(2)}) async-start(f32[16,1,128]{2,1,0:T(1,128)} %bitcast.2), calls=%async_computation.2 | async-start | bytes 16384 | tf_op jit(solution)/shard_map/all_to_all | solution.py:699
  70.6 1.7 %copy-done.5 = f32[40,40,384]{2,1,0:T(8,128)S(1)} copy-done((f32[40,40,384]{2,1,0:T(8,128)S(1)}, f32[40,40,384]{2,1,0:T(8,128)}, u32[]{:S(2)}) %copy-start.5) | copy-done | bytes 2457624
  72.3 1.7 %copy-done.7 = f32[40,40,384]{2,1,0:T(8,128)S(1)} copy-done((f32[40,40,384]{2,1,0:T(8,128)S(1)}, f32[40,40,384]{2,1,0:T(8,128)}, u32[]{:S(2)}) %copy-start.7) | copy-done | bytes 2457624
  74.0 0.8 copy-done.14
  74.8 7.9 %shard_map.91 = f32[32,32,256]{2,1,0:T(8,128)} custom-call(f32[32,32,256]{2,1,0:T(8,128)S(1)} %copy-done.1, f32[40,40,384]{2,1,0:T(8,128)S(1)} %copy-done.5, f32[40,40,384]{2,1,0:T(8,128)S(1)} %copy-done.7, f32[40,384]{1,0:T(8,128)S(1)} %get-tuple-element.20.levels_hbm, f32[40,384]{1,0:T(8,128)S(1)} %copy-done.14, ...), custom_call_target="tpu_custom_call" | custom-call | flops 36864000 | bytes 9216000 | tf_op jit(solution)/shard_map/pallas_call | solution.py:570
  82.7 1.3 %shard_map.92 = f32[8,128]{1,0:T(8,128)} custom-call(s32[8,8]{1,0:T(8,128)S(1)} %bitcast.7, f32[16,128]{1,0:T(8,128)S(1)} %bitcast.5), custom_call_target="tpu_custom_call" | custom-call | flops 30720 | bytes 7680 | tf_op jit(solution)/shard_map/pallas_call | solution.py:570
  (37 shorter events, 0.1 us)
Async XLA Ops:
  0.6 1.2 %copy-start = (f32[32,32,256]{2,1,0:T(8,128)S(1)}, f32[32,32,256]{2,1,0:T(8,128)}, u32[]{:S(2)}) copy-start(f32[32,32,256]{2,1,0:T(8,128)} %temp_hbm.5) | copy-start | bytes 3145732
  1.9 0.8 copy-start.15
  2.6 0.8 copy-start.17
  3.4 19.7 %copy-start.1 = (f32[32,32,256]{2,1,0:T(8,128)S(1)}, f32[32,32,256]{2,1,0:T(8,128)}, u32[]{:S(2)}) copy-start(f32[32,32,256]{2,1,0:T(8,128)} %temp_hbm.5) | copy-start | bytes 3145732
  3.4 19.7 %copy-start.31 = (s32[2,64]{1,0:T(2,128)S(1)}, s32[2,64]{1,0:T(2,128)}, u32[]{:S(2)}) copy-start(s32[2,64]{1,0:T(2,128)} %slots_hbm.3) | copy-start | bytes 1540
  3.5 0.8 copy-start.28
  4.3 0.7 copy-start.30
  6.6 16.6 %all-to-all-start = ((f32[8,48,128]{2,1,0:T(8,128)}), f32[8,48,128]{2,1,0:T(8,128)S(1)}, u32[]{:S(2)}, u32[]{:S(2)}) async-start(f32[8,48,128]{2,1,0:T(8,128)} %shard_map.87), calls=%async_computation | async-start | bytes 393216 | tf_op jit(solution)/shard_map/all_to_all | solution.py:638
  12.9 9.5 %collective-permute-start = (f32[34,4,256]{2,1,0:T(4,128)S(1)}, f32[34,4,256]{2,1,0:T(4,128)S(1)}, u32[]{:S(2)}, u32[]{:S(2)}) collective-permute-start(f32[34,4,256]{2,1,0:T(4,128)S(1)} %get-tuple-element.16.after_ref), channel_id=1, source_target_pairs={{4,0},{8,4},{12,8},{5,1},{9,5},{13,9},{6,2},{10,6},{14,10},{7,3},{... | collective-permute-start | bytes 417800 | tf_op jit(solution)/shard_map/ppermute | solution.py:626
  14.2 8.2 %collective-permute-start.1 = (f32[34,4,256]{2,1,0:T(4,128)S(1)}, f32[34,4,256]{2,1,0:T(4,128)S(1)}, u32[]{:S(2)}, u32[]{:S(2)}) collective-permute-start(f32[34,4,256]{2,1,0:T(4,128)S(1)} %get-tuple-element.17), channel_id=1, source_target_pairs={{0,4},{4,8},{8,12},{1,5},{5,9},{9,13},{2,6},{6,10},{10,14},{3,7},{... | collective-permute-start | bytes 417800 | tf_op jit(solution)/shard_map/ppermute | solution.py:625
  22.5 0.7 copy-start.8
  23.1 1.6 %copy-start.2 = (bf16[64,128,128]{2,1,0:T(8,128)(2,1)S(1)}, bf16[64,128,128]{2,1,0:T(8,128)(2,1)}, u32[]{:S(2)}) copy-start(bf16[64,128,128]{2,1,0:T(8,128)(2,1)} %weights_hbm.1) | copy-start | bytes 6291460
  24.7 0.9 %copy-start.9 = (f32[34,4,256]{2,1,0:T(4,128)S(1)}, f32[34,4,256]{2,1,0:T(4,128)}, u32[]{:S(2)}) copy-start(f32[34,4,256]{2,1,0:T(4,128)} %copy-done.8) | copy-start | bytes 417796
  25.6 0.8 copy-start.16
  26.4 0.8 copy-start.18
  27.1 28.5 %copy-start.3 = (bf16[64,128,128]{2,1,0:T(8,128)(2,1)S(1)}, bf16[64,128,128]{2,1,0:T(8,128)(2,1)}, u32[]{:S(2)}) copy-start(bf16[64,128,128]{2,1,0:T(8,128)(2,1)} %weights_hbm.1) | copy-start | bytes 6291460
  30.6 0.6 copy-start.11
  31.2 0.7 copy-start.23
  31.8 0.6 copy-start.24
  32.5 0.6 copy-start.26
  33.1 7.2 %collective-permute-start.2 = (f32[9,40,384]{2,1,0:T(8,128)}, f32[9,40,384]{2,1,0:T(8,128)}, u32[]{:S(2)}, u32[]{:S(2)}) collective-permute-start(f32[9,40,384]{2,1,0:T(8,128)} %get-tuple-element.19), channel_id=1, source_target_pairs={{0,1},{1,0},{2,3},{3,2},{4,5},{5,4},{6,7},{7,6},{8,9},{9,8},{10,11... | collective-permute-start | bytes 1658888 | tf_op jit(solution)/shard_map/ppermute | solution.py:663
  33.9 21.8 %all-to-all-start.1 = ((f32[16,16,128]{2,1,0:T(8,128)}), f32[16,16,128]{2,1,0:T(8,128)}, u32[]{:S(2)}, u32[]{:S(2)}) async-start(f32[16,16,128]{2,1,0:T(8,128)} %copy-done.23), calls=%async_computation.1 | async-start | bytes 262144 | tf_op jit(solution)/shard_map/all_to_all | solution.py:665
  40.0 15.6 %collective-permute-start.3 = (f32[2,32,256]{2,1,0:T(8,128)}, f32[2,32,256]{2,1,0:T(8,128)S(1)}, u32[]{:S(2)}, u32[]{:S(2)}) collective-permute-start(f32[2,32,256]{2,1,0:T(8,128)} %copy-done.24), channel_id=1, source_target_pairs={{0,1},{1,0},{2,3},{3,2},{4,5},{5,4},{6,7},{7,6},{8,9},{9,8},{10,11... | collective-permute-start | bytes 196616 | tf_op jit(solution)/shard_map/ppermute | solution.py:662
  40.3 0.9 %copy-start.10 = (f32[34,4,256]{2,1,0:T(4,128)S(1)}, f32[34,4,256]{2,1,0:T(4,128)}, u32[]{:S(2)}) copy-start(f32[34,4,256]{2,1,0:T(4,128)} %copy-done.8) | copy-start | bytes 417796
  41.2 0.8 copy-start.12
  42.0 0.8 copy-start.27
  51.3 1.4 %copy-start.4 = (f32[40,40,384]{2,1,0:T(8,128)}, f32[40,40,384]{2,1,0:T(8,128)S(1)}, u32[]{:S(2)}) copy-start(f32[40,40,384]{2,1,0:T(8,128)S(1)} %get-tuple-element.22.moved_hbm) | copy-start | bytes 7372804
  52.7 1.5 %copy-start.6 = (f32[40,40,384]{2,1,0:T(8,128)}, f32[40,40,384]{2,1,0:T(8,128)S(1)}, u32[]{:S(2)}) copy-start(f32[40,40,384]{2,1,0:T(8,128)S(1)} %get-tuple-element.23.keep_hbm) | copy-start | bytes 7372804
  54.2 0.7 copy-start.19
  54.9 0.7 copy-start.21
  55.7 0.8 copy-start.13
  56.5 0.9 %copy-start.20 = (f32[4,40,384]{2,1,0:T(8,128)S(1)}, f32[4,40,384]{2,1,0:T(8,128)}, u32[]{:S(2)}) copy-start(f32[4,40,384]{2,1,0:T(8,128)} %copy-done.19) | copy-start | bytes 737284
  57.4 0.9 %copy-start.22 = (f32[4,40,384]{2,1,0:T(8,128)S(1)}, f32[4,40,384]{2,1,0:T(8,128)}, u32[]{:S(2)}) copy-start(f32[4,40,384]{2,1,0:T(8,128)} %copy-done.21) | copy-start | bytes 737284
  58.4 0.8 copy-start.25
  64.6 18.1 %all-to-all-start.2 = ((f32[16,1,128]{2,1,0:T(1,128)}), f32[16,1,128]{2,1,0:T(1,128)S(1)}, u32[]{:S(2)}, u32[]{:S(2)}) async-start(f32[16,1,128]{2,1,0:T(1,128)} %bitcast.2), calls=%async_computation.2 | async-start | bytes 16384 | tf_op jit(solution)/shard_map/all_to_all | solution.py:699
  70.6 1.7 %copy-start.5 = (f32[40,40,384]{2,1,0:T(8,128)S(1)}, f32[40,40,384]{2,1,0:T(8,128)}, u32[]{:S(2)}) copy-start(f32[40,40,384]{2,1,0:T(8,128)} %copy-done.4) | copy-start | bytes 7372804
  72.3 1.7 %copy-start.7 = (f32[40,40,384]{2,1,0:T(8,128)S(1)}, f32[40,40,384]{2,1,0:T(8,128)}, u32[]{:S(2)}) copy-start(f32[40,40,384]{2,1,0:T(8,128)} %copy-done.6) | copy-start | bytes 7372804
  74.0 0.8 copy-start.14
  74.8 7.9 %copy-start.29 = (s32[8,8,1]{1,2,0:T(1,128)S(1)}, s32[8,8,1]{1,2,0:T(1,128)}, u32[]{:S(2)}) copy-start(s32[8,8,1]{1,2,0:T(1,128)} %param.11) | copy-start | bytes 772

commit v3 on v2

--- a/solution.py
+++ b/solution.py
@@ -19,7 +19,7 @@
 CHUNKS = 4
 BLOCKS_AXES = ("gx", "gy")
 ALL_AXES = ("gx", "gy", "gz")
-VMEM_LIMIT = 24 * 1024 * 1024
+VMEM_LIMIT = 60 * 1024 * 1024
 
 
 def position_of(few, dx, dy):

time: 85.6 us -> 63 us (0.74); the launches traced: 84 us -> 62.4 us
  local copies, waits for them, and re-layouts: 26 us -> 3.41 us
    unnamed x64 -> x14, local copies, waits for them, and re-layouts: 26 us -> 3.41 us
  transfers between devices with their start and end apart: 7 -> 7, of which waited for: 1 -> 1; matrix products, arithmetic and copies ran while one was open for 0% -> 0% of each run, Pallas kernels for 20% -> 23%
where the time goes in v3:
time: 63 us; the launch traced here: 62.4 us
  Pallas kernels  29 us (46%)
  starting transfers between devices  25 us (40%)
  waiting for transfers between devices  4.25 us (7%)
  local copies, waits for them, and re-layouts  3.41 us (5%)
  between operations  0.75 us (1%)
    pallas_call x7, Pallas kernels, call(): pl.pallas_call(body, out_shape=[jax.ShapeDtypeStruct(out, jnp.float32) fo...  29 us
    all_to_all x1, starting transfers between devices, per_device(): lax.all_to_all(sent[0], BLOCKS_AXES, split_axis=0, concat_axis=0, tiled=T...  6.37 us
    all_to_all x1, starting transfers between devices, per_device(): lax.all_to_all(edges, ALL_AXES, split_axis=0, concat_axis=0, tiled=True)  6.31 us
    all_to_all x1, starting transfers between devices, per_device(): lax.all_to_all(back, ALL_AXES, split_axis=0, concat_axis=0, tiled=True)  6.03 us
    ppermute x1, waiting for transfers between devices, per_device(): after_rows = lax.ppermute(low, 'gx', backward)  4.23 us
    ppermute x1, starting transfers between devices, per_device(): before_rows = lax.ppermute(high, 'gx', forward)  4 us
    unnamed x14, local copies, waits for them, and re-layouts  3.41 us
    ppermute x1, starting transfers between devices, per_device(): after_rows = lax.ppermute(low, 'gx', backward)  1.28 us
  transfers between devices with their start and end apart: 7, of which 1 were waited for; matrix products, arithmetic and copies ran while one was open for 0% of the time, Pallas kernels for 23%

profile of v3, /device:TPU:1, one launch (start us, length us, event | category | flops | bytes accessed | tf_op | source)
XLA Modules:
  0.0 62.4 jit_solution(8136099861339261013)
XLA Ops:
  0.6 1.8 %shard_map.86 = (f32[34,4,256]{2,1,0:T(4,128)}, f32[34,4,256]{2,1,0:T(4,128)}) custom-call(f32[32,32,256]{2,1,0:T(8,128)} %temp_hbm.5, s32[32,256]{1,0:T(8,128)} %refs_3_.1, f32[32,256]{1,0:T(8,128)} %refs_4_.1), custom_call_target="tpu_custom_call" | custom-call | flops 307200 | bytes 76800 | tf_op jit(solution)/shard_map/pallas_call | solution.py:570
  2.5 2.0 %shard_map.87 = f32[8,48,128]{2,1,0:T(8,128)} custom-call(s32[8,8]{1,0:T(8,128)} %bitcast.6, bf16[8,2,128]{2,1,0:T(2,128)(2,1)} %flux_hbm.1, f32[32,32,256]{2,1,0:T(8,128)} %temp_hbm.5, s32[32,256]{1,0:T(8,128)} %refs_3_.1, f32[32,256]{1,0:T(8,128)} %refs_4_.1, f32[34,4,256]{2,1,0:T(4,128)} %get-tuple-element.16.after_ref), custom_call_target="tpu_custom_call" | custom-call | flops 614400 | bytes 153600 | tf_op jit(solution)/shard_map/pallas_call | solution.py:570
  4.5 6.4 %all-to-all-start = ((f32[8,48,128]{2,1,0:T(8,128)}), f32[8,48,128]{2,1,0:T(8,128)S(1)}, u32[]{:S(2)}, u32[]{:S(2)}) async-start(f32[8,48,128]{2,1,0:T(8,128)} %shard_map.87), calls=%async_computation | async-start | bytes 393216 | tf_op jit(solution)/shard_map/all_to_all | solution.py:638
  10.9 1.3 %collective-permute-start = (f32[34,4,256]{2,1,0:T(4,128)}, f32[34,4,256]{2,1,0:T(4,128)S(1)}, u32[]{:S(2)}, u32[]{:S(2)}) collective-permute-start(f32[34,4,256]{2,1,0:T(4,128)} %get-tuple-element.16.after_ref), channel_id=1, source_target_pairs={{4,0},{8,4},{12,8},{5,1},{9,5},{13,9},{6,2},{10,6},{14,10},{7,3},{... | collective-permute-start | bytes 417800 | tf_op jit(solution)/shard_map/ppermute | solution.py:626
  12.2 4.0 %collective-permute-start.1 = (f32[34,4,256]{2,1,0:T(4,128)}, f32[34,4,256]{2,1,0:T(4,128)S(1)}, u32[]{:S(2)}, u32[]{:S(2)}) collective-permute-start(f32[34,4,256]{2,1,0:T(4,128)} %get-tuple-element.17), channel_id=1, source_target_pairs={{0,4},{4,8},{8,12},{1,5},{5,9},{9,13},{2,6},{6,10},{10,14},{3,7},{... | collective-permute-start | bytes 417800 | tf_op jit(solution)/shard_map/ppermute | solution.py:625
  16.2 4.2 %collective-permute-done.refs_5_.next_hbm = f32[34,4,256]{2,1,0:T(4,128)S(1)} collective-permute-done((f32[34,4,256]{2,1,0:T(4,128)}, f32[34,4,256]{2,1,0:T(4,128)S(1)}, u32[]{:S(2)}, u32[]{:S(2)}) %collective-permute-start) | collective-permute-done | bytes 139296 | tf_op jit(solution)/shard_map/ppermute | solution.py:626
  20.4 0.0 copy-start.1
  20.4 0.0 collective-permute-done.1.refs_6_.prev_hbm
  20.4 0.0 copy-start.2
  20.4 0.0 all-to-all-done.refs_0_
  20.4 0.7 %copy-done.1 = f32[34,4,256]{2,1,0:T(4,128)} copy-done((f32[34,4,256]{2,1,0:T(4,128)}, f32[34,4,256]{2,1,0:T(4,128)S(1)}, u32[]{:S(2)}) %copy-start.1) | copy-done | bytes 139288
  21.1 0.0 copy-done.2
  21.1 0.0 copy-start
  21.1 0.7 %copy-done = f32[8,48,128]{2,1,0:T(8,128)} copy-done((f32[8,48,128]{2,1,0:T(8,128)}, f32[8,48,128]{2,1,0:T(8,128)S(1)}, u32[]{:S(2)}) %copy-start) | copy-done | bytes 196632
  21.8 4.4 %shard_map.88 = (f32[2,32,256]{2,1,0:T(8,128)}, f32[16,16,128]{2,1,0:T(8,128)}, f32[9,40,384]{2,1,0:T(8,128)}, f32[40,384]{1,0:T(8,128)}, f32[40,384]{1,0:T(8,128)}, /*index=5*/f32[2,40,128]{2,1,0:T(8,128)}) custom-call(s32[2,64]{1,0:T(2,128)} %slots_hbm.3, f32[8,48,128]{2,1,0:T(8,128)} %copy-done, bf16[64,128,128]{2,1,0:T(8,128)(2,1)} %weights_hbm.1, ...), custom_call_target="tpu_custom_call" | custom-call | flops 3072000 | bytes 768000 | tf_op jit(solution)/shard_map/pallas_call | solution.py:570
  26.2 0.9 %collective-permute-start.2 = (f32[9,40,384]{2,1,0:T(8,128)}, f32[9,40,384]{2,1,0:T(8,128)S(1)}, u32[]{:S(2)}, u32[]{:S(2)}) collective-permute-start(f32[9,40,384]{2,1,0:T(8,128)} %get-tuple-element.19), channel_id=1, source_target_pairs={{0,1},{1,0},{2,3},{3,2},{4,5},{5,4},{6,7},{7,6},{8,9},{9,8},{10,11... | collective-permute-start | bytes 1658888 | tf_op jit(solution)/shard_map/ppermute | solution.py:663
  27.1 6.3 %all-to-all-start.1 = ((f32[16,16,128]{2,1,0:T(8,128)}), f32[16,16,128]{2,1,0:T(8,128)S(1)}, u32[]{:S(2)}, u32[]{:S(2)}) async-start(f32[16,16,128]{2,1,0:T(8,128)} %get-tuple-element.25), calls=%async_computation.1 | async-start | bytes 262144 | tf_op jit(solution)/shard_map/all_to_all | solution.py:665
  33.4 0.2 collective-permute-start.3
  33.6 0.0 collective-permute-done.2.other_hbm
  33.6 0.0 copy-start.3
  33.6 0.8 %copy-done.3 = f32[9,40,384]{2,1,0:T(8,128)} copy-done((f32[9,40,384]{2,1,0:T(8,128)}, f32[9,40,384]{2,1,0:T(8,128)S(1)}, u32[]{:S(2)}) %copy-start.3) | copy-done | bytes 552984
  34.4 6.3 %shard_map.89 = (f32[40,40,384]{2,1,0:T(8,128)}, f32[40,40,384]{2,1,0:T(8,128)}, f32[4,40,384]{2,1,0:T(8,128)}, f32[4,40,384]{2,1,0:T(8,128)}) custom-call(f32[32,32,256]{2,1,0:T(8,128)} %temp_hbm.5, f32[34,4,256]{2,1,0:T(4,128)} %copy-done.1, f32[34,4,256]{2,1,0:T(4,128)} %copy-done.2, f32[2,40,128]{2,1,0:T(8,128)} %get-tuple-element.18.packed_hbm, ...), custom_call_target="tpu_custom_call" | custom-call | flops 24576000 | bytes 6144000 | tf_op jit(solution)/shard_map/pallas_call | solution.py:570
  40.7 0.0 collective-permute-done.3.other_hbm
  40.7 0.0 copy-start.5
  40.7 0.0 all-to-all-done.1.edges_ref
  40.7 0.0 copy-start.4
  40.8 0.6 copy-done.5
  41.4 0.0 copy-done.4
  41.4 5.0 %shard_map.90 = (f32[2,40,384]{2,1,0:T(8,128)}, f32[16,128]{1,0:T(8,128)}) custom-call(s32[2,64]{1,0:T(2,128)} %slots_hbm.3, f32[2,32,256]{2,1,0:T(8,128)} %get-tuple-element.24.partial_hbm, f32[2,32,256]{2,1,0:T(8,128)} %copy-done.5, f32[16,16,128]{2,1,0:T(8,128)} %copy-done.4, bf16[64,128,128]{2,1,0:T(8,128)(2,1)} %weights_hbm.1, ...), custom_call_target="tpu_custom_call" | custom-call | flops 6144000 | bytes 1536000 | tf_op jit(solution)/shard_map/pallas_call | solution.py:570
  46.4 6.0 %all-to-all-start.2 = ((f32[16,1,128]{2,1,0:T(1,128)}), f32[16,1,128]{2,1,0:T(1,128)S(1)}, u32[]{:S(2)}, u32[]{:S(2)}) async-start(f32[16,1,128]{2,1,0:T(1,128)} %bitcast.8), calls=%async_computation.2 | async-start | bytes 16384 | tf_op jit(solution)/shard_map/all_to_all | solution.py:699
  52.4 8.0 %shard_map.91 = f32[32,32,256]{2,1,0:T(8,128)} custom-call(f32[32,32,256]{2,1,0:T(8,128)} %temp_hbm.5, f32[40,40,384]{2,1,0:T(8,128)} %get-tuple-element.22.moved_hbm, f32[40,40,384]{2,1,0:T(8,128)} %get-tuple-element.23.keep_hbm, f32[40,384]{1,0:T(8,128)} %get-tuple-element.20.levels_hbm, f32[40,384]{1,0:T(8,128)} %get-tuple-element.21.mix_hbm, ...), custom_call_target="tpu_custom_call" | custom-call | flops 36864000 | bytes 9216000 | tf_op jit(solution)/shard_map/pallas_call | solution.py:570
  60.4 0.0 all-to-all-done.2
  60.4 0.0 copy-start.6
  60.4 0.6 copy-done.6
  61.0 1.4 %shard_map.92 = f32[8,128]{1,0:T(8,128)} custom-call(s32[8,8]{1,0:T(8,128)} %bitcast.7, f32[16,128]{1,0:T(8,128)} %bitcast.5), custom_call_target="tpu_custom_call" | custom-call | flops 30720 | bytes 7680 | tf_op jit(solution)/shard_map/pallas_call | solution.py:570
Async XLA Ops:
  4.5 15.9 %all-to-all-start = ((f32[8,48,128]{2,1,0:T(8,128)}), f32[8,48,128]{2,1,0:T(8,128)S(1)}, u32[]{:S(2)}, u32[]{:S(2)}) async-start(f32[8,48,128]{2,1,0:T(8,128)} %shard_map.87), calls=%async_computation | async-start | bytes 393216 | tf_op jit(solution)/shard_map/all_to_all | solution.py:638
  10.9 9.5 %collective-permute-start = (f32[34,4,256]{2,1,0:T(4,128)}, f32[34,4,256]{2,1,0:T(4,128)S(1)}, u32[]{:S(2)}, u32[]{:S(2)}) collective-permute-start(f32[34,4,256]{2,1,0:T(4,128)} %get-tuple-element.16.after_ref), channel_id=1, source_target_pairs={{4,0},{8,4},{12,8},{5,1},{9,5},{13,9},{6,2},{10,6},{14,10},{7,3},{... | collective-permute-start | bytes 417800 | tf_op jit(solution)/shard_map/ppermute | solution.py:626
  12.2 8.2 %collective-permute-start.1 = (f32[34,4,256]{2,1,0:T(4,128)}, f32[34,4,256]{2,1,0:T(4,128)S(1)}, u32[]{:S(2)}, u32[]{:S(2)}) collective-permute-start(f32[34,4,256]{2,1,0:T(4,128)} %get-tuple-element.17), channel_id=1, source_target_pairs={{0,4},{4,8},{8,12},{1,5},{5,9},{9,13},{2,6},{6,10},{10,14},{3,7},{... | collective-permute-start | bytes 417800 | tf_op jit(solution)/shard_map/ppermute | solution.py:625
  20.4 0.7 %copy-start.1 = (f32[34,4,256]{2,1,0:T(4,128)}, f32[34,4,256]{2,1,0:T(4,128)S(1)}, u32[]{:S(2)}) copy-start(f32[34,4,256]{2,1,0:T(4,128)S(1)} %collective-permute-done.refs_5_.next_hbm) | copy-start | bytes 417796
  20.4 0.7 %copy-start.2 = (f32[34,4,256]{2,1,0:T(4,128)}, f32[34,4,256]{2,1,0:T(4,128)S(1)}, u32[]{:S(2)}) copy-start(f32[34,4,256]{2,1,0:T(4,128)S(1)} %collective-permute-done.1.refs_6_.prev_hbm) | copy-start | bytes 417796
  21.1 0.7 %copy-start = (f32[8,48,128]{2,1,0:T(8,128)}, f32[8,48,128]{2,1,0:T(8,128)S(1)}, u32[]{:S(2)}) copy-start(f32[8,48,128]{2,1,0:T(8,128)S(1)} %all-to-all-done.refs_0_) | copy-start | bytes 589828
  26.2 7.4 %collective-permute-start.2 = (f32[9,40,384]{2,1,0:T(8,128)}, f32[9,40,384]{2,1,0:T(8,128)S(1)}, u32[]{:S(2)}, u32[]{:S(2)}) collective-permute-start(f32[9,40,384]{2,1,0:T(8,128)} %get-tuple-element.19), channel_id=1, source_target_pairs={{0,1},{1,0},{2,3},{3,2},{4,5},{5,4},{6,7},{7,6},{8,9},{9,8},{10,11... | collective-permute-start | bytes 1658888 | tf_op jit(solution)/shard_map/ppermute | solution.py:663
  27.1 13.6 %all-to-all-start.1 = ((f32[16,16,128]{2,1,0:T(8,128)}), f32[16,16,128]{2,1,0:T(8,128)S(1)}, u32[]{:S(2)}, u32[]{:S(2)}) async-start(f32[16,16,128]{2,1,0:T(8,128)} %get-tuple-element.25), calls=%async_computation.1 | async-start | bytes 262144 | tf_op jit(solution)/shard_map/all_to_all | solution.py:665
  33.4 7.3 %collective-permute-start.3 = (f32[2,32,256]{2,1,0:T(8,128)}, f32[2,32,256]{2,1,0:T(8,128)S(1)}, u32[]{:S(2)}, u32[]{:S(2)}) collective-permute-start(f32[2,32,256]{2,1,0:T(8,128)} %get-tuple-element.24.partial_hbm), channel_id=1, source_target_pairs={{0,1},{1,0},{2,3},{3,2},{4,5},{5,4},{6,7},{7,6},{8,9},{9,8},{10,11... | collective-permute-start | bytes 196616 | tf_op jit(solution)/shard_map/ppermute | solution.py:662
  33.6 0.8 %copy-start.3 = (f32[9,40,384]{2,1,0:T(8,128)}, f32[9,40,384]{2,1,0:T(8,128)S(1)}, u32[]{:S(2)}) copy-start(f32[9,40,384]{2,1,0:T(8,128)S(1)} %collective-permute-done.2.other_hbm) | copy-start | bytes 1658884
  40.7 0.6 %copy-start.5 = (f32[2,32,256]{2,1,0:T(8,128)}, f32[2,32,256]{2,1,0:T(8,128)S(1)}, u32[]{:S(2)}) copy-start(f32[2,32,256]{2,1,0:T(8,128)S(1)} %collective-permute-done.3.other_hbm) | copy-start | bytes 196612
  40.7 0.7 %copy-start.4 = (f32[16,16,128]{2,1,0:T(8,128)}, f32[16,16,128]{2,1,0:T(8,128)S(1)}, u32[]{:S(2)}) copy-start(f32[16,16,128]{2,1,0:T(8,128)S(1)} %all-to-all-done.1.edges_ref) | copy-start | bytes 393220
  46.4 14.0 %all-to-all-start.2 = ((f32[16,1,128]{2,1,0:T(1,128)}), f32[16,1,128]{2,1,0:T(1,128)S(1)}, u32[]{:S(2)}, u32[]{:S(2)}) async-start(f32[16,1,128]{2,1,0:T(1,128)} %bitcast.8), calls=%async_computation.2 | async-start | bytes 16384 | tf_op jit(solution)/shard_map/all_to_all | solution.py:699
  60.4 0.6 copy-start.6

commit v4 on v3

--- a/solution.py
+++ b/solution.py
@@ -70,6 +70,15 @@
     return jnp.where(levels > level, new, 0.0)
 
 
+def last_slab(center, over, under, keep, mixing, forcing):
+    rows, columns = over.shape
+    tall, lanes = center.shape
+    own = slice(0, rows), slice(0, columns)
+    lateral = pltpu.roll(center, 1, 0)[own] + pltpu.roll(center, tall - 1, 0)[own]
+    lateral = lateral + (pltpu.roll(center[0:rows], 1, 1)[own] + pltpu.roll(center[0:rows], lanes - 1, 1)[own])
+    return center[own] * keep + 0.1 * (lateral + forcing) + mixing * (over + under)
+
+
 def depth_share(level, total_levels):
     return jnp.exp(jnp.full((1, 1), -4.0 / total_levels, jnp.float32) * level)
 
@@ -101,7 +110,7 @@
         body(start + index)
 
 
-def rows_kernel(temp_ref, bathy_ref, mixing_ref, low_ref, high_ref, temp_rows, bathy_rows, mixing_rows, semaphores):
+def rows_kernel(temp_ref, bathy_ref, mixing_ref, one_ref, two_ref, temp_rows, bathy_rows, mixing_rows, semaphores):
     layers, rows, columns = temp_ref.shape
     copies = []
     for side in range(2):
@@ -109,13 +118,18 @@
         copies += [(temp_ref.at[:, part], temp_rows.at[side]), (bathy_ref.at[part], bathy_rows.at[side])]
         copies += [(mixing_ref.at[part], mixing_rows.at[side])]
     finish(begin(copies, semaphores))
-    for side, (out_ref, part) in enumerate(((low_ref, slice(0, HALO)), (high_ref, slice(TILE - HALO, TILE)))):
-        out_ref[0:layers] = temp_rows[side, :, part]
-        out_ref[layers] = bathy_rows[side, part].astype(jnp.float32)
-        out_ref[layers + 1] = mixing_rows[side, part]
-
-
-def send_kernel(sends_hbm, flux_hbm, temp_hbm, bathy_hbm, mixing_hbm, after_ref, *refs, few, sides):
+    even = lax.rem(lax.axis_index("gx"), 2) == 0
+    fields = [
+        (slice(0, layers), lambda side: temp_rows[side]), (layers, lambda side: bathy_rows[side].astype(jnp.float32)),
+        (layers + 1, lambda side: mixing_rows[side]),
+    ]
+    for place, read in fields:
+        low, high = read(0)[..., 0:HALO, :], read(1)[..., TILE - HALO :, :]
+        one_ref[place] = jnp.where(even, high, low)
+        two_ref[place] = jnp.where(even, low, high)
+
+
+def send_kernel(sends_hbm, flux_hbm, temp_hbm, bathy_hbm, mixing_hbm, *refs, few, sides):
     if few:
         message_ref, sends_ref, flux_ref, temp_ref, bathy_ref, mixing_ref, semaphores, flux_scratch, strips_ref = refs
         fluxes_ref = message_ref
@@ -174,66 +188,25 @@
         lax.fori_loop(0, fluxes_ref.shape[0], one, 0)
 
 
-def regrid_kernel(slots_hbm, *refs, few):
-    if few:
-        sides_ref, *refs = refs
-        flux_ref = sides_ref
-    else:
-        flux_ref, sides_ref, *refs = refs
-    (
-        weights_hbm, temp_hbm, bathy_hbm, mixing_hbm, next_ref, prev_ref,
-        partial_ref, edges_ref, shared_ref, levels_hbm, mix_hbm, packed_hbm,
-        slots_ref, weights_ref, temp_ref, bathy_ref, mixing_ref, levels_ref, mix_ref, packed_ref, semaphores,
-        sums_ref, *strip_scratch,
-    ) = refs
-    layers, rows, columns = temp_hbm.shape
+def regrid_kernel(
+    slots_hbm, flux_hbm, weights_hbm, partial_hbm, edges_ref,
+    slots_ref, flux_ref, weights_ref, partial_ref, semaphores, sums_ref, *strip_scratch, few,
+):
+    fields, rows, columns = partial_ref.shape
     slot_count, tile_atm, patch = weights_ref.shape
     halves = columns // LANES
-    lasts = pl.ds(layers - HALO, HALO)
-    needed = begin([
-        (temp_hbm.at[pl.ds(0, TOP)], temp_ref.at[pl.ds(0, TOP)]), (temp_hbm.at[lasts], temp_ref.at[pl.ds(TOP, HALO)]),
-        (bathy_hbm, bathy_ref), (mixing_hbm, mixing_ref), (slots_hbm, slots_ref),
-    ], semaphores)
+    needed = begin([(slots_hbm, slots_ref), (flux_hbm.at[:, pl.ds(0, TILE)], flux_ref)], semaphores)
     chunk = slot_count // CHUNKS
     arriving = begin([
         (weights_hbm.at[pl.ds(part * chunk, chunk)], weights_ref.at[pl.ds(part * chunk, chunk)])
         for part in range(CHUNKS)
     ], semaphores, len(needed))
     sums_ref[...] = jnp.zeros_like(sums_ref)
-
-    gx, gx_count = lax.axis_index("gx"), lax.axis_size("gx")
-    gy, gy_count = lax.axis_index("gy"), lax.axis_size("gy")
-    plain = []
-    for side, dy in ((0, -1), (1, 1)):
-        own, after, before = (position_of(few, dx, dy) for dx in (0, 1, -1))
-        packed_ref[side, 0:rows] = sides_ref[own, 2 * TILE : 2 * TILE + rows]
-        packed_ref[side, rows : rows + HALO] = sides_ref[after, 2 * TILE : 2 * TILE + HALO]
-        packed_ref[side, rows + HALO :] = sides_ref[before, 2 * TILE + rows - HALO : 2 * TILE + rows]
-        tile = sides_ref[own, TILE : 2 * TILE]
-        parts = [tile] + [pltpu.roll(tile, LANES - 2 * HALO * part, 1) for part in range(1, rows // TILE)]
-        last = pltpu.roll(sides_ref[before, TILE : 2 * TILE], LANES - 2 * HALO * (rows // TILE - 1), 1)
-        row = lax.broadcasted_iota(jnp.int32, (TILE, LANES), 0)
-        parts.append(jnp.where(row < HALO, sides_ref[after, TILE : 2 * TILE], last))
-        plain.append(jnp.concatenate(parts, axis=0))
     finish(needed)
-    size = (rows + 2 * HALO, LANES)
-    lane, row = (lax.broadcasted_iota(jnp.int32, size, dim) for dim in (1, 0))
-    there = (lane < HALO) & (gy < gy_count - 1) | (lane >= HALO) & (gy > 0)
-    there = there & ((row < rows) | (row < rows + HALO) & (gx < gx_count - 1) | (row >= rows + HALO) & (gx > 0))
-    tile = jnp.where(there, side_tile(plain[0], plain[1], 0), 0.0)
-    put_slab(levels_ref, bathy_ref[...].astype(jnp.float32), next_ref[layers], prev_ref[layers], tile)
-    tile = side_tile(plain[0], plain[1], 1)
-    put_slab(mix_ref, mixing_ref[...], next_ref[layers + 1], prev_ref[layers + 1], tile)
-    for place, level in enumerate(list(range(TOP)) + list(range(layers - HALO, layers))):
-        tile = side_tile(packed_ref[0], packed_ref[1], level)
-        put_slab(shared_ref.at[place], temp_ref[place], next_ref[level], prev_ref[level], tile)
-    leaving = begin(
-        [(levels_ref, levels_hbm), (mix_ref, mix_hbm), (packed_ref, packed_hbm)], semaphores, len(needed) + CHUNKS
-    )
     for slot in range(slot_count):
         if slot % chunk == 0:
             arriving[slot // chunk].wait()
-        fluxes = flux_ref[slots_ref[0, slot], 0:TILE, :].astype(jnp.bfloat16)
+        fluxes = flux_ref[slots_ref[0, slot]].astype(jnp.bfloat16)
         got = jnp.dot(fluxes, weights_ref[slot], preferred_element_type=jnp.float32)
         place = pl.multiple_of(slots_ref[1, slot] * TILE, TILE)
         sums_ref[pl.ds(place, TILE)] += got
@@ -258,6 +231,7 @@
                     columns_low = jnp.where(inside, pltpu.roll(block, place % LANES, 1), columns_low)
                 if half == halves - 1:
                     columns_high = jnp.where(inside, pltpu.roll(block, (place + HALO) % LANES, 1), columns_high)
+    leaving = begin([(partial_ref, partial_hbm)], semaphores, len(needed) + CHUNKS)
     strips_ref[2, 0:TILE] = columns_low
     strips_ref[3, 0:TILE] = columns_high
     if few:
@@ -270,17 +244,63 @@
     finish(leaving)
 
 
+def halo_kernel(
+    sides_hbm, temp_hbm, bathy_hbm, mixing_hbm, one_hbm, two_hbm, after_ref,
+    shared_ref, levels_hbm, mix_hbm, packed_hbm,
+    sides_ref, temp_ref, bathy_ref, mixing_ref, pair_ref, levels_ref, mix_ref, packed_ref, semaphores, *, few,
+):
+    layers, rows, columns = temp_hbm.shape
+    lasts = pl.ds(layers - HALO, HALO)
+    needed = begin([
+        (sides_hbm, sides_ref), (temp_hbm.at[pl.ds(0, TOP)], temp_ref.at[pl.ds(0, TOP)]),
+        (temp_hbm.at[lasts], temp_ref.at[pl.ds(TOP, HALO)]), (bathy_hbm, bathy_ref), (mixing_hbm, mixing_ref),
+        (one_hbm, pair_ref.at[0]), (two_hbm, pair_ref.at[1]),
+    ], semaphores)
+    odd = lax.rem(lax.axis_index("gx"), 2)
+    next_ref, prev_ref = pair_ref.at[odd], pair_ref.at[1 - odd]
+    finish(needed)
+    gx, gx_count = lax.axis_index("gx"), lax.axis_size("gx")
+    gy, gy_count = lax.axis_index("gy"), lax.axis_size("gy")
+    plain = []
+    for side, dy in ((0, -1), (1, 1)):
+        own, after, before = (position_of(few, dx, dy) for dx in (0, 1, -1))
+        packed_ref[side, 0:rows] = sides_ref[own, 2 * TILE : 2 * TILE + rows]
+        packed_ref[side, rows : rows + HALO] = sides_ref[after, 2 * TILE : 2 * TILE + HALO]
+        packed_ref[side, rows + HALO :] = sides_ref[before, 2 * TILE + rows - HALO : 2 * TILE + rows]
+        tile = sides_ref[own, TILE : 2 * TILE]
+        parts = [tile] + [pltpu.roll(tile, LANES - 2 * HALO * part, 1) for part in range(1, rows // TILE)]
+        last = pltpu.roll(sides_ref[before, TILE : 2 * TILE], LANES - 2 * HALO * (rows // TILE - 1), 1)
+        row = lax.broadcasted_iota(jnp.int32, (TILE, LANES), 0)
+        parts.append(jnp.where(row < HALO, sides_ref[after, TILE : 2 * TILE], last))
+        plain.append(jnp.concatenate(parts, axis=0))
+    size = (rows + 2 * HALO, LANES)
+    lane, row = (lax.broadcasted_iota(jnp.int32, size, dim) for dim in (1, 0))
+    there = (lane < HALO) & (gy < gy_count - 1) | (lane >= HALO) & (gy > 0)
+    there = there & ((row < rows) | (row < rows + HALO) & (gx < gx_count - 1) | (row >= rows + HALO) & (gx > 0))
+    tile = jnp.where(there, side_tile(plain[0], plain[1], 0), 0.0)
+    put_slab(levels_ref, bathy_ref[...].astype(jnp.float32), next_ref[layers], prev_ref[layers], tile)
+    tile = side_tile(plain[0], plain[1], 1)
+    put_slab(mix_ref, mixing_ref[...], next_ref[layers + 1], prev_ref[layers + 1], tile)
+    leaving = begin(
+        [(levels_ref, levels_hbm), (mix_ref, mix_hbm), (packed_ref, packed_hbm)], semaphores, len(needed)
+    )
+    for place, level in enumerate(list(range(TOP)) + list(range(layers - HALO, layers))):
+        tile = side_tile(packed_ref[0], packed_ref[1], level)
+        put_slab(shared_ref.at[place], temp_ref[place], next_ref[level], prev_ref[level], tile)
+    finish(leaving)
+
+
 def first_kernel(
-    temp_hbm, next_hbm, prev_hbm, packed_hbm, other_hbm, levels_hbm, mix_hbm,
+    temp_hbm, one_hbm, two_hbm, packed_hbm, other_hbm, levels_hbm, mix_hbm,
     moved_hbm, keep_hbm, top_hbm, top_keep_hbm,
-    temp_ref, next_ref, prev_ref, packed_ref, other_ref, levels_ref, mix_ref,
+    temp_ref, pair_ref, packed_ref, other_ref, levels_ref, mix_ref,
     moved_ref, keep_ref, top_ref, top_keep_ref, first_ref, skin_ref, semaphores,
 ):
     layers = temp_hbm.shape[0]
     gz = lax.axis_index("gz")
     first_level = gz * layers - HALO
     needed = begin([
-        (next_hbm, next_ref), (prev_hbm, prev_ref), (packed_hbm, packed_ref), (levels_hbm, levels_ref),
+        (one_hbm, pair_ref.at[0]), (two_hbm, pair_ref.at[1]), (packed_hbm, packed_ref), (levels_hbm, levels_ref),
         (mix_hbm, mix_ref), (other_hbm, other_ref),
     ], semaphores)
     chunk = layers // CHUNKS
@@ -288,6 +308,8 @@
     used = len(needed)
     arriving = begin([(temp_hbm.at[part], temp_ref.at[part]) for part in parts], semaphores, used)
     used += CHUNKS
+    odd = lax.rem(lax.axis_index("gx"), 2)
+    next_ref, prev_ref = pair_ref.at[odd], pair_ref.at[1 - odd]
     finish(needed)
 
     def level_of(place):
@@ -352,9 +374,9 @@
 
 
 def skin_kernel(
-    slots_hbm, partial_hbm, other_hbm, edges_ref, weights_hbm, levels_hbm, mix_hbm, top_hbm, top_keep_hbm,
+    sends_hbm, slots_hbm, partial_hbm, other_hbm, edges_hbm, weights_hbm, levels_hbm, mix_hbm, top_hbm, top_keep_hbm,
     surface_hbm, back_ref,
-    slots_ref, partial_ref, other_ref, weights_ref, levels_ref, mix_ref, top_ref, top_keep_ref, surface_ref, semaphores,
+    sends_ref, slots_ref, partial_ref, other_ref, edges_ref, weights_ref, levels_ref, mix_ref, top_ref, top_keep_ref, surface_ref, semaphores,
     first_ref, second_ref, sst_ref, rows_ref, *sums_scratch, few, total_levels,
 ):
     fields, rows, columns = partial_ref.shape
@@ -363,6 +385,7 @@
     needed = begin([
         (partial_hbm, partial_ref), (other_hbm, other_ref), (levels_hbm, levels_ref), (mix_hbm, mix_ref),
         (top_hbm, top_ref), (top_keep_hbm, top_keep_ref), (slots_hbm, slots_ref),
+        (sends_hbm, sends_ref), (edges_hbm, edges_ref),
     ], semaphores)
     chunk = slot_count // CHUNKS
     used = len(needed)
@@ -379,13 +402,13 @@
         where = EDGES.index((dx, dy))
         return edges_ref[2 * where] + edges_ref[2 * where + 1]
 
+    finish(needed)
     after, before = edge(1, 0), edge(-1, 0)
     right, left = edge(0, 1), edge(0, -1)
     corners = {(dx, dy): edge(dx, dy) for dx in (1, -1) for dy in (1, -1)}
     lane = lax.broadcasted_iota(jnp.int32, (TILE, LANES), 1)
     short = lax.broadcasted_iota(jnp.int32, (HALO, LANES), 1)
     surface_ref[...] = jnp.zeros_like(surface_ref)
-    finish(needed)
     for field in range(fields):
         surface_ref[field, 0:rows, 0:columns] = partial_ref[field] + other_ref[field]
         for half in range(halves):
@@ -444,12 +467,24 @@
                 given, weights_ref[slot], (((1,), (1,)), ((), ())), preferred_element_type=jnp.float32
             )
             sums_ref[pl.ds(slots_ref[0, slot], 1)] += got[row : row + 1]
+    me = lax.axis_index("gx") * lax.axis_size("gy") + lax.axis_index("gy")
+    blocks = sums_ref.shape[0]
+    copies = back_ref.shape[0] // blocks
+
+    def place_rows(block):
+        tile = sends_ref[block, me]
+        back_ref[pl.ds(block * copies, copies)] = jnp.zeros((copies,) + back_ref.shape[1:], jnp.float32)
+
+        @pl.when(tile >= 0)
+        def _():
+            for copy in range(copies):
+                back_ref[block * copies + copy, pl.ds(tile, 1)] = sums_ref[pl.ds(block, 1)]
+
     if few:
-        for block in range(sums_ref.shape[0]):
-            both = jnp.broadcast_to(sums_ref[block : block + 1], (2, LANES))
-            back_ref[2 * block : 2 * block + 2] = both
+        for block in range(blocks):
+            place_rows(block)
     else:
-        back_ref[...] = sums_ref[...]
+        lax.fori_loop(0, blocks, lambda block, carry: (place_rows(block), carry)[1], 0)
     finish(leaving)
 
 
@@ -505,16 +540,20 @@
 
         def one(place, source=source, target=target, step=step):
             level = level_of(place)
-            new = step_slab(
-                source[place], source[place - 1], source[place + 1], keep_ref[place], mix_ref[...], levels_ref[...],
-                level, depth_share(level, total_levels) * surface_ref[1],
-            )
+            share = depth_share(level, total_levels)
             if step < STEPS:
-                target[place] = new
+                target[place] = step_slab(
+                    source[place], source[place - 1], source[place + 1], keep_ref[place], mix_ref[...],
+                    levels_ref[...], level, share * surface_ref[1],
+                )
             else:
+                own = slice(0, rows), slice(0, columns)
+                new = last_slab(
+                    source[place], source[(place - 1,) + own], source[(place + 1,) + own], keep_ref[(place,) + own],
+                    mix_ref[own], share * surface_ref[(1,) + own],
+                )
                 index = place - HALO
-                wet = levels_ref[0:rows, 0:columns] > level
-                temp_ref[index] = jnp.where(wet, new[0:rows, 0:columns], temp_ref[index])
+                temp_ref[index] = jnp.where(levels_ref[own] > level, new, temp_ref[index])
 
         if step < STEPS:
             in_order(jnp.where(gz == 0, HALO, step), layers + HALO - step, one)
@@ -536,24 +575,6 @@
                 used += 1
             finish(leaving)
         source, target = target, source
-
-
-def gather_kernel(sends_ref, returned_ref, surface_ref):
-    me = lax.axis_index("gx") * lax.axis_size("gy") + lax.axis_index("gy")
-    surface_ref[...] = jnp.zeros_like(surface_ref)
-    blocks = sends_ref.shape[0]
-    copies = returned_ref.shape[0] // blocks
-
-    def one(block, carry):
-        tile = sends_ref[me, block]
-        place = jnp.maximum(tile, 0)
-        got = returned_ref[pl.ds(block * copies, 1)]
-        for copy in range(1, copies):
-            got = got + returned_ref[pl.ds(block * copies + copy, 1)]
-        surface_ref[pl.ds(place, 1)] += jnp.where(tile >= 0, got, 0.0)
-        return carry
-
-    lax.fori_loop(0, blocks, one, 0)
 
 
 def call(body, outs, scratch, operands, places, out_places, cost=0):
@@ -615,15 +636,17 @@
     deep = (layers + 2 * HALO,) + slab
 
     high_rows = (2, layers, TILE, columns)
-    low, high = call(
+    one, two = call(
         rows_kernel, [strip, strip],
         [high_rows, pltpu.VMEM((2, TILE, columns), jnp.int32), (2, TILE, columns), 6],
         (ocean_temp, bathy_levels, mixing), "hhh", "vv", cost=slab_cost,
     )
-    forward = [(i, i + 1) for i in range(gx_count - 1)]
-    backward = [(target, source) for source, target in forward]
-    before_rows = lax.ppermute(high, "gx", forward)
-    after_rows = lax.ppermute(low, "gx", backward)
+    rows_one, rows_two = (
+        lax.ppermute(part, "gx", [
+            pair for x in range(start, gx_count - 1, 2) for pair in ((x, x + 1), (x + 1, x))
+        ]) for start, part in enumerate((one, two))
+    )
+
     outs = [(blocks, tall, LANES)] if few else [(blocks, TILE, LANES), (2, tall, LANES)]
     sides = 1 if few and gy_count == 2 else 2
     scratch = [
@@ -633,7 +656,7 @@
     ]
     sent = call(
         functools.partial(send_kernel, few=few, sides=sides), outs, scratch + ([(sides, tall, LANES)] if few else []),
-        (sends, atm_flux, ocean_temp, bathy_levels, mixing, low), "hhhhhh", "v" * len(outs), cost=2 * slab_cost,
+        (sends, atm_flux, ocean_temp, bathy_levels, mixing), "hhhhh", "v" * len(outs), cost=2 * slab_cost,
     )
     got = [lax.all_to_all(sent[0], BLOCKS_AXES, split_axis=0, concat_axis=0, tiled=True)]
     if not few:
@@ -644,20 +667,24 @@
 
     strips = (4, 2 * TILE, LANES)
     packed_shape = (2, slab[0], LANES)
-    partial, edges, shared, levels, mix, packed = call(
+    pair_shape = (2,) + strip
+    partial, edges = call(
         functools.partial(regrid_kernel, few=few),
+        [(fields, rows, columns), (2 * blocks, 2 * TILE, LANES) if few else strips],
         [
-            (fields, rows, columns), (2 * blocks, 2 * TILE, LANES) if few else strips,
-            (TOP + HALO,) + slab, slab, slab, packed_shape,
+            pltpu.SMEM(regrid_slots.shape, jnp.int32), (blocks, TILE, LANES), like(regrid_weights),
+            (fields, rows, columns), 3 + CHUNKS, (rows * columns // LANES * TILE, LANES),
+        ] + ([strips] if few else []),
+        (regrid_slots, got[0], regrid_weights), "hhh", "hv", cost=4 * slab_cost,
+    )
+    shared, levels, mix, packed = call(
+        functools.partial(halo_kernel, few=few),
+        [(TOP + HALO,) + slab, slab, slab, packed_shape],
+        [
+            got[-1].shape, (TOP + HALO, rows, columns), like(bathy_levels), like(mixing), pair_shape, slab, slab,
+            packed_shape, 10,
         ],
-        [
-            pltpu.SMEM(regrid_slots.shape, jnp.int32), like(regrid_weights), (TOP + HALO, rows, columns),
-            like(bathy_levels), like(mixing), slab, slab, packed_shape, 8 + CHUNKS,
-            (rows * columns // LANES * TILE, LANES),
-        ] + ([strips] if few else []),
-        (
-            regrid_slots, *got, regrid_weights, ocean_temp, bathy_levels, mixing, after_rows, before_rows,
-        ), "h" + "v" * len(got) + "hhhhvv", "vvvhhh", cost=10 * slab_cost,
+        (got[-1], ocean_temp, bathy_levels, mixing, rows_one, rows_two, partial), "h" * 7, "vhhh", cost=slab_cost,
     )
     other_partial = lax.ppermute(partial, "gz", swap)
     other_shared = lax.ppermute(shared, "gz", swap)
@@ -679,21 +706,21 @@
     moved, keep, top_moved, top_keep = call(
         first_kernel, [deep, deep, top, top],
         [
-            like(ocean_temp), strip, strip, packed_shape, (TOP + HALO,) + slab, slab, slab,
+            like(ocean_temp), pair_shape, packed_shape, (TOP + HALO,) + slab, slab, slab,
             deep, deep, top, top, deep, (TOP,) + slab, 9 + CHUNKS + parts,
         ],
-        (ocean_temp, after_rows, before_rows, packed, other_shared, levels, mix), "h" * 7, "hhhh", cost=80 * slab_cost,
+        (ocean_temp, rows_one, rows_two, packed, other_shared, levels, mix), "h" * 7, "hhhh", cost=slab_cost,
     )
     surface, back = call(
         functools.partial(skin_kernel, few=few, total_levels=total_levels),
-        [(fields,) + slab, ((2 if few else 1) * blocks, LANES)],
+        [(fields,) + slab, ((2 if few else 1) * blocks, own_tiles, LANES)],
         [
-            pltpu.SMEM(regrid_slots.shape, jnp.int32), like(partial), like(partial), like(regrid_weights), slab, slab,
-            top, top, (fields,) + slab, 8 + CHUNKS,
+            pltpu.SMEM(sends.shape, jnp.int32), pltpu.SMEM(regrid_slots.shape, jnp.int32), like(partial), like(partial),
+            edges.shape, like(regrid_weights), slab, slab, top, top, (fields,) + slab, 10 + CHUNKS,
             top, top, (rows * columns // LANES, LANES), (regrid_weights.shape[0], LANES), (blocks, LANES),
         ],
-        (regrid_slots, partial, other_partial, edges, regrid_weights, levels, mix, top_moved, top_keep),
-        "hhhvhhhhh", "hv", cost=20 * slab_cost,
+        (sends, regrid_slots, partial, other_partial, edges, regrid_weights, levels, mix, top_moved, top_keep),
+        "hhhhhhhhhh", "hv", cost=20 * slab_cost,
     )
     if few:
         returned = lax.all_to_all(back, ALL_AXES, split_axis=0, concat_axis=0, tiled=True)
@@ -705,7 +732,7 @@
         [like(ocean_temp), deep, slab, slab, (fields,) + slab, 5 + parts + len(pieces(layers)), deep, deep],
         (ocean_temp, moved, keep, levels, mix, surface), "h" * 6, "h", cost=120 * slab_cost,
     )
-    atm_surface, = call(gather_kernel, [(own_tiles, LANES)], [], (sends, returned), "sv", "v", cost=slab_cost // 10)
+    atm_surface = returned.sum(axis=0)
     return (ocean, atm_surface)
 
 

time: 63 us -> 57.3 us (0.910)
  starting transfers between devices: 25 us -> 21.1 us
  waiting for transfers between devices: 4.25 us -> 2.63 us
    ppermute x2, waiting for transfers between devices: 4.23 us -> 0.01 us  [per_device(): lax.ppermute(part, 'gx', [pair for x in range(start, gx_count - 1, 2) for...]
    ppermute x2, starting transfers between devices: 5.28 us -> 2.18 us  [per_device(): lax.ppermute(part, 'gx', [pair for x in range(start, gx_count - 1, 2) for...]
    all_to_all x1, starting transfers between devices: 6.31 us -> 3.41 us  [per_device(): lax.all_to_all(edges, ALL_AXES, split_axis=0, concat_axis=0, tiled=True)]
    all_to_all x1, waiting for transfers between devices: 0.01 us -> 2.62 us  [per_device(): lax.all_to_all(sent[0], BLOCKS_AXES, split_axis=0, concat_axis=0, tiled=T...]
    ppermute x1, starting transfers between devices: 0.89 us -> 2.94 us  [per_device(): other_shared = lax.ppermute(shared, 'gz', swap)]
    unnamed x14 -> x12, local copies, waits for them, and re-layouts: 3.41 us -> 2.84 us
  transfers between devices with their start and end apart: 7 -> 7, of which waited for: 1 -> 1; matrix products, arithmetic and copies ran while one was open for 0% -> 0% of each run, Pallas kernels for 23% -> 35%
where the time goes in v4:
time: 57.3 us; the launch traced here: 56.8 us
  Pallas kernels  28.8 us (50%)
  starting transfers between devices  21.1 us (37%)
  local copies, waits for them, and re-layouts  2.84 us (5%)
  waiting for transfers between devices  2.63 us (5%)
  between operations  0.78 us (1%)
  other arithmetic  0.61 us (1%)
    pallas_call x7, Pallas kernels, call(): pl.pallas_call(body, out_shape=[jax.ShapeDtypeStruct(out, jnp.float32) fo...  28.8 us
    all_to_all x1, starting transfers between devices, per_device(): lax.all_to_all(sent[0], BLOCKS_AXES, split_axis=0, concat_axis=0, tiled=T...  6.37 us
    all_to_all x1, starting transfers between devices, per_device(): lax.all_to_all(back, ALL_AXES, split_axis=0, concat_axis=0, tiled=True)  5.98 us
    all_to_all x1, starting transfers between devices, per_device(): lax.all_to_all(edges, ALL_AXES, split_axis=0, concat_axis=0, tiled=True)  3.41 us
    ppermute x1, starting transfers between devices, per_device(): other_shared = lax.ppermute(shared, 'gz', swap)  2.94 us
    unnamed x12, local copies, waits for them, and re-layouts  2.84 us
    all_to_all x1, waiting for transfers between devices, per_device(): lax.all_to_all(sent[0], BLOCKS_AXES, split_axis=0, concat_axis=0, tiled=T...  2.62 us
    ppermute x2, starting transfers between devices, per_device(): lax.ppermute(part, 'gx', [pair for x in range(start, gx_count - 1, 2) for...  2.18 us
  transfers between devices with their start and end apart: 7, of which 1 were waited for; matrix products, arithmetic and copies ran while one was open for 0% of the time, Pallas kernels for 35%

profile of v4, /device:TPU:1, one launch (start us, length us, event | category | flops | bytes accessed | tf_op | source)
XLA Modules:
  0.0 56.8 jit_solution(6154323861196290268)
XLA Ops:
  0.6 2.0 %shard_map.87 = f32[8,48,128]{2,1,0:T(8,128)} custom-call(s32[8,8]{1,0:T(8,128)} %bitcast.1, bf16[8,2,128]{2,1,0:T(2,128)(2,1)} %flux_hbm.1, f32[32,32,256]{2,1,0:T(8,128)} %temp_hbm.7, s32[32,256]{1,0:T(8,128)} %bathy_hbm.3, f32[32,256]{1,0:T(8,128)} %mixing_hbm.3), custom_call_target="tpu_custom_call" | custom-call | flops 614400 | bytes 153600 | tf_op jit(solution)/shard_map/pallas_call | solution.py:591
  2.7 6.4 %all-to-all-start = ((f32[8,48,128]{2,1,0:T(8,128)}), f32[8,48,128]{2,1,0:T(8,128)S(1)}, u32[]{:S(2)}, u32[]{:S(2)}) async-start(f32[8,48,128]{2,1,0:T(8,128)} %shard_map.87), calls=%async_computation | async-start | bytes 393216 | tf_op jit(solution)/shard_map/all_to_all | solution.py:661
  9.0 1.9 %shard_map.86 = (f32[34,4,256]{2,1,0:T(4,128)}, f32[34,4,256]{2,1,0:T(4,128)}) custom-call(f32[32,32,256]{2,1,0:T(8,128)} %temp_hbm.7, s32[32,256]{1,0:T(8,128)} %bathy_hbm.3, f32[32,256]{1,0:T(8,128)} %mixing_hbm.3), custom_call_target="tpu_custom_call" | custom-call | flops 307200 | bytes 76800 | tf_op jit(solution)/shard_map/pallas_call | solution.py:591
  10.9 1.5 %collective-permute-start = (f32[34,4,256]{2,1,0:T(4,128)}, f32[34,4,256]{2,1,0:T(4,128)S(1)}, u32[]{:S(2)}, u32[]{:S(2)}) collective-permute-start(f32[34,4,256]{2,1,0:T(4,128)} %get-tuple-element.16), channel_id=1, source_target_pairs={{0,4},{4,0},{8,12},{12,8},{1,5},{5,1},{9,13},{13,9},{2,6},{6,2},{1... | collective-permute-start | bytes 417800 | tf_op jit(solution)/shard_map/ppermute | solution.py:645
  12.5 0.7 %collective-permute-start.1 = (f32[34,4,256]{2,1,0:T(4,128)}, f32[34,4,256]{2,1,0:T(4,128)S(1)}, u32[]{:S(2)}, u32[]{:S(2)}) collective-permute-start(f32[34,4,256]{2,1,0:T(4,128)} %get-tuple-element.17), channel_id=1, source_target_pairs={{4,8},{8,4},{5,9},{9,5},{6,10},{10,6},{7,11},{11,7},{20,24},{24,20... | collective-permute-start | bytes 417800 | tf_op jit(solution)/shard_map/ppermute | solution.py:645
  13.1 2.6 %all-to-all-done.flux_hbm.sides_hbm = f32[8,48,128]{2,1,0:T(8,128)S(1)} async-done(((f32[8,48,128]{2,1,0:T(8,128)}), f32[8,48,128]{2,1,0:T(8,128)S(1)}, u32[]{:S(2)}, u32[]{:S(2)}) %all-to-all-start) | async-done | bytes 196640 | tf_op jit(solution)/shard_map/all_to_all | solution.py:661
  15.7 0.0 copy-start
  15.7 0.7 %copy-done = f32[8,48,128]{2,1,0:T(8,128)} copy-done((f32[8,48,128]{2,1,0:T(8,128)}, f32[8,48,128]{2,1,0:T(8,128)S(1)}, u32[]{:S(2)}) %copy-start) | copy-done | bytes 196632
  16.4 3.5 %shard_map.88 = (f32[2,32,256]{2,1,0:T(8,128)}, f32[16,16,128]{2,1,0:T(8,128)}) custom-call(s32[2,64]{1,0:T(2,128)} %slots_hbm.3, f32[8,48,128]{2,1,0:T(8,128)} %copy-done, bf16[64,128,128]{2,1,0:T(8,128)(2,1)} %weights_hbm.3), custom_call_target="tpu_custom_call" | custom-call | flops 1228800 | bytes 307200 | tf_op jit(solution)/shard_map/pallas_call | solution.py:591
  19.9 0.0 collective-permute-done.one_hbm
  19.9 0.0 copy-start.1
  19.9 0.0 collective-permute-done.1.two_hbm
  19.9 0.0 copy-start.2
  20.0 0.6 %copy-done.1 = f32[34,4,256]{2,1,0:T(4,128)} copy-done((f32[34,4,256]{2,1,0:T(4,128)}, f32[34,4,256]{2,1,0:T(4,128)S(1)}, u32[]{:S(2)}) %copy-start.1) | copy-done | bytes 139288
  20.6 0.1 copy-done.2
  20.7 2.9 %shard_map.89 = (f32[9,40,384]{2,1,0:T(8,128)}, f32[40,384]{1,0:T(8,128)}, f32[40,384]{1,0:T(8,128)}, f32[2,40,128]{2,1,0:T(8,128)}) custom-call(f32[8,48,128]{2,1,0:T(8,128)} %copy-done, f32[32,32,256]{2,1,0:T(8,128)} %temp_hbm.7, s32[32,256]{1,0:T(8,128)} %bathy_hbm.3, f32[32,256]{1,0:T(8,128)} %mixing_hbm.3, f32[34,4,256]{2,1,0:T(4,128)} %copy-done.1, ...), custom_call_target="tpu_custom_call" | custom-call | flops 307200 | bytes 76800 | tf_op jit(solution)/shard_map/pallas_call | solution.py:591
  23.6 2.9 %collective-permute-start.2 = (f32[9,40,384]{2,1,0:T(8,128)}, f32[9,40,384]{2,1,0:T(8,128)S(1)}, u32[]{:S(2)}, u32[]{:S(2)}) collective-permute-start(f32[9,40,384]{2,1,0:T(8,128)} %get-tuple-element.20), channel_id=1, source_target_pairs={{0,1},{1,0},{2,3},{3,2},{4,5},{5,4},{6,7},{7,6},{8,9},{9,8},{10,11... | collective-permute-start | bytes 1658888 | tf_op jit(solution)/shard_map/ppermute | solution.py:690
  26.5 3.4 %all-to-all-start.1 = ((f32[16,16,128]{2,1,0:T(8,128)}), f32[16,16,128]{2,1,0:T(8,128)S(1)}, u32[]{:S(2)}, u32[]{:S(2)}) async-start(f32[16,16,128]{2,1,0:T(8,128)} %get-tuple-element.25), calls=%async_computation.1 | async-start | bytes 262144 | tf_op jit(solution)/shard_map/all_to_all | solution.py:692
  29.9 0.2 collective-permute-start.3
  30.1 0.0 collective-permute-done.2.other_hbm
  30.1 0.0 copy-start.3
  30.1 0.8 %copy-done.3 = f32[9,40,384]{2,1,0:T(8,128)} copy-done((f32[9,40,384]{2,1,0:T(8,128)}, f32[9,40,384]{2,1,0:T(8,128)S(1)}, u32[]{:S(2)}) %copy-start.3) | copy-done | bytes 552984
  30.9 6.3 %shard_map.90 = (f32[40,40,384]{2,1,0:T(8,128)}, f32[40,40,384]{2,1,0:T(8,128)}, f32[4,40,384]{2,1,0:T(8,128)}, f32[4,40,384]{2,1,0:T(8,128)}) custom-call(f32[32,32,256]{2,1,0:T(8,128)} %temp_hbm.7, f32[34,4,256]{2,1,0:T(4,128)} %copy-done.1, f32[34,4,256]{2,1,0:T(4,128)} %copy-done.2, f32[2,40,128]{2,1,0:T(8,128)} %get-tuple-element.19.packed_hbm, ...), custom_call_target="tpu_custom_call" | custom-call | flops 307200 | bytes 76800 | tf_op jit(solution)/shard_map/pallas_call | solution.py:591
  37.2 0.0 collective-permute-done.3.other_hbm
  37.3 0.0 copy-start.5
  37.3 0.0 all-to-all-done.1.edges_hbm
  37.3 0.0 copy-start.4
  37.3 0.6 %copy-done.5 = f32[2,32,256]{2,1,0:T(8,128)} copy-done((f32[2,32,256]{2,1,0:T(8,128)}, f32[2,32,256]{2,1,0:T(8,128)S(1)}, u32[]{:S(2)}) %copy-start.5) | copy-done | bytes 65560
  37.9 0.1 copy-done.4
  37.9 4.2 %shard_map.91 = (f32[2,40,384]{2,1,0:T(8,128)}, f32[16,8,128]{2,1,0:T(8,128)}) custom-call(s32[8,8]{1,0:T(8,128)} %bitcast.2, s32[2,64]{1,0:T(2,128)} %slots_hbm.3, f32[2,32,256]{2,1,0:T(8,128)} %get-tuple-element.18.after_ref.partial_hbm, f32[2,32,256]{2,1,0:T(8,128)} %copy-done.5, f32[16,16,128]{2,1,0:T(8,128)} %copy-done.4, ...), custom_call_target="tpu_custom_call" | custom-call | flops 6144000 | bytes 1536000 | tf_op jit(solution)/shard_map/pallas_call | solution.py:591
  42.2 6.0 %all-to-all-start.2 = ((f32[16,8,128]{2,1,0:T(8,128)}), f32[16,8,128]{2,1,0:T(8,128)S(1)}, u32[]{:S(2)}, u32[]{:S(2)}) async-start(f32[16,8,128]{2,1,0:T(8,128)} %get-tuple-element.29), calls=%async_computation.2 | async-start | bytes 131072 | tf_op jit(solution)/shard_map/all_to_all | solution.py:726
  48.1 8.0 %shard_map.92 = f32[32,32,256]{2,1,0:T(8,128)} custom-call(f32[32,32,256]{2,1,0:T(8,128)} %temp_hbm.7, f32[40,40,384]{2,1,0:T(8,128)} %get-tuple-element.23.moved_hbm, f32[40,40,384]{2,1,0:T(8,128)} %get-tuple-element.24.keep_hbm, f32[40,384]{1,0:T(8,128)} %get-tuple-element.21.levels_hbm, f32[40,384]{1,0:T(8,128)} %get-tuple-element.22.mix_hbm, ...), custom_call_target="tpu_custom_call" | custom-call | flops 36864000 | bytes 9216000 | tf_op jit(solution)/shard_map/pallas_call | solution.py:591
  56.1 0.0 all-to-all-done.2
  56.2 0.6 %reduce_sum.9 = f32[8,128]{1,0:T(8,128)} reduce(f32[16,8,128]{2,1,0:T(8,128)S(1)} %all-to-all-done.2, f32[]{:T(128)} %constant.0.clone.1), dimensions={0}, to_apply=%region_0.0 | reduce | flops 15360 | bytes 69636 | tf_op jit(solution)/shard_map/reduce_sum | solution.py:735
Async XLA Ops:
  2.7 13.1 %all-to-all-start = ((f32[8,48,128]{2,1,0:T(8,128)}), f32[8,48,128]{2,1,0:T(8,128)S(1)}, u32[]{:S(2)}, u32[]{:S(2)}) async-start(f32[8,48,128]{2,1,0:T(8,128)} %shard_map.87), calls=%async_computation | async-start | bytes 393216 | tf_op jit(solution)/shard_map/all_to_all | solution.py:661
  10.9 9.0 %collective-permute-start = (f32[34,4,256]{2,1,0:T(4,128)}, f32[34,4,256]{2,1,0:T(4,128)S(1)}, u32[]{:S(2)}, u32[]{:S(2)}) collective-permute-start(f32[34,4,256]{2,1,0:T(4,128)} %get-tuple-element.16), channel_id=1, source_target_pairs={{0,4},{4,0},{8,12},{12,8},{1,5},{5,1},{9,13},{13,9},{2,6},{6,2},{1... | collective-permute-start | bytes 417800 | tf_op jit(solution)/shard_map/ppermute | solution.py:645
  12.5 7.5 %collective-permute-start.1 = (f32[34,4,256]{2,1,0:T(4,128)}, f32[34,4,256]{2,1,0:T(4,128)S(1)}, u32[]{:S(2)}, u32[]{:S(2)}) collective-permute-start(f32[34,4,256]{2,1,0:T(4,128)} %get-tuple-element.17), channel_id=1, source_target_pairs={{4,8},{8,4},{5,9},{9,5},{6,10},{10,6},{7,11},{11,7},{20,24},{24,20... | collective-permute-start | bytes 417800 | tf_op jit(solution)/shard_map/ppermute | solution.py:645
  15.7 0.7 %copy-start = (f32[8,48,128]{2,1,0:T(8,128)}, f32[8,48,128]{2,1,0:T(8,128)S(1)}, u32[]{:S(2)}) copy-start(f32[8,48,128]{2,1,0:T(8,128)S(1)} %all-to-all-done.flux_hbm.sides_hbm) | copy-start | bytes 589828
  19.9 0.7 %copy-start.1 = (f32[34,4,256]{2,1,0:T(4,128)}, f32[34,4,256]{2,1,0:T(4,128)S(1)}, u32[]{:S(2)}) copy-start(f32[34,4,256]{2,1,0:T(4,128)S(1)} %collective-permute-done.one_hbm) | copy-start | bytes 417796
  19.9 0.7 %copy-start.2 = (f32[34,4,256]{2,1,0:T(4,128)}, f32[34,4,256]{2,1,0:T(4,128)S(1)}, u32[]{:S(2)}) copy-start(f32[34,4,256]{2,1,0:T(4,128)S(1)} %collective-permute-done.1.two_hbm) | copy-start | bytes 417796
  23.6 6.6 %collective-permute-start.2 = (f32[9,40,384]{2,1,0:T(8,128)}, f32[9,40,384]{2,1,0:T(8,128)S(1)}, u32[]{:S(2)}, u32[]{:S(2)}) collective-permute-start(f32[9,40,384]{2,1,0:T(8,128)} %get-tuple-element.20), channel_id=1, source_target_pairs={{0,1},{1,0},{2,3},{3,2},{4,5},{5,4},{6,7},{7,6},{8,9},{9,8},{10,11... | collective-permute-start | bytes 1658888 | tf_op jit(solution)/shard_map/ppermute | solution.py:690
  26.5 10.7 %all-to-all-start.1 = ((f32[16,16,128]{2,1,0:T(8,128)}), f32[16,16,128]{2,1,0:T(8,128)S(1)}, u32[]{:S(2)}, u32[]{:S(2)}) async-start(f32[16,16,128]{2,1,0:T(8,128)} %get-tuple-element.25), calls=%async_computation.1 | async-start | bytes 262144 | tf_op jit(solution)/shard_map/all_to_all | solution.py:692
  29.9 7.3 %collective-permute-start.3 = (f32[2,32,256]{2,1,0:T(8,128)}, f32[2,32,256]{2,1,0:T(8,128)S(1)}, u32[]{:S(2)}, u32[]{:S(2)}) collective-permute-start(f32[2,32,256]{2,1,0:T(8,128)} %get-tuple-element.18.after_ref.partial_hbm), channel_id=1, source_target_pairs={{0,1},{1,0},{2,3},{3,2},{4,5},{5,4},{6,7},{7,6},{8,9},{9,8},{10,11... | collective-permute-start | bytes 196616 | tf_op jit(solution)/shard_map/ppermute | solution.py:689
  30.1 0.8 %copy-start.3 = (f32[9,40,384]{2,1,0:T(8,128)}, f32[9,40,384]{2,1,0:T(8,128)S(1)}, u32[]{:S(2)}) copy-start(f32[9,40,384]{2,1,0:T(8,128)S(1)} %collective-permute-done.2.other_hbm) | copy-start | bytes 1658884
  37.3 0.6 %copy-start.5 = (f32[2,32,256]{2,1,0:T(8,128)}, f32[2,32,256]{2,1,0:T(8,128)S(1)}, u32[]{:S(2)}) copy-start(f32[2,32,256]{2,1,0:T(8,128)S(1)} %collective-permute-done.3.other_hbm) | copy-start | bytes 196612
  37.3 0.7 %copy-start.4 = (f32[16,16,128]{2,1,0:T(8,128)}, f32[16,16,128]{2,1,0:T(8,128)S(1)}, u32[]{:S(2)}) copy-start(f32[16,16,128]{2,1,0:T(8,128)S(1)} %all-to-all-done.1.edges_hbm) | copy-start | bytes 393220
  42.2 14.0 %all-to-all-start.2 = ((f32[16,8,128]{2,1,0:T(8,128)}), f32[16,8,128]{2,1,0:T(8,128)S(1)}, u32[]{:S(2)}, u32[]{:S(2)}) async-start(f32[16,8,128]{2,1,0:T(8,128)} %get-tuple-element.29), calls=%async_computation.2 | async-start | bytes 131072 | tf_op jit(solution)/shard_map/all_to_all | solution.py:726

commit v5 on v4

--- a/solution.py
+++ b/solution.py
@@ -47,17 +47,12 @@
     ref[:, columns:] = tile
 
 
-def wet_around(levels, level):
-    rows, lanes = levels.shape
-    wet = jnp.where(levels > level, 0.1, 0.0)
-    total = pltpu.roll(wet, 1, 0) + pltpu.roll(wet, rows - 1, 0)
-    return total + (pltpu.roll(wet, 1, 1) + pltpu.roll(wet, lanes - 1, 1))
-
-
-def keep_share(levels, mixing, level):
+def keep_share(levels, around_ref, mixing, level):
+    wet = [jnp.where(around_ref[side] > level, 0.1, 0.0) for side in range(4)]
+    wet_around = (wet[0] + wet[1]) + (wet[2] + wet[3])
     above = jnp.where(level > 0.0, 1.0, 0.0)
     vertical = above + jnp.where(levels > level + 1.0, 1.0, 0.0)
-    return 1.0 - wet_around(levels, level) - mixing * vertical
+    return 1.0 - wet_around - mixing * vertical
 
 
 def step_slab(center, over, under, keep, mixing, levels, level, forcing):
@@ -110,7 +105,9 @@
         body(start + index)
 
 
-def rows_kernel(temp_ref, bathy_ref, mixing_ref, one_ref, two_ref, temp_rows, bathy_rows, mixing_rows, semaphores):
+def rows_kernel(
+    temp_ref, bathy_ref, mixing_ref, one_hbm, two_hbm, temp_rows, bathy_rows, mixing_rows, one_ref, two_ref, semaphores,
+):
     layers, rows, columns = temp_ref.shape
     copies = []
     for side in range(2):
@@ -127,15 +124,20 @@
         low, high = read(0)[..., 0:HALO, :], read(1)[..., TILE - HALO :, :]
         one_ref[place] = jnp.where(even, high, low)
         two_ref[place] = jnp.where(even, low, high)
+    finish(begin([(one_ref, one_hbm), (two_ref, two_hbm)], semaphores, len(copies)))
 
 
 def send_kernel(sends_hbm, flux_hbm, temp_hbm, bathy_hbm, mixing_hbm, *refs, few, sides):
     if few:
-        message_ref, sends_ref, flux_ref, temp_ref, bathy_ref, mixing_ref, semaphores, flux_scratch, strips_ref = refs
+        (
+            message_hbm, sends_ref, flux_ref, temp_ref, bathy_ref, mixing_ref, semaphores, flux_scratch, message_ref,
+            strips_ref,
+        ) = refs
         fluxes_ref = message_ref
     else:
         (
-            fluxes_ref, strips_ref, sends_ref, flux_ref, temp_ref, bathy_ref, mixing_ref, semaphores, flux_scratch,
+            fluxes_hbm, strips_hbm, sends_ref, flux_ref, temp_ref, bathy_ref, mixing_ref, semaphores, flux_scratch,
+            fluxes_ref, strips_ref,
         ) = refs
     layers, rows, columns = temp_hbm.shape
     gy, gy_count = lax.axis_index("gy"), lax.axis_size("gy")
@@ -181,16 +183,22 @@
         fluxes_ref[block, 0:fields] = sent
         return carry
 
+    used = len(copies)
     if few:
+        leaving = []
         for block in range(fluxes_ref.shape[0]):
             one(block, 0)
+            leaving += begin([(message_ref.at[block], message_hbm.at[block])], semaphores, used + block)
     else:
+        leaving = begin([(strips_ref, strips_hbm)], semaphores, used)
         lax.fori_loop(0, fluxes_ref.shape[0], one, 0)
+        leaving += begin([(fluxes_ref, fluxes_hbm)], semaphores, used + 1)
+    finish(leaving)
 
 
 def regrid_kernel(
-    slots_hbm, flux_hbm, weights_hbm, partial_hbm, edges_ref,
-    slots_ref, flux_ref, weights_ref, partial_ref, semaphores, sums_ref, *strip_scratch, few,
+    slots_hbm, flux_hbm, weights_hbm, partial_hbm, edges_hbm,
+    edges_ref, slots_ref, flux_ref, weights_ref, partial_ref, semaphores, sums_ref, *strip_scratch, few,
 ):
     fields, rows, columns = partial_ref.shape
     slot_count, tile_atm, patch = weights_ref.shape
@@ -241,13 +249,14 @@
             choice = jnp.where(x < gx, 0, jnp.where(x > gx, 1, jnp.where(y < gy, 2, 3)))
             edges_ref[entry] = strips_ref[choice]
 
+    leaving += begin([(edges_ref, edges_hbm)], semaphores, len(needed) + CHUNKS + 1)
     finish(leaving)
 
 
 def halo_kernel(
     sides_hbm, temp_hbm, bathy_hbm, mixing_hbm, one_hbm, two_hbm, after_ref,
-    shared_ref, levels_hbm, mix_hbm, packed_hbm,
-    sides_ref, temp_ref, bathy_ref, mixing_ref, pair_ref, levels_ref, mix_ref, packed_ref, semaphores, *, few,
+    shared_hbm, levels_hbm, mix_hbm, packed_hbm,
+    shared_ref, sides_ref, temp_ref, bathy_ref, mixing_ref, pair_ref, levels_ref, mix_ref, packed_ref, semaphores, *, few,
 ):
     layers, rows, columns = temp_hbm.shape
     lasts = pl.ds(layers - HALO, HALO)
@@ -284,9 +293,11 @@
     leaving = begin(
         [(levels_ref, levels_hbm), (mix_ref, mix_hbm), (packed_ref, packed_hbm)], semaphores, len(needed)
     )
+    used = len(needed) + 3
     for place, level in enumerate(list(range(TOP)) + list(range(layers - HALO, layers))):
         tile = side_tile(packed_ref[0], packed_ref[1], level)
         put_slab(shared_ref.at[place], temp_ref[place], next_ref[level], prev_ref[level], tile)
+        leaving += begin([(shared_ref.at[place], shared_hbm.at[place])], semaphores, used + place)
     finish(leaving)
 
 
@@ -294,7 +305,7 @@
     temp_hbm, one_hbm, two_hbm, packed_hbm, other_hbm, levels_hbm, mix_hbm,
     moved_hbm, keep_hbm, top_hbm, top_keep_hbm,
     temp_ref, pair_ref, packed_ref, other_ref, levels_ref, mix_ref,
-    moved_ref, keep_ref, top_ref, top_keep_ref, first_ref, skin_ref, semaphores,
+    moved_ref, keep_ref, top_ref, top_keep_ref, first_ref, skin_ref, around_ref, semaphores,
 ):
     layers = temp_hbm.shape[0]
     gz = lax.axis_index("gz")
@@ -311,6 +322,9 @@
     odd = lax.rem(lax.axis_index("gx"), 2)
     next_ref, prev_ref = pair_ref.at[odd], pair_ref.at[1 - odd]
     finish(needed)
+    tall, lanes = levels_ref.shape
+    for side, (shift, dim) in enumerate(((1, 0), (tall - 1, 0), (1, 1), (lanes - 1, 1))):
+        around_ref[side] = pltpu.roll(levels_ref[...], shift, dim)
 
     def level_of(place):
         return (first_level + place).astype(jnp.float32)
@@ -318,7 +332,7 @@
     def settle(place):
         level = level_of(place)
         first_ref[place] = jnp.where(levels_ref[...] > level, first_ref[place], 0.0)
-        keep_ref[place] = keep_share(levels_ref[...], mix_ref[...], level)
+        keep_ref[place] = keep_share(levels_ref[...], around_ref, mix_ref[...], level)
 
     def own_level(index):
         tile = side_tile(packed_ref[0], packed_ref[1], index)
@@ -345,7 +359,7 @@
         slab = jnp.where(gz == 0, first_ref[HALO + level], other_ref[level])
         skin_ref[level] = jnp.where(levels > float(level), slab, 0.0)
     for level in range(STEPS):
-        top_keep_ref[level] = keep_share(levels, mix_ref[...], jnp.float32(level))
+        top_keep_ref[level] = keep_share(levels, around_ref, mix_ref[...], jnp.float32(level))
         over = skin_ref[level - 1] if level else jnp.zeros_like(levels)
         top_ref[level] = step_slab(
             skin_ref[level], over, skin_ref[level + 1], top_keep_ref[level], mix_ref[...], levels, float(level), None
@@ -375,8 +389,8 @@
 
 def skin_kernel(
     sends_hbm, slots_hbm, partial_hbm, other_hbm, edges_hbm, weights_hbm, levels_hbm, mix_hbm, top_hbm, top_keep_hbm,
-    surface_hbm, back_ref,
-    sends_ref, slots_ref, partial_ref, other_ref, edges_ref, weights_ref, levels_ref, mix_ref, top_ref, top_keep_ref, surface_ref, semaphores,
+    surface_hbm, back_hbm,
+    back_ref, sends_ref, slots_ref, partial_ref, other_ref, edges_ref, weights_ref, levels_ref, mix_ref, top_ref, top_keep_ref, surface_ref, semaphores,
     first_ref, second_ref, sst_ref, rows_ref, *sums_scratch, few, total_levels,
 ):
     fields, rows, columns = partial_ref.shape
@@ -485,6 +499,7 @@
             place_rows(block)
     else:
         lax.fori_loop(0, blocks, lambda block, carry: (place_rows(block), carry)[1], 0)
+    leaving += begin([(back_ref, back_hbm)], semaphores, used + 1)
     finish(leaving)
 
 
@@ -578,7 +593,6 @@
 
 
 def call(body, outs, scratch, operands, places, out_places, cost=0):
-    space = {"v": pltpu.VMEM, "s": pltpu.SMEM, "h": pl.ANY}
     assert len(places) == len(operands) and len(out_places) == len(outs)
     scratch_shapes = []
     for item in scratch:
@@ -591,8 +605,8 @@
     return pl.pallas_call(
         body,
         out_shape=[jax.ShapeDtypeStruct(out, jnp.float32) for out in outs],
-        in_specs=[pl.BlockSpec(memory_space=space[place]) for place in places],
-        out_specs=[pl.BlockSpec(memory_space=space[place]) for place in out_places],
+        in_specs=[pl.BlockSpec(memory_space=pl.ANY) for place in places],
+        out_specs=[pl.BlockSpec(memory_space=pl.ANY) for place in out_places],
         scratch_shapes=scratch_shapes,
         compiler_params=pltpu.CompilerParams(vmem_limit_bytes=VMEM_LIMIT),
         cost_estimate=pl.CostEstimate(flops=cost, bytes_accessed=4 * cost // 16, transcendentals=0),
@@ -638,8 +652,8 @@
     high_rows = (2, layers, TILE, columns)
     one, two = call(
         rows_kernel, [strip, strip],
-        [high_rows, pltpu.VMEM((2, TILE, columns), jnp.int32), (2, TILE, columns), 6],
-        (ocean_temp, bathy_levels, mixing), "hhh", "vv", cost=slab_cost,
+        [high_rows, pltpu.VMEM((2, TILE, columns), jnp.int32), (2, TILE, columns), strip, strip, 8],
+        (ocean_temp, bathy_levels, mixing), "hhh", "hh", cost=slab_cost,
     )
     rows_one, rows_two = (
         lax.ppermute(part, "gx", [
@@ -651,12 +665,12 @@
     sides = 1 if few and gy_count == 2 else 2
     scratch = [
         pltpu.SMEM(sends.shape, jnp.int32), like(atm_flux), (sides, layers, rows, LANES),
-        pltpu.VMEM((sides, rows, LANES), jnp.int32), (sides, rows, LANES), 2 + 3 * sides,
-        (own_tiles, fields, LANES),
+        pltpu.VMEM((sides, rows, LANES), jnp.int32), (sides, rows, LANES), 4 + 3 * sides + FEW,
+        (own_tiles, fields, LANES), outs[0], (sides, tall, LANES),
     ]
     sent = call(
-        functools.partial(send_kernel, few=few, sides=sides), outs, scratch + ([(sides, tall, LANES)] if few else []),
-        (sends, atm_flux, ocean_temp, bathy_levels, mixing), "hhhhh", "v" * len(outs), cost=2 * slab_cost,
+        functools.partial(send_kernel, few=few, sides=sides), outs, scratch,
+        (sends, atm_flux, ocean_temp, bathy_levels, mixing), "hhhhh", "h" * len(outs), cost=2 * slab_cost,
     )
     got = [lax.all_to_all(sent[0], BLOCKS_AXES, split_axis=0, concat_axis=0, tiled=True)]
     if not few:
@@ -672,19 +686,20 @@
         functools.partial(regrid_kernel, few=few),
         [(fields, rows, columns), (2 * blocks, 2 * TILE, LANES) if few else strips],
         [
+            (2 * blocks, 2 * TILE, LANES) if few else strips,
             pltpu.SMEM(regrid_slots.shape, jnp.int32), (blocks, TILE, LANES), like(regrid_weights),
-            (fields, rows, columns), 3 + CHUNKS, (rows * columns // LANES * TILE, LANES),
+            (fields, rows, columns), 4 + CHUNKS, (rows * columns // LANES * TILE, LANES),
         ] + ([strips] if few else []),
-        (regrid_slots, got[0], regrid_weights), "hhh", "hv", cost=4 * slab_cost,
+        (regrid_slots, got[0], regrid_weights), "hhh", "hh", cost=4 * slab_cost,
     )
     shared, levels, mix, packed = call(
         functools.partial(halo_kernel, few=few),
         [(TOP + HALO,) + slab, slab, slab, packed_shape],
         [
-            got[-1].shape, (TOP + HALO, rows, columns), like(bathy_levels), like(mixing), pair_shape, slab, slab,
-            packed_shape, 10,
+            (TOP + HALO,) + slab, got[-1].shape, (TOP + HALO, rows, columns), like(bathy_levels), like(mixing),
+            pair_shape, slab, slab, packed_shape, 10 + TOP + HALO,
         ],
-        (got[-1], ocean_temp, bathy_levels, mixing, rows_one, rows_two, partial), "h" * 7, "vhhh", cost=slab_cost,
+        (got[-1], ocean_temp, bathy_levels, mixing, rows_one, rows_two, partial), "h" * 7, "hhhh", cost=slab_cost,
     )
     other_partial = lax.ppermute(partial, "gz", swap)
     other_shared = lax.ppermute(shared, "gz", swap)
@@ -707,7 +722,7 @@
         first_kernel, [deep, deep, top, top],
         [
             like(ocean_temp), pair_shape, packed_shape, (TOP + HALO,) + slab, slab, slab,
-            deep, deep, top, top, deep, (TOP,) + slab, 9 + CHUNKS + parts,
+            deep, deep, top, top, deep, (TOP,) + slab, (4,) + slab, 9 + CHUNKS + parts,
         ],
         (ocean_temp, rows_one, rows_two, packed, other_shared, levels, mix), "h" * 7, "hhhh", cost=slab_cost,
     )
@@ -715,12 +730,13 @@
         functools.partial(skin_kernel, few=few, total_levels=total_levels),
         [(fields,) + slab, ((2 if few else 1) * blocks, own_tiles, LANES)],
         [
+            ((2 if few else 1) * blocks, own_tiles, LANES),
             pltpu.SMEM(sends.shape, jnp.int32), pltpu.SMEM(regrid_slots.shape, jnp.int32), like(partial), like(partial),
-            edges.shape, like(regrid_weights), slab, slab, top, top, (fields,) + slab, 10 + CHUNKS,
+            edges.shape, like(regrid_weights), slab, slab, top, top, (fields,) + slab, 11 + CHUNKS,
             top, top, (rows * columns // LANES, LANES), (regrid_weights.shape[0], LANES), (blocks, LANES),
         ],
         (sends, regrid_slots, partial, other_partial, edges, regrid_weights, levels, mix, top_moved, top_keep),
-        "hhhhhhhhhh", "hv", cost=20 * slab_cost,
+        "hhhhhhhhhh", "hh", cost=20 * slab_cost,
     )
     if few:
         returned = lax.all_to_all(back, ALL_AXES, split_axis=0, concat_axis=0, tiled=True)

time: 57.3 us -> 56.2 us (0.981)
  Pallas kernels: 28.8 us -> 27.7 us
    pallas_call x7, Pallas kernels: 28.8 us -> 27.7 us  [call(): pl.pallas_call(body, out_shape=[jax.ShapeDtypeStruct(out, jnp.float32) fo...]
  transfers between devices with their start and end apart: 7 -> 7, of which waited for: 1 -> 1; matrix products, arithmetic and copies ran while one was open for 0% -> 0% of each run, Pallas kernels for 35% -> 34%
where the time goes in v5:
time: 56.2 us; the launch traced here: 55.7 us
  Pallas kernels  27.7 us (49%)
  starting transfers between devices  21.1 us (38%)
  local copies, waits for them, and re-layouts  2.84 us (5%)
  waiting for transfers between devices  2.63 us (5%)
  between operations  0.77 us (1%)
  other arithmetic  0.61 us (1%)
    pallas_call x7, Pallas kernels, call(): pl.pallas_call(body, out_shape=[jax.ShapeDtypeStruct(out, jnp.float32) fo...  27.7 us
    all_to_all x1, starting transfers between devices, per_device(): lax.all_to_all(sent[0], BLOCKS_AXES, split_axis=0, concat_axis=0, tiled=T...  6.37 us
    all_to_all x1, starting transfers between devices, per_device(): lax.all_to_all(back, ALL_AXES, split_axis=0, concat_axis=0, tiled=True)  6.01 us
    all_to_all x1, starting transfers between devices, per_device(): lax.all_to_all(edges, ALL_AXES, split_axis=0, concat_axis=0, tiled=True)  3.47 us
    ppermute x1, starting transfers between devices, per_device(): other_shared = lax.ppermute(shared, 'gz', swap)  2.93 us
    unnamed x12, local copies, waits for them, and re-layouts  2.84 us
    all_to_all x1, waiting for transfers between devices, per_device(): lax.all_to_all(sent[0], BLOCKS_AXES, split_axis=0, concat_axis=0, tiled=T...  2.61 us
    ppermute x2, starting transfers between devices, per_device(): lax.ppermute(part, 'gx', [pair for x in range(start, gx_count - 1, 2) for...  2.18 us
  transfers between devices with their start and end apart: 7, of which 1 were waited for; matrix products, arithmetic and copies ran while one was open for 0% of the time, Pallas kernels for 34%

profile of v5, /device:TPU:1, one launch (start us, length us, event | category | flops | bytes accessed | tf_op | source)
XLA Modules:
  0.0 55.7 jit_solution(8034608645720550346)
XLA Ops:
  0.6 2.2 %shard_map.87 = f32[8,48,128]{2,1,0:T(8,128)} custom-call(s32[8,8]{1,0:T(8,128)} %bitcast.1, bf16[8,2,128]{2,1,0:T(2,128)(2,1)} %flux_hbm.1, f32[32,32,256]{2,1,0:T(8,128)} %temp_hbm.7, s32[32,256]{1,0:T(8,128)} %bathy_hbm.3, f32[32,256]{1,0:T(8,128)} %mixing_hbm.3), custom_call_target="tpu_custom_call" | custom-call | flops 614400 | bytes 153600 | tf_op jit(solution)/shard_map/pallas_call | solution.py:605
  2.8 6.4 %all-to-all-start = ((f32[8,48,128]{2,1,0:T(8,128)}), f32[8,48,128]{2,1,0:T(8,128)S(1)}, u32[]{:S(2)}, u32[]{:S(2)}) async-start(f32[8,48,128]{2,1,0:T(8,128)} %shard_map.87), calls=%async_computation | async-start | bytes 393216 | tf_op jit(solution)/shard_map/all_to_all | solution.py:675
  9.2 1.9 %shard_map.86 = (f32[34,4,256]{2,1,0:T(4,128)}, f32[34,4,256]{2,1,0:T(4,128)}) custom-call(f32[32,32,256]{2,1,0:T(8,128)} %temp_hbm.7, s32[32,256]{1,0:T(8,128)} %bathy_hbm.3, f32[32,256]{1,0:T(8,128)} %mixing_hbm.3), custom_call_target="tpu_custom_call" | custom-call | flops 307200 | bytes 76800 | tf_op jit(solution)/shard_map/pallas_call | solution.py:605
  11.1 1.5 %collective-permute-start = (f32[34,4,256]{2,1,0:T(4,128)}, f32[34,4,256]{2,1,0:T(4,128)S(1)}, u32[]{:S(2)}, u32[]{:S(2)}) collective-permute-start(f32[34,4,256]{2,1,0:T(4,128)} %get-tuple-element.16), channel_id=1, source_target_pairs={{0,4},{4,0},{8,12},{12,8},{1,5},{5,1},{9,13},{13,9},{2,6},{6,2},{1... | collective-permute-start | bytes 417800 | tf_op jit(solution)/shard_map/ppermute | solution.py:659
  12.6 0.7 %collective-permute-start.1 = (f32[34,4,256]{2,1,0:T(4,128)}, f32[34,4,256]{2,1,0:T(4,128)S(1)}, u32[]{:S(2)}, u32[]{:S(2)}) collective-permute-start(f32[34,4,256]{2,1,0:T(4,128)} %get-tuple-element.17), channel_id=1, source_target_pairs={{4,8},{8,4},{5,9},{9,5},{6,10},{10,6},{7,11},{11,7},{20,24},{24,20... | collective-permute-start | bytes 417800 | tf_op jit(solution)/shard_map/ppermute | solution.py:659
  13.3 2.6 %all-to-all-done.flux_hbm.sides_hbm = f32[8,48,128]{2,1,0:T(8,128)S(1)} async-done(((f32[8,48,128]{2,1,0:T(8,128)}), f32[8,48,128]{2,1,0:T(8,128)S(1)}, u32[]{:S(2)}, u32[]{:S(2)}) %all-to-all-start) | async-done | bytes 196640 | tf_op jit(solution)/shard_map/all_to_all | solution.py:675
  15.9 0.0 copy-start
  15.9 0.7 %copy-done = f32[8,48,128]{2,1,0:T(8,128)} copy-done((f32[8,48,128]{2,1,0:T(8,128)}, f32[8,48,128]{2,1,0:T(8,128)S(1)}, u32[]{:S(2)}) %copy-start) | copy-done | bytes 196632
  16.6 2.9 %shard_map.88 = (f32[2,32,256]{2,1,0:T(8,128)}, f32[16,16,128]{2,1,0:T(8,128)}) custom-call(s32[2,64]{1,0:T(2,128)} %slots_hbm.3, f32[8,48,128]{2,1,0:T(8,128)} %copy-done, bf16[64,128,128]{2,1,0:T(8,128)(2,1)} %weights_hbm.3), custom_call_target="tpu_custom_call" | custom-call | flops 1228800 | bytes 307200 | tf_op jit(solution)/shard_map/pallas_call | solution.py:605
  19.5 0.0 collective-permute-done.one_hbm
  19.5 0.0 copy-start.1
  19.5 0.0 collective-permute-done.1.two_hbm
  19.6 0.0 copy-start.2
  19.6 0.6 %copy-done.1 = f32[34,4,256]{2,1,0:T(4,128)} copy-done((f32[34,4,256]{2,1,0:T(4,128)}, f32[34,4,256]{2,1,0:T(4,128)S(1)}, u32[]{:S(2)}) %copy-start.1) | copy-done | bytes 139288
  20.2 0.1 copy-done.2
  20.3 2.4 %shard_map.89 = (f32[9,40,384]{2,1,0:T(8,128)}, f32[40,384]{1,0:T(8,128)}, f32[40,384]{1,0:T(8,128)}, f32[2,40,128]{2,1,0:T(8,128)}) custom-call(f32[8,48,128]{2,1,0:T(8,128)} %copy-done, f32[32,32,256]{2,1,0:T(8,128)} %temp_hbm.7, s32[32,256]{1,0:T(8,128)} %bathy_hbm.3, f32[32,256]{1,0:T(8,128)} %mixing_hbm.3, f32[34,4,256]{2,1,0:T(4,128)} %copy-done.1, ...), custom_call_target="tpu_custom_call" | custom-call | flops 307200 | bytes 76800 | tf_op jit(solution)/shard_map/pallas_call | solution.py:605
  22.7 2.9 %collective-permute-start.2 = (f32[9,40,384]{2,1,0:T(8,128)}, f32[9,40,384]{2,1,0:T(8,128)S(1)}, u32[]{:S(2)}, u32[]{:S(2)}) collective-permute-start(f32[9,40,384]{2,1,0:T(8,128)} %get-tuple-element.20), channel_id=1, source_target_pairs={{0,1},{1,0},{2,3},{3,2},{4,5},{5,4},{6,7},{7,6},{8,9},{9,8},{10,11... | collective-permute-start | bytes 1658888 | tf_op jit(solution)/shard_map/ppermute | solution.py:705
  25.6 3.5 %all-to-all-start.1 = ((f32[16,16,128]{2,1,0:T(8,128)}), f32[16,16,128]{2,1,0:T(8,128)S(1)}, u32[]{:S(2)}, u32[]{:S(2)}) async-start(f32[16,16,128]{2,1,0:T(8,128)} %get-tuple-element.25), calls=%async_computation.1 | async-start | bytes 262144 | tf_op jit(solution)/shard_map/all_to_all | solution.py:707
  29.1 0.2 collective-permute-start.3
  29.2 0.0 collective-permute-done.2.other_hbm
  29.2 0.0 copy-start.3
  29.2 0.8 %copy-done.3 = f32[9,40,384]{2,1,0:T(8,128)} copy-done((f32[9,40,384]{2,1,0:T(8,128)}, f32[9,40,384]{2,1,0:T(8,128)S(1)}, u32[]{:S(2)}) %copy-start.3) | copy-done | bytes 552984
  30.0 6.1 %shard_map.90 = (f32[40,40,384]{2,1,0:T(8,128)}, f32[40,40,384]{2,1,0:T(8,128)}, f32[4,40,384]{2,1,0:T(8,128)}, f32[4,40,384]{2,1,0:T(8,128)}) custom-call(f32[32,32,256]{2,1,0:T(8,128)} %temp_hbm.7, f32[34,4,256]{2,1,0:T(4,128)} %copy-done.1, f32[34,4,256]{2,1,0:T(4,128)} %copy-done.2, f32[2,40,128]{2,1,0:T(8,128)} %get-tuple-element.19.packed_hbm, ...), custom_call_target="tpu_custom_call" | custom-call | flops 307200 | bytes 76800 | tf_op jit(solution)/shard_map/pallas_call | solution.py:605
  36.1 0.0 collective-permute-done.3.other_hbm
  36.1 0.0 copy-start.5
  36.1 0.0 all-to-all-done.1.edges_hbm
  36.1 0.0 copy-start.4
  36.1 0.6 %copy-done.5 = f32[2,32,256]{2,1,0:T(8,128)} copy-done((f32[2,32,256]{2,1,0:T(8,128)}, f32[2,32,256]{2,1,0:T(8,128)S(1)}, u32[]{:S(2)}) %copy-start.5) | copy-done | bytes 65560
  36.7 0.1 copy-done.4
  36.8 4.2 %shard_map.91 = (f32[2,40,384]{2,1,0:T(8,128)}, f32[16,8,128]{2,1,0:T(8,128)}) custom-call(s32[8,8]{1,0:T(8,128)} %bitcast.2, s32[2,64]{1,0:T(2,128)} %slots_hbm.3, f32[2,32,256]{2,1,0:T(8,128)} %get-tuple-element.18.after_ref.partial_hbm, f32[2,32,256]{2,1,0:T(8,128)} %copy-done.5, f32[16,16,128]{2,1,0:T(8,128)} %copy-done.4, ...), custom_call_target="tpu_custom_call" | custom-call | flops 6144000 | bytes 1536000 | tf_op jit(solution)/shard_map/pallas_call | solution.py:605
  41.0 6.0 %all-to-all-start.2 = ((f32[16,8,128]{2,1,0:T(8,128)}), f32[16,8,128]{2,1,0:T(8,128)S(1)}, u32[]{:S(2)}, u32[]{:S(2)}) async-start(f32[16,8,128]{2,1,0:T(8,128)} %get-tuple-element.29), calls=%async_computation.2 | async-start | bytes 131072 | tf_op jit(solution)/shard_map/all_to_all | solution.py:742
  47.0 8.0 %shard_map.92 = f32[32,32,256]{2,1,0:T(8,128)} custom-call(f32[32,32,256]{2,1,0:T(8,128)} %temp_hbm.7, f32[40,40,384]{2,1,0:T(8,128)} %get-tuple-element.23.moved_hbm, f32[40,40,384]{2,1,0:T(8,128)} %get-tuple-element.24.keep_hbm, f32[40,384]{1,0:T(8,128)} %get-tuple-element.21.levels_hbm, f32[40,384]{1,0:T(8,128)} %get-tuple-element.22.mix_hbm, ...), custom_call_target="tpu_custom_call" | custom-call | flops 36864000 | bytes 9216000 | tf_op jit(solution)/shard_map/pallas_call | solution.py:605
  55.0 0.0 all-to-all-done.2
  55.0 0.6 %reduce_sum.9 = f32[8,128]{1,0:T(8,128)} reduce(f32[16,8,128]{2,1,0:T(8,128)S(1)} %all-to-all-done.2, f32[]{:T(128)} %constant.0.clone.1), dimensions={0}, to_apply=%region_0.0 | reduce | flops 15360 | bytes 69636 | tf_op jit(solution)/shard_map/reduce_sum | solution.py:751
Async XLA Ops:
  2.8 13.1 %all-to-all-start = ((f32[8,48,128]{2,1,0:T(8,128)}), f32[8,48,128]{2,1,0:T(8,128)S(1)}, u32[]{:S(2)}, u32[]{:S(2)}) async-start(f32[8,48,128]{2,1,0:T(8,128)} %shard_map.87), calls=%async_computation | async-start | bytes 393216 | tf_op jit(solution)/shard_map/all_to_all | solution.py:675
  11.1 8.4 %collective-permute-start = (f32[34,4,256]{2,1,0:T(4,128)}, f32[34,4,256]{2,1,0:T(4,128)S(1)}, u32[]{:S(2)}, u32[]{:S(2)}) collective-permute-start(f32[34,4,256]{2,1,0:T(4,128)} %get-tuple-element.16), channel_id=1, source_target_pairs={{0,4},{4,0},{8,12},{12,8},{1,5},{5,1},{9,13},{13,9},{2,6},{6,2},{1... | collective-permute-start | bytes 417800 | tf_op jit(solution)/shard_map/ppermute | solution.py:659
  12.6 6.9 %collective-permute-start.1 = (f32[34,4,256]{2,1,0:T(4,128)}, f32[34,4,256]{2,1,0:T(4,128)S(1)}, u32[]{:S(2)}, u32[]{:S(2)}) collective-permute-start(f32[34,4,256]{2,1,0:T(4,128)} %get-tuple-element.17), channel_id=1, source_target_pairs={{4,8},{8,4},{5,9},{9,5},{6,10},{10,6},{7,11},{11,7},{20,24},{24,20... | collective-permute-start | bytes 417800 | tf_op jit(solution)/shard_map/ppermute | solution.py:659
  15.9 0.7 %copy-start = (f32[8,48,128]{2,1,0:T(8,128)}, f32[8,48,128]{2,1,0:T(8,128)S(1)}, u32[]{:S(2)}) copy-start(f32[8,48,128]{2,1,0:T(8,128)S(1)} %all-to-all-done.flux_hbm.sides_hbm) | copy-start | bytes 589828
  19.5 0.7 %copy-start.1 = (f32[34,4,256]{2,1,0:T(4,128)}, f32[34,4,256]{2,1,0:T(4,128)S(1)}, u32[]{:S(2)}) copy-start(f32[34,4,256]{2,1,0:T(4,128)S(1)} %collective-permute-done.one_hbm) | copy-start | bytes 417796
  19.6 0.7 %copy-start.2 = (f32[34,4,256]{2,1,0:T(4,128)}, f32[34,4,256]{2,1,0:T(4,128)S(1)}, u32[]{:S(2)}) copy-start(f32[34,4,256]{2,1,0:T(4,128)S(1)} %collective-permute-done.1.two_hbm) | copy-start | bytes 417796
  22.7 6.6 %collective-permute-start.2 = (f32[9,40,384]{2,1,0:T(8,128)}, f32[9,40,384]{2,1,0:T(8,128)S(1)}, u32[]{:S(2)}, u32[]{:S(2)}) collective-permute-start(f32[9,40,384]{2,1,0:T(8,128)} %get-tuple-element.20), channel_id=1, source_target_pairs={{0,1},{1,0},{2,3},{3,2},{4,5},{5,4},{6,7},{7,6},{8,9},{9,8},{10,11... | collective-permute-start | bytes 1658888 | tf_op jit(solution)/shard_map/ppermute | solution.py:705
  25.6 10.5 %all-to-all-start.1 = ((f32[16,16,128]{2,1,0:T(8,128)}), f32[16,16,128]{2,1,0:T(8,128)S(1)}, u32[]{:S(2)}, u32[]{:S(2)}) async-start(f32[16,16,128]{2,1,0:T(8,128)} %get-tuple-element.25), calls=%async_computation.1 | async-start | bytes 262144 | tf_op jit(solution)/shard_map/all_to_all | solution.py:707
  29.1 7.0 %collective-permute-start.3 = (f32[2,32,256]{2,1,0:T(8,128)}, f32[2,32,256]{2,1,0:T(8,128)S(1)}, u32[]{:S(2)}, u32[]{:S(2)}) collective-permute-start(f32[2,32,256]{2,1,0:T(8,128)} %get-tuple-element.18.after_ref.partial_hbm), channel_id=1, source_target_pairs={{0,1},{1,0},{2,3},{3,2},{4,5},{5,4},{6,7},{7,6},{8,9},{9,8},{10,11... | collective-permute-start | bytes 196616 | tf_op jit(solution)/shard_map/ppermute | solution.py:704
  29.2 0.8 %copy-start.3 = (f32[9,40,384]{2,1,0:T(8,128)}, f32[9,40,384]{2,1,0:T(8,128)S(1)}, u32[]{:S(2)}) copy-start(f32[9,40,384]{2,1,0:T(8,128)S(1)} %collective-permute-done.2.other_hbm) | copy-start | bytes 1658884
  36.1 0.6 %copy-start.5 = (f32[2,32,256]{2,1,0:T(8,128)}, f32[2,32,256]{2,1,0:T(8,128)S(1)}, u32[]{:S(2)}) copy-start(f32[2,32,256]{2,1,0:T(8,128)S(1)} %collective-permute-done.3.other_hbm) | copy-start | bytes 196612
  36.1 0.7 %copy-start.4 = (f32[16,16,128]{2,1,0:T(8,128)}, f32[16,16,128]{2,1,0:T(8,128)S(1)}, u32[]{:S(2)}) copy-start(f32[16,16,128]{2,1,0:T(8,128)S(1)} %all-to-all-done.1.edges_hbm) | copy-start | bytes 393220
  41.0 14.0 %all-to-all-start.2 = ((f32[16,8,128]{2,1,0:T(8,128)}), f32[16,8,128]{2,1,0:T(8,128)S(1)}, u32[]{:S(2)}, u32[]{:S(2)}) async-start(f32[16,8,128]{2,1,0:T(8,128)} %get-tuple-element.29), calls=%async_computation.2 | async-start | bytes 131072 | tf_op jit(solution)/shard_map/all_to_all | solution.py:742

commit v6 on v5

--- a/solution.py
+++ b/solution.py
@@ -65,13 +65,37 @@
     return jnp.where(levels > level, new, 0.0)
 
 
-def last_slab(center, over, under, keep, mixing, forcing):
-    rows, columns = over.shape
-    tall, lanes = center.shape
-    own = slice(0, rows), slice(0, columns)
-    lateral = pltpu.roll(center, 1, 0)[own] + pltpu.roll(center, tall - 1, 0)[own]
-    lateral = lateral + (pltpu.roll(center[0:rows], 1, 1)[own] + pltpu.roll(center[0:rows], lanes - 1, 1)[own])
-    return center[own] * keep + 0.1 * (lateral + forcing) + mixing * (over + under)
+def march(source, store, keep_ref, mix_ref, levels_ref, start, count, level_of, surface_ref, shares, size, done):
+    tall, lanes = levels_ref.shape
+    rows, columns = size
+    row = lax.broadcasted_iota(jnp.int32, (TILE, lanes), 0)[:, 0:columns]
+    tiles = tall // TILE
+    for tile in range(rows // TILE):
+        here, above, below = (
+            slice(TILE * (place % tiles), TILE * (place % tiles) + TILE) for place in (tile, tile - 1, tile + 1)
+        )
+        own = here, slice(0, columns)
+        mixing, levels = mix_ref[own], levels_ref[own]
+        surface = None if surface_ref is None else surface_ref[(1,) + own]
+        over, wide = source[(start - 1,) + own], source[start, here]
+        for offset in range(count):
+            place = start + offset
+            level = level_of(place)
+            below_wide = source[place + 1, here]
+            center, under = wide[:, 0:columns], below_wide[:, 0:columns]
+            up = jnp.where(row == 0, pltpu.roll(source[(place, above, own[1])], 1, 0), pltpu.roll(center, 1, 0))
+            down = jnp.where(
+                row == TILE - 1, pltpu.roll(source[(place, below, own[1])], TILE - 1, 0),
+                pltpu.roll(center, TILE - 1, 0),
+            )
+            side = pltpu.roll(wide, 1, 1)[:, 0:columns] + pltpu.roll(wide, lanes - 1, 1)[:, 0:columns]
+            lateral = (up + down) + side
+            if surface is not None:
+                lateral = lateral + shares[offset] * surface
+            new = center * keep_ref[(place,) + own] + 0.1 * lateral + mixing * (over + under)
+            store(place, own, levels > level, new)
+            over, wide = center, below_wide
+        done(tile, own)
 
 
 def depth_share(level, total_levels):
@@ -312,7 +336,7 @@
     first_level = gz * layers - HALO
     needed = begin([
         (one_hbm, pair_ref.at[0]), (two_hbm, pair_ref.at[1]), (packed_hbm, packed_ref), (levels_hbm, levels_ref),
-        (mix_hbm, mix_ref), (other_hbm, other_ref),
+        (mix_hbm, mix_ref),
     ], semaphores)
     chunk = layers // CHUNKS
     parts = [pl.ds(part * chunk, chunk) for part in range(CHUNKS)]
@@ -321,6 +345,8 @@
     used += CHUNKS
     odd = lax.rem(lax.axis_index("gx"), 2)
     next_ref, prev_ref = pair_ref.at[odd], pair_ref.at[1 - odd]
+    others = begin([(other_hbm, other_ref)], semaphores, used)
+    used += 1
     finish(needed)
     tall, lanes = levels_ref.shape
     for side, (shift, dim) in enumerate(((1, 0), (tall - 1, 0), (1, 1), (lanes - 1, 1))):
@@ -343,6 +369,7 @@
         arriving[part].wait()
         in_order(part * chunk, chunk, own_level)
 
+    finish(others)
     for index in range(HALO):
         slot = jnp.where(gz == 0, index, TOP + index)
         place = jnp.where(gz == 0, HALO + layers + index, index)
@@ -369,17 +396,17 @@
     edge = jnp.where(gz == 0, HALO - 1, HALO + layers)
     first_ref[edge] = jnp.zeros_like(first_ref[0])
 
-    def one(place):
-        moved_ref[place] = step_slab(
-            first_ref[place], first_ref[place - 1], first_ref[place + 1], keep_ref[place], mix_ref[...],
-            levels_ref[...], level_of(place), None,
-        )
-
-    for start, size in pieces(count):
-        in_order(base + start, size, one)
-        here = pl.ds(base + start, size)
-        leaving += begin([(moved_ref.at[here], moved_hbm.at[here])], semaphores, used)
-        used += 1
+    def store(place, own, wet, new):
+        moved_ref[(place,) + own] = jnp.where(wet, new, 0.0)
+
+    def done(tile, own):
+        leaving.extend(begin([
+            (moved_ref.at[span, pl.ds(TILE * tile, TILE)], moved_hbm.at[span, pl.ds(TILE * tile, TILE)])
+        ], semaphores, used + tile))
+
+    march(
+        first_ref, store, keep_ref, mix_ref, levels_ref, base, count, level_of, None, None, levels_ref.shape, done
+    )
     finish(leaving)
 
 
@@ -529,7 +556,7 @@
     finish(needed)
 
     def level_of(place):
-        return (first_level + place).astype(jnp.float32)
+        return jnp.asarray(first_level + place).astype(jnp.float32)
 
     def add(place):
         level = level_of(place)
@@ -548,48 +575,49 @@
         first_ref[HALO] = first_ref[HALO] + top_forcing()
 
     later[0].wait()
+    leaving = []
     source, target = first_ref, second_ref
     for step in range(2, STEPS + 1):
-        if step == STEPS:
+        start = jnp.where(gz == 0, HALO, step)
+        size = levels_ref.shape
+        shares = [
+            depth_share(level_of(start + offset), total_levels) for offset in range(layers + HALO - step)
+        ]
+        if step < STEPS:
+            def store(place, own, wet, new, target=target):
+                target[(place,) + own] = jnp.where(wet, new, 0.0)
+
+            def done(tile, own, target=target):
+                @pl.when(gz == 0)
+                def _():
+                    target[(HALO,) + own] = target[(HALO,) + own] + jnp.where(
+                        levels_ref[own] > 0.0, 0.1 * surface_ref[(0,) + own], 0.0
+                    )
+        else:
             later[1].wait()
-
-        def one(place, source=source, target=target, step=step):
-            level = level_of(place)
-            share = depth_share(level, total_levels)
-            if step < STEPS:
-                target[place] = step_slab(
-                    source[place], source[place - 1], source[place + 1], keep_ref[place], mix_ref[...],
-                    levels_ref[...], level, share * surface_ref[1],
+            start, size = HALO, (rows, columns)
+
+            def store(place, own, wet, new):
+                temp_ref[(place - HALO,) + own] = jnp.where(wet, new, temp_ref[(place - HALO,) + own])
+
+            def done(tile, own):
+                @pl.when(gz == 0)
+                def _():
+                    temp_ref[(0,) + own] = temp_ref[(0,) + own] + jnp.where(
+                        levels_ref[own] > 0.0, 0.1 * surface_ref[(0,) + own], 0.0
+                    )
+
+                part = pl.ds(TILE * tile, TILE)
+                leaving.extend(
+                    begin([(temp_ref.at[:, part], ocean_hbm.at[:, part])], semaphores, used + tile)
                 )
-            else:
-                own = slice(0, rows), slice(0, columns)
-                new = last_slab(
-                    source[place], source[(place - 1,) + own], source[(place + 1,) + own], keep_ref[(place,) + own],
-                    mix_ref[own], share * surface_ref[(1,) + own],
-                )
-                index = place - HALO
-                temp_ref[index] = jnp.where(levels_ref[own] > level, new, temp_ref[index])
-
-        if step < STEPS:
-            in_order(jnp.where(gz == 0, HALO, step), layers + HALO - step, one)
-
-            @pl.when(gz == 0)
-            def _(target=target):
-                target[HALO] = target[HALO] + top_forcing()
-        else:
-            leaving = []
-            for start, size in pieces(layers):
-                in_order(HALO + start, size, one)
-                if start == 0:
-                    @pl.when(gz == 0)
-                    def _():
-                        temp_ref[0] = temp_ref[0] + top_forcing()[0:rows, 0:columns]
-
-                here = pl.ds(start, size)
-                leaving += begin([(temp_ref.at[here], ocean_hbm.at[here])], semaphores, used)
-                used += 1
-            finish(leaving)
+
+        march(
+            source, store, keep_ref, mix_ref, levels_ref, start, layers + HALO - step, level_of, surface_ref, shares,
+            size, done,
+        )
         source, target = target, source
+    finish(leaving)
 
 
 def call(body, outs, scratch, operands, places, out_places, cost=0):

time: 56.2 us -> 55.9 us (level)
  transfers between devices with their start and end apart: 7 -> 7, of which waited for: 1 -> 2; matrix products, arithmetic and copies ran while one was open for 0% -> 0% of each run, Pallas kernels for 34% -> 34%
where the time goes in v6:
time: 55.9 us; the launch traced here: 55.4 us
  Pallas kernels  27.4 us (49%)
  starting transfers between devices  21.1 us (38%)
  local copies, waits for them, and re-layouts  2.85 us (5%)
  waiting for transfers between devices  2.71 us (5%)
  between operations  0.76 us (1%)
  other arithmetic  0.61 us (1%)
    pallas_call x7, Pallas kernels, call(): pl.pallas_call(body, out_shape=[jax.ShapeDtypeStruct(out, jnp.float32) fo...  27.4 us
    all_to_all x1, starting transfers between devices, per_device(): lax.all_to_all(sent[0], BLOCKS_AXES, split_axis=0, concat_axis=0, tiled=T...  6.37 us
    all_to_all x1, starting transfers between devices, per_device(): lax.all_to_all(back, ALL_AXES, split_axis=0, concat_axis=0, tiled=True)  5.94 us
    all_to_all x1, starting transfers between devices, per_device(): lax.all_to_all(edges, ALL_AXES, split_axis=0, concat_axis=0, tiled=True)  3.47 us
    ppermute x1, starting transfers between devices, per_device(): other_shared = lax.ppermute(shared, 'gz', swap)  2.94 us
    unnamed x12, local copies, waits for them, and re-layouts  2.85 us
    all_to_all x1, waiting for transfers between devices, per_device(): lax.all_to_all(sent[0], BLOCKS_AXES, split_axis=0, concat_axis=0, tiled=T...  2.61 us
    ppermute x2, starting transfers between devices, per_device(): lax.ppermute(part, 'gx', [pair for x in range(start, gx_count - 1, 2) for...  2.18 us
  transfers between devices with their start and end apart: 7, of which 2 were waited for; matrix products, arithmetic and copies ran while one was open for 0% of the time, Pallas kernels for 34%

profile of v6, /device:TPU:1, one launch (start us, length us, event | category | flops | bytes accessed | tf_op | source)
XLA Modules:
  0.0 55.4 jit_solution(8023722685967243574)
XLA Ops:
  0.6 2.2 %shard_map.87 = f32[8,48,128]{2,1,0:T(8,128)} custom-call(s32[8,8]{1,0:T(8,128)} %bitcast.1, bf16[8,2,128]{2,1,0:T(2,128)(2,1)} %flux_hbm.1, f32[32,32,256]{2,1,0:T(8,128)} %temp_hbm.7, s32[32,256]{1,0:T(8,128)} %bathy_hbm.3, f32[32,256]{1,0:T(8,128)} %mixing_hbm.3), custom_call_target="tpu_custom_call" | custom-call | flops 614400 | bytes 153600 | tf_op jit(solution)/shard_map/pallas_call | solution.py:633
  2.8 6.4 %all-to-all-start = ((f32[8,48,128]{2,1,0:T(8,128)}), f32[8,48,128]{2,1,0:T(8,128)S(1)}, u32[]{:S(2)}, u32[]{:S(2)}) async-start(f32[8,48,128]{2,1,0:T(8,128)} %shard_map.87), calls=%async_computation | async-start | bytes 393216 | tf_op jit(solution)/shard_map/all_to_all | solution.py:703
  9.2 1.9 %shard_map.86 = (f32[34,4,256]{2,1,0:T(4,128)}, f32[34,4,256]{2,1,0:T(4,128)}) custom-call(f32[32,32,256]{2,1,0:T(8,128)} %temp_hbm.7, s32[32,256]{1,0:T(8,128)} %bathy_hbm.3, f32[32,256]{1,0:T(8,128)} %mixing_hbm.3), custom_call_target="tpu_custom_call" | custom-call | flops 307200 | bytes 76800 | tf_op jit(solution)/shard_map/pallas_call | solution.py:633
  11.1 1.5 %collective-permute-start = (f32[34,4,256]{2,1,0:T(4,128)}, f32[34,4,256]{2,1,0:T(4,128)S(1)}, u32[]{:S(2)}, u32[]{:S(2)}) collective-permute-start(f32[34,4,256]{2,1,0:T(4,128)} %get-tuple-element.16), channel_id=1, source_target_pairs={{0,4},{4,0},{8,12},{12,8},{1,5},{5,1},{9,13},{13,9},{2,6},{6,2},{1... | collective-permute-start | bytes 417800 | tf_op jit(solution)/shard_map/ppermute | solution.py:687
  12.6 0.7 %collective-permute-start.1 = (f32[34,4,256]{2,1,0:T(4,128)}, f32[34,4,256]{2,1,0:T(4,128)S(1)}, u32[]{:S(2)}, u32[]{:S(2)}) collective-permute-start(f32[34,4,256]{2,1,0:T(4,128)} %get-tuple-element.17), channel_id=1, source_target_pairs={{4,8},{8,4},{5,9},{9,5},{6,10},{10,6},{7,11},{11,7},{20,24},{24,20... | collective-permute-start | bytes 417800 | tf_op jit(solution)/shard_map/ppermute | solution.py:687
  13.3 2.6 %all-to-all-done.flux_hbm.sides_hbm = f32[8,48,128]{2,1,0:T(8,128)S(1)} async-done(((f32[8,48,128]{2,1,0:T(8,128)}), f32[8,48,128]{2,1,0:T(8,128)S(1)}, u32[]{:S(2)}, u32[]{:S(2)}) %all-to-all-start) | async-done | bytes 196640 | tf_op jit(solution)/shard_map/all_to_all | solution.py:703
  15.9 0.0 copy-start
  15.9 0.7 %copy-done = f32[8,48,128]{2,1,0:T(8,128)} copy-done((f32[8,48,128]{2,1,0:T(8,128)}, f32[8,48,128]{2,1,0:T(8,128)S(1)}, u32[]{:S(2)}) %copy-start) | copy-done | bytes 196632
  16.6 2.9 %shard_map.88 = (f32[2,32,256]{2,1,0:T(8,128)}, f32[16,16,128]{2,1,0:T(8,128)}) custom-call(s32[2,64]{1,0:T(2,128)} %slots_hbm.3, f32[8,48,128]{2,1,0:T(8,128)} %copy-done, bf16[64,128,128]{2,1,0:T(8,128)(2,1)} %weights_hbm.3), custom_call_target="tpu_custom_call" | custom-call | flops 1228800 | bytes 307200 | tf_op jit(solution)/shard_map/pallas_call | solution.py:633
  19.5 0.0 collective-permute-done.one_hbm
  19.5 0.0 copy-start.1
  19.5 0.0 collective-permute-done.1.two_hbm
  19.5 0.0 copy-start.2
  19.6 0.6 %copy-done.1 = f32[34,4,256]{2,1,0:T(4,128)} copy-done((f32[34,4,256]{2,1,0:T(4,128)}, f32[34,4,256]{2,1,0:T(4,128)S(1)}, u32[]{:S(2)}) %copy-start.1) | copy-done | bytes 139288
  20.2 0.1 copy-done.2
  20.3 2.4 %shard_map.89 = (f32[9,40,384]{2,1,0:T(8,128)}, f32[40,384]{1,0:T(8,128)}, f32[40,384]{1,0:T(8,128)}, f32[2,40,128]{2,1,0:T(8,128)}) custom-call(f32[8,48,128]{2,1,0:T(8,128)} %copy-done, f32[32,32,256]{2,1,0:T(8,128)} %temp_hbm.7, s32[32,256]{1,0:T(8,128)} %bathy_hbm.3, f32[32,256]{1,0:T(8,128)} %mixing_hbm.3, f32[34,4,256]{2,1,0:T(4,128)} %copy-done.1, ...), custom_call_target="tpu_custom_call" | custom-call | flops 307200 | bytes 76800 | tf_op jit(solution)/shard_map/pallas_call | solution.py:633
  22.6 2.9 %collective-permute-start.2 = (f32[9,40,384]{2,1,0:T(8,128)}, f32[9,40,384]{2,1,0:T(8,128)S(1)}, u32[]{:S(2)}, u32[]{:S(2)}) collective-permute-start(f32[9,40,384]{2,1,0:T(8,128)} %get-tuple-element.20), channel_id=1, source_target_pairs={{0,1},{1,0},{2,3},{3,2},{4,5},{5,4},{6,7},{7,6},{8,9},{9,8},{10,11... | collective-permute-start | bytes 1658888 | tf_op jit(solution)/shard_map/ppermute | solution.py:733
  25.6 3.5 %all-to-all-start.1 = ((f32[16,16,128]{2,1,0:T(8,128)}), f32[16,16,128]{2,1,0:T(8,128)S(1)}, u32[]{:S(2)}, u32[]{:S(2)}) async-start(f32[16,16,128]{2,1,0:T(8,128)} %get-tuple-element.25), calls=%async_computation.1 | async-start | bytes 262144 | tf_op jit(solution)/shard_map/all_to_all | solution.py:735
  29.1 0.2 collective-permute-start.3
  29.2 0.0 collective-permute-done.2.other_hbm
  29.2 0.0 copy-start.3
  29.2 0.8 %copy-done.3 = f32[9,40,384]{2,1,0:T(8,128)} copy-done((f32[9,40,384]{2,1,0:T(8,128)}, f32[9,40,384]{2,1,0:T(8,128)S(1)}, u32[]{:S(2)}) %copy-start.3) | copy-done | bytes 552984
  30.0 5.8 %shard_map.90 = (f32[40,40,384]{2,1,0:T(8,128)}, f32[40,40,384]{2,1,0:T(8,128)}, f32[4,40,384]{2,1,0:T(8,128)}, f32[4,40,384]{2,1,0:T(8,128)}) custom-call(f32[32,32,256]{2,1,0:T(8,128)} %temp_hbm.7, f32[34,4,256]{2,1,0:T(4,128)} %copy-done.1, f32[34,4,256]{2,1,0:T(4,128)} %copy-done.2, f32[2,40,128]{2,1,0:T(8,128)} %get-tuple-element.19.packed_hbm, ...), custom_call_target="tpu_custom_call" | custom-call | flops 307200 | bytes 76800 | tf_op jit(solution)/shard_map/pallas_call | solution.py:633
  35.8 0.0 collective-permute-done.3.other_hbm
  35.8 0.0 copy-start.5
  35.8 0.1 all-to-all-done.1.edges_hbm
  35.9 0.0 copy-start.4
  35.9 0.5 copy-done.5
  36.5 0.1 copy-done.4
  36.6 4.2 %shard_map.91 = (f32[2,40,384]{2,1,0:T(8,128)}, f32[16,8,128]{2,1,0:T(8,128)}) custom-call(s32[8,8]{1,0:T(8,128)} %bitcast.2, s32[2,64]{1,0:T(2,128)} %slots_hbm.3, f32[2,32,256]{2,1,0:T(8,128)} %get-tuple-element.18.after_ref.partial_hbm, f32[2,32,256]{2,1,0:T(8,128)} %copy-done.5, f32[16,16,128]{2,1,0:T(8,128)} %copy-done.4, ...), custom_call_target="tpu_custom_call" | custom-call | flops 6144000 | bytes 1536000 | tf_op jit(solution)/shard_map/pallas_call | solution.py:633
  40.8 5.9 %all-to-all-start.2 = ((f32[16,8,128]{2,1,0:T(8,128)}), f32[16,8,128]{2,1,0:T(8,128)S(1)}, u32[]{:S(2)}, u32[]{:S(2)}) async-start(f32[16,8,128]{2,1,0:T(8,128)} %get-tuple-element.29), calls=%async_computation.2 | async-start | bytes 131072 | tf_op jit(solution)/shard_map/all_to_all | solution.py:770
  46.8 8.0 %shard_map.92 = f32[32,32,256]{2,1,0:T(8,128)} custom-call(f32[32,32,256]{2,1,0:T(8,128)} %temp_hbm.7, f32[40,40,384]{2,1,0:T(8,128)} %get-tuple-element.23.moved_hbm, f32[40,40,384]{2,1,0:T(8,128)} %get-tuple-element.24.keep_hbm, f32[40,384]{1,0:T(8,128)} %get-tuple-element.21.levels_hbm, f32[40,384]{1,0:T(8,128)} %get-tuple-element.22.mix_hbm, ...), custom_call_target="tpu_custom_call" | custom-call | flops 36864000 | bytes 9216000 | tf_op jit(solution)/shard_map/pallas_call | solution.py:633
  54.8 0.0 all-to-all-done.2
  54.8 0.6 %reduce_sum.9 = f32[8,128]{1,0:T(8,128)} reduce(f32[16,8,128]{2,1,0:T(8,128)S(1)} %all-to-all-done.2, f32[]{:T(128)} %constant.0.clone.1), dimensions={0}, to_apply=%region_0.0 | reduce | flops 15360 | bytes 69636 | tf_op jit(solution)/shard_map/reduce_sum | solution.py:779
Async XLA Ops:
  2.8 13.1 %all-to-all-start = ((f32[8,48,128]{2,1,0:T(8,128)}), f32[8,48,128]{2,1,0:T(8,128)S(1)}, u32[]{:S(2)}, u32[]{:S(2)}) async-start(f32[8,48,128]{2,1,0:T(8,128)} %shard_map.87), calls=%async_computation | async-start | bytes 393216 | tf_op jit(solution)/shard_map/all_to_all | solution.py:703
  11.1 8.4 %collective-permute-start = (f32[34,4,256]{2,1,0:T(4,128)}, f32[34,4,256]{2,1,0:T(4,128)S(1)}, u32[]{:S(2)}, u32[]{:S(2)}) collective-permute-start(f32[34,4,256]{2,1,0:T(4,128)} %get-tuple-element.16), channel_id=1, source_target_pairs={{0,4},{4,0},{8,12},{12,8},{1,5},{5,1},{9,13},{13,9},{2,6},{6,2},{1... | collective-permute-start | bytes 417800 | tf_op jit(solution)/shard_map/ppermute | solution.py:687
  12.6 6.9 %collective-permute-start.1 = (f32[34,4,256]{2,1,0:T(4,128)}, f32[34,4,256]{2,1,0:T(4,128)S(1)}, u32[]{:S(2)}, u32[]{:S(2)}) collective-permute-start(f32[34,4,256]{2,1,0:T(4,128)} %get-tuple-element.17), channel_id=1, source_target_pairs={{4,8},{8,4},{5,9},{9,5},{6,10},{10,6},{7,11},{11,7},{20,24},{24,20... | collective-permute-start | bytes 417800 | tf_op jit(solution)/shard_map/ppermute | solution.py:687
  15.9 0.7 %copy-start = (f32[8,48,128]{2,1,0:T(8,128)}, f32[8,48,128]{2,1,0:T(8,128)S(1)}, u32[]{:S(2)}) copy-start(f32[8,48,128]{2,1,0:T(8,128)S(1)} %all-to-all-done.flux_hbm.sides_hbm) | copy-start | bytes 589828
  19.5 0.7 %copy-start.1 = (f32[34,4,256]{2,1,0:T(4,128)}, f32[34,4,256]{2,1,0:T(4,128)S(1)}, u32[]{:S(2)}) copy-start(f32[34,4,256]{2,1,0:T(4,128)S(1)} %collective-permute-done.one_hbm) | copy-start | bytes 417796
  19.5 0.7 %copy-start.2 = (f32[34,4,256]{2,1,0:T(4,128)}, f32[34,4,256]{2,1,0:T(4,128)S(1)}, u32[]{:S(2)}) copy-start(f32[34,4,256]{2,1,0:T(4,128)S(1)} %collective-permute-done.1.two_hbm) | copy-start | bytes 417796
  22.6 6.6 %collective-permute-start.2 = (f32[9,40,384]{2,1,0:T(8,128)}, f32[9,40,384]{2,1,0:T(8,128)S(1)}, u32[]{:S(2)}, u32[]{:S(2)}) collective-permute-start(f32[9,40,384]{2,1,0:T(8,128)} %get-tuple-element.20), channel_id=1, source_target_pairs={{0,1},{1,0},{2,3},{3,2},{4,5},{5,4},{6,7},{7,6},{8,9},{9,8},{10,11... | collective-permute-start | bytes 1658888 | tf_op jit(solution)/shard_map/ppermute | solution.py:733
  25.6 10.3 %all-to-all-start.1 = ((f32[16,16,128]{2,1,0:T(8,128)}), f32[16,16,128]{2,1,0:T(8,128)S(1)}, u32[]{:S(2)}, u32[]{:S(2)}) async-start(f32[16,16,128]{2,1,0:T(8,128)} %get-tuple-element.25), calls=%async_computation.1 | async-start | bytes 262144 | tf_op jit(solution)/shard_map/all_to_all | solution.py:735
  29.1 6.8 %collective-permute-start.3 = (f32[2,32,256]{2,1,0:T(8,128)}, f32[2,32,256]{2,1,0:T(8,128)S(1)}, u32[]{:S(2)}, u32[]{:S(2)}) collective-permute-start(f32[2,32,256]{2,1,0:T(8,128)} %get-tuple-element.18.after_ref.partial_hbm), channel_id=1, source_target_pairs={{0,1},{1,0},{2,3},{3,2},{4,5},{5,4},{6,7},{7,6},{8,9},{9,8},{10,11... | collective-permute-start | bytes 196616 | tf_op jit(solution)/shard_map/ppermute | solution.py:732
  29.2 0.8 %copy-start.3 = (f32[9,40,384]{2,1,0:T(8,128)}, f32[9,40,384]{2,1,0:T(8,128)S(1)}, u32[]{:S(2)}) copy-start(f32[9,40,384]{2,1,0:T(8,128)S(1)} %collective-permute-done.2.other_hbm) | copy-start | bytes 1658884
  35.8 0.6 %copy-start.5 = (f32[2,32,256]{2,1,0:T(8,128)}, f32[2,32,256]{2,1,0:T(8,128)S(1)}, u32[]{:S(2)}) copy-start(f32[2,32,256]{2,1,0:T(8,128)S(1)} %collective-permute-done.3.other_hbm) | copy-start | bytes 196612
  35.9 0.7 %copy-start.4 = (f32[16,16,128]{2,1,0:T(8,128)}, f32[16,16,128]{2,1,0:T(8,128)S(1)}, u32[]{:S(2)}) copy-start(f32[16,16,128]{2,1,0:T(8,128)S(1)} %all-to-all-done.1.edges_hbm) | copy-start | bytes 393220
  40.8 14.0 %all-to-all-start.2 = ((f32[16,8,128]{2,1,0:T(8,128)}), f32[16,8,128]{2,1,0:T(8,128)S(1)}, u32[]{:S(2)}, u32[]{:S(2)}) async-start(f32[16,8,128]{2,1,0:T(8,128)} %get-tuple-element.29), calls=%async_computation.2 | async-start | bytes 131072 | tf_op jit(solution)/shard_map/all_to_all | solution.py:770

commit v7 on v6

--- a/solution.py
+++ b/solution.py
@@ -16,7 +16,7 @@
 GROUP = LANES // HALO
 FEW = 16
 UNROLL = 8
-CHUNKS = 4
+CHUNKS = 2
 BLOCKS_AXES = ("gx", "gy")
 ALL_AXES = ("gx", "gy", "gz")
 VMEM_LIMIT = 60 * 1024 * 1024

time: 55.9 us -> 55.9 us (level)
  transfers between devices with their start and end apart: 7 -> 7, of which waited for: 2 -> 1; matrix products, arithmetic and copies ran while one was open for 0% -> 0% of each run, Pallas kernels for 34% -> 34%
where the time goes in v7:
time: 55.9 us; the launch traced here: 55.4 us
  Pallas kernels  27.4 us (49%)
  starting transfers between devices  21.2 us (38%)
  local copies, waits for them, and re-layouts  2.84 us (5%)
  waiting for transfers between devices  2.63 us (5%)
  between operations  0.77 us (1%)
  other arithmetic  0.61 us (1%)
    pallas_call x7, Pallas kernels, call(): pl.pallas_call(body, out_shape=[jax.ShapeDtypeStruct(out, jnp.float32) fo...  27.4 us
    all_to_all x1, starting transfers between devices, per_device(): lax.all_to_all(sent[0], BLOCKS_AXES, split_axis=0, concat_axis=0, tiled=T...  6.37 us
    all_to_all x1, starting transfers between devices, per_device(): lax.all_to_all(back, ALL_AXES, split_axis=0, concat_axis=0, tiled=True)  6.01 us
    all_to_all x1, starting transfers between devices, per_device(): lax.all_to_all(edges, ALL_AXES, split_axis=0, concat_axis=0, tiled=True)  3.53 us
    ppermute x1, starting transfers between devices, per_device(): other_shared = lax.ppermute(shared, 'gz', swap)  2.94 us
    unnamed x12, local copies, waits for them, and re-layouts  2.84 us
    all_to_all x1, waiting for transfers between devices, per_device(): lax.all_to_all(sent[0], BLOCKS_AXES, split_axis=0, concat_axis=0, tiled=T...  2.61 us
    ppermute x2, starting transfers between devices, per_device(): lax.ppermute(part, 'gx', [pair for x in range(start, gx_count - 1, 2) for...  2.18 us
  transfers between devices with their start and end apart: 7, of which 1 were waited for; matrix products, arithmetic and copies ran while one was open for 0% of the time, Pallas kernels for 34%

profile of v7, /device:TPU:1, one launch (start us, length us, event | category | flops | bytes accessed | tf_op | source)
XLA Modules:
  0.0 55.4 jit_solution(5849223265795013962)
XLA Ops:
  0.6 2.2 %shard_map.87 = f32[8,48,128]{2,1,0:T(8,128)} custom-call(s32[8,8]{1,0:T(8,128)} %bitcast.1, bf16[8,2,128]{2,1,0:T(2,128)(2,1)} %flux_hbm.1, f32[32,32,256]{2,1,0:T(8,128)} %temp_hbm.7, s32[32,256]{1,0:T(8,128)} %bathy_hbm.3, f32[32,256]{1,0:T(8,128)} %mixing_hbm.3), custom_call_target="tpu_custom_call" | custom-call | flops 614400 | bytes 153600 | tf_op jit(solution)/shard_map/pallas_call | solution.py:633
  2.8 6.4 %all-to-all-start = ((f32[8,48,128]{2,1,0:T(8,128)}), f32[8,48,128]{2,1,0:T(8,128)S(1)}, u32[]{:S(2)}, u32[]{:S(2)}) async-start(f32[8,48,128]{2,1,0:T(8,128)} %shard_map.87), calls=%async_computation | async-start | bytes 393216 | tf_op jit(solution)/shard_map/all_to_all | solution.py:703
  9.2 1.9 %shard_map.86 = (f32[34,4,256]{2,1,0:T(4,128)}, f32[34,4,256]{2,1,0:T(4,128)}) custom-call(f32[32,32,256]{2,1,0:T(8,128)} %temp_hbm.7, s32[32,256]{1,0:T(8,128)} %bathy_hbm.3, f32[32,256]{1,0:T(8,128)} %mixing_hbm.3), custom_call_target="tpu_custom_call" | custom-call | flops 307200 | bytes 76800 | tf_op jit(solution)/shard_map/pallas_call | solution.py:633
  11.1 1.5 %collective-permute-start = (f32[34,4,256]{2,1,0:T(4,128)}, f32[34,4,256]{2,1,0:T(4,128)S(1)}, u32[]{:S(2)}, u32[]{:S(2)}) collective-permute-start(f32[34,4,256]{2,1,0:T(4,128)} %get-tuple-element.16), channel_id=1, source_target_pairs={{0,4},{4,0},{8,12},{12,8},{1,5},{5,1},{9,13},{13,9},{2,6},{6,2},{1... | collective-permute-start | bytes 417800 | tf_op jit(solution)/shard_map/ppermute | solution.py:687
  12.6 0.7 %collective-permute-start.1 = (f32[34,4,256]{2,1,0:T(4,128)}, f32[34,4,256]{2,1,0:T(4,128)S(1)}, u32[]{:S(2)}, u32[]{:S(2)}) collective-permute-start(f32[34,4,256]{2,1,0:T(4,128)} %get-tuple-element.17), channel_id=1, source_target_pairs={{4,8},{8,4},{5,9},{9,5},{6,10},{10,6},{7,11},{11,7},{20,24},{24,20... | collective-permute-start | bytes 417800 | tf_op jit(solution)/shard_map/ppermute | solution.py:687
  13.3 2.6 %all-to-all-done.flux_hbm.sides_hbm = f32[8,48,128]{2,1,0:T(8,128)S(1)} async-done(((f32[8,48,128]{2,1,0:T(8,128)}), f32[8,48,128]{2,1,0:T(8,128)S(1)}, u32[]{:S(2)}, u32[]{:S(2)}) %all-to-all-start) | async-done | bytes 196640 | tf_op jit(solution)/shard_map/all_to_all | solution.py:703
  15.9 0.0 copy-start
  15.9 0.7 %copy-done = f32[8,48,128]{2,1,0:T(8,128)} copy-done((f32[8,48,128]{2,1,0:T(8,128)}, f32[8,48,128]{2,1,0:T(8,128)S(1)}, u32[]{:S(2)}) %copy-start) | copy-done | bytes 196632
  16.6 2.9 %shard_map.88 = (f32[2,32,256]{2,1,0:T(8,128)}, f32[16,16,128]{2,1,0:T(8,128)}) custom-call(s32[2,64]{1,0:T(2,128)} %slots_hbm.3, f32[8,48,128]{2,1,0:T(8,128)} %copy-done, bf16[64,128,128]{2,1,0:T(8,128)(2,1)} %weights_hbm.3), custom_call_target="tpu_custom_call" | custom-call | flops 1228800 | bytes 307200 | tf_op jit(solution)/shard_map/pallas_call | solution.py:633
  19.5 0.0 collective-permute-done.one_hbm
  19.5 0.0 copy-start.1
  19.5 0.0 collective-permute-done.1.two_hbm
  19.5 0.0 copy-start.2
  19.5 0.6 %copy-done.1 = f32[34,4,256]{2,1,0:T(4,128)} copy-done((f32[34,4,256]{2,1,0:T(4,128)}, f32[34,4,256]{2,1,0:T(4,128)S(1)}, u32[]{:S(2)}) %copy-start.1) | copy-done | bytes 139288
  20.1 0.1 copy-done.2
  20.2 2.4 %shard_map.89 = (f32[9,40,384]{2,1,0:T(8,128)}, f32[40,384]{1,0:T(8,128)}, f32[40,384]{1,0:T(8,128)}, f32[2,40,128]{2,1,0:T(8,128)}) custom-call(f32[8,48,128]{2,1,0:T(8,128)} %copy-done, f32[32,32,256]{2,1,0:T(8,128)} %temp_hbm.7, s32[32,256]{1,0:T(8,128)} %bathy_hbm.3, f32[32,256]{1,0:T(8,128)} %mixing_hbm.3, f32[34,4,256]{2,1,0:T(4,128)} %copy-done.1, ...), custom_call_target="tpu_custom_call" | custom-call | flops 307200 | bytes 76800 | tf_op jit(solution)/shard_map/pallas_call | solution.py:633
  22.6 2.9 %collective-permute-start.2 = (f32[9,40,384]{2,1,0:T(8,128)}, f32[9,40,384]{2,1,0:T(8,128)S(1)}, u32[]{:S(2)}, u32[]{:S(2)}) collective-permute-start(f32[9,40,384]{2,1,0:T(8,128)} %get-tuple-element.20), channel_id=1, source_target_pairs={{0,1},{1,0},{2,3},{3,2},{4,5},{5,4},{6,7},{7,6},{8,9},{9,8},{10,11... | collective-permute-start | bytes 1658888 | tf_op jit(solution)/shard_map/ppermute | solution.py:733
  25.5 3.5 %all-to-all-start.1 = ((f32[16,16,128]{2,1,0:T(8,128)}), f32[16,16,128]{2,1,0:T(8,128)S(1)}, u32[]{:S(2)}, u32[]{:S(2)}) async-start(f32[16,16,128]{2,1,0:T(8,128)} %get-tuple-element.25), calls=%async_computation.1 | async-start | bytes 262144 | tf_op jit(solution)/shard_map/all_to_all | solution.py:735
  29.1 0.2 collective-permute-start.3
  29.2 0.0 collective-permute-done.2.other_hbm
  29.2 0.0 copy-start.3
  29.2 0.8 %copy-done.3 = f32[9,40,384]{2,1,0:T(8,128)} copy-done((f32[9,40,384]{2,1,0:T(8,128)}, f32[9,40,384]{2,1,0:T(8,128)S(1)}, u32[]{:S(2)}) %copy-start.3) | copy-done | bytes 552984
  30.0 6.0 %shard_map.90 = (f32[40,40,384]{2,1,0:T(8,128)}, f32[40,40,384]{2,1,0:T(8,128)}, f32[4,40,384]{2,1,0:T(8,128)}, f32[4,40,384]{2,1,0:T(8,128)}) custom-call(f32[32,32,256]{2,1,0:T(8,128)} %temp_hbm.7, f32[34,4,256]{2,1,0:T(4,128)} %copy-done.1, f32[34,4,256]{2,1,0:T(4,128)} %copy-done.2, f32[2,40,128]{2,1,0:T(8,128)} %get-tuple-element.19.packed_hbm, ...), custom_call_target="tpu_custom_call" | custom-call | flops 307200 | bytes 76800 | tf_op jit(solution)/shard_map/pallas_call | solution.py:633
  36.1 0.0 collective-permute-done.3.other_hbm
  36.1 0.0 copy-start.5
  36.1 0.0 all-to-all-done.1.edges_hbm
  36.1 0.0 copy-start.4
  36.1 0.6 %copy-done.5 = f32[2,32,256]{2,1,0:T(8,128)} copy-done((f32[2,32,256]{2,1,0:T(8,128)}, f32[2,32,256]{2,1,0:T(8,128)S(1)}, u32[]{:S(2)}) %copy-start.5) | copy-done | bytes 65560
  36.7 0.1 copy-done.4
  36.7 4.0 %shard_map.91 = (f32[2,40,384]{2,1,0:T(8,128)}, f32[16,8,128]{2,1,0:T(8,128)}) custom-call(s32[8,8]{1,0:T(8,128)} %bitcast.2, s32[2,64]{1,0:T(2,128)} %slots_hbm.3, f32[2,32,256]{2,1,0:T(8,128)} %get-tuple-element.18.after_ref.partial_hbm, f32[2,32,256]{2,1,0:T(8,128)} %copy-done.5, f32[16,16,128]{2,1,0:T(8,128)} %copy-done.4, ...), custom_call_target="tpu_custom_call" | custom-call | flops 6144000 | bytes 1536000 | tf_op jit(solution)/shard_map/pallas_call | solution.py:633
  40.7 6.0 %all-to-all-start.2 = ((f32[16,8,128]{2,1,0:T(8,128)}), f32[16,8,128]{2,1,0:T(8,128)S(1)}, u32[]{:S(2)}, u32[]{:S(2)}) async-start(f32[16,8,128]{2,1,0:T(8,128)} %get-tuple-element.29), calls=%async_computation.2 | async-start | bytes 131072 | tf_op jit(solution)/shard_map/all_to_all | solution.py:770
  46.8 8.0 %shard_map.92 = f32[32,32,256]{2,1,0:T(8,128)} custom-call(f32[32,32,256]{2,1,0:T(8,128)} %temp_hbm.7, f32[40,40,384]{2,1,0:T(8,128)} %get-tuple-element.23.moved_hbm, f32[40,40,384]{2,1,0:T(8,128)} %get-tuple-element.24.keep_hbm, f32[40,384]{1,0:T(8,128)} %get-tuple-element.21.levels_hbm, f32[40,384]{1,0:T(8,128)} %get-tuple-element.22.mix_hbm, ...), custom_call_target="tpu_custom_call" | custom-call | flops 36864000 | bytes 9216000 | tf_op jit(solution)/shard_map/pallas_call | solution.py:633
  54.8 0.0 all-to-all-done.2
  54.8 0.6 %reduce_sum.9 = f32[8,128]{1,0:T(8,128)} reduce(f32[16,8,128]{2,1,0:T(8,128)S(1)} %all-to-all-done.2, f32[]{:T(128)} %constant.0.clone.1), dimensions={0}, to_apply=%region_0.0 | reduce | flops 15360 | bytes 69636 | tf_op jit(solution)/shard_map/reduce_sum | solution.py:779
Async XLA Ops:
  2.8 13.1 %all-to-all-start = ((f32[8,48,128]{2,1,0:T(8,128)}), f32[8,48,128]{2,1,0:T(8,128)S(1)}, u32[]{:S(2)}, u32[]{:S(2)}) async-start(f32[8,48,128]{2,1,0:T(8,128)} %shard_map.87), calls=%async_computation | async-start | bytes 393216 | tf_op jit(solution)/shard_map/all_to_all | solution.py:703
  11.1 8.4 %collective-permute-start = (f32[34,4,256]{2,1,0:T(4,128)}, f32[34,4,256]{2,1,0:T(4,128)S(1)}, u32[]{:S(2)}, u32[]{:S(2)}) collective-permute-start(f32[34,4,256]{2,1,0:T(4,128)} %get-tuple-element.16), channel_id=1, source_target_pairs={{0,4},{4,0},{8,12},{12,8},{1,5},{5,1},{9,13},{13,9},{2,6},{6,2},{1... | collective-permute-start | bytes 417800 | tf_op jit(solution)/shard_map/ppermute | solution.py:687
  12.6 6.9 %collective-permute-start.1 = (f32[34,4,256]{2,1,0:T(4,128)}, f32[34,4,256]{2,1,0:T(4,128)S(1)}, u32[]{:S(2)}, u32[]{:S(2)}) collective-permute-start(f32[34,4,256]{2,1,0:T(4,128)} %get-tuple-element.17), channel_id=1, source_target_pairs={{4,8},{8,4},{5,9},{9,5},{6,10},{10,6},{7,11},{11,7},{20,24},{24,20... | collective-permute-start | bytes 417800 | tf_op jit(solution)/shard_map/ppermute | solution.py:687
  15.9 0.7 %copy-start = (f32[8,48,128]{2,1,0:T(8,128)}, f32[8,48,128]{2,1,0:T(8,128)S(1)}, u32[]{:S(2)}) copy-start(f32[8,48,128]{2,1,0:T(8,128)S(1)} %all-to-all-done.flux_hbm.sides_hbm) | copy-start | bytes 589828
  19.5 0.7 %copy-start.1 = (f32[34,4,256]{2,1,0:T(4,128)}, f32[34,4,256]{2,1,0:T(4,128)S(1)}, u32[]{:S(2)}) copy-start(f32[34,4,256]{2,1,0:T(4,128)S(1)} %collective-permute-done.one_hbm) | copy-start | bytes 417796
  19.5 0.7 %copy-start.2 = (f32[34,4,256]{2,1,0:T(4,128)}, f32[34,4,256]{2,1,0:T(4,128)S(1)}, u32[]{:S(2)}) copy-start(f32[34,4,256]{2,1,0:T(4,128)S(1)} %collective-permute-done.1.two_hbm) | copy-start | bytes 417796
  22.6 6.6 %collective-permute-start.2 = (f32[9,40,384]{2,1,0:T(8,128)}, f32[9,40,384]{2,1,0:T(8,128)S(1)}, u32[]{:S(2)}, u32[]{:S(2)}) collective-permute-start(f32[9,40,384]{2,1,0:T(8,128)} %get-tuple-element.20), channel_id=1, source_target_pairs={{0,1},{1,0},{2,3},{3,2},{4,5},{5,4},{6,7},{7,6},{8,9},{9,8},{10,11... | collective-permute-start | bytes 1658888 | tf_op jit(solution)/shard_map/ppermute | solution.py:733
  25.5 10.6 %all-to-all-start.1 = ((f32[16,16,128]{2,1,0:T(8,128)}), f32[16,16,128]{2,1,0:T(8,128)S(1)}, u32[]{:S(2)}, u32[]{:S(2)}) async-start(f32[16,16,128]{2,1,0:T(8,128)} %get-tuple-element.25), calls=%async_computation.1 | async-start | bytes 262144 | tf_op jit(solution)/shard_map/all_to_all | solution.py:735
  29.1 7.0 %collective-permute-start.3 = (f32[2,32,256]{2,1,0:T(8,128)}, f32[2,32,256]{2,1,0:T(8,128)S(1)}, u32[]{:S(2)}, u32[]{:S(2)}) collective-permute-start(f32[2,32,256]{2,1,0:T(8,128)} %get-tuple-element.18.after_ref.partial_hbm), channel_id=1, source_target_pairs={{0,1},{1,0},{2,3},{3,2},{4,5},{5,4},{6,7},{7,6},{8,9},{9,8},{10,11... | collective-permute-start | bytes 196616 | tf_op jit(solution)/shard_map/ppermute | solution.py:732
  29.2 0.8 %copy-start.3 = (f32[9,40,384]{2,1,0:T(8,128)}, f32[9,40,384]{2,1,0:T(8,128)S(1)}, u32[]{:S(2)}) copy-start(f32[9,40,384]{2,1,0:T(8,128)S(1)} %collective-permute-done.2.other_hbm) | copy-start | bytes 1658884
  36.1 0.6 %copy-start.5 = (f32[2,32,256]{2,1,0:T(8,128)}, f32[2,32,256]{2,1,0:T(8,128)S(1)}, u32[]{:S(2)}) copy-start(f32[2,32,256]{2,1,0:T(8,128)S(1)} %collective-permute-done.3.other_hbm) | copy-start | bytes 196612
  36.1 0.7 %copy-start.4 = (f32[16,16,128]{2,1,0:T(8,128)}, f32[16,16,128]{2,1,0:T(8,128)S(1)}, u32[]{:S(2)}) copy-start(f32[16,16,128]{2,1,0:T(8,128)S(1)} %all-to-all-done.1.edges_hbm) | copy-start | bytes 393220
  40.7 14.0 %all-to-all-start.2 = ((f32[16,8,128]{2,1,0:T(8,128)}), f32[16,8,128]{2,1,0:T(8,128)S(1)}, u32[]{:S(2)}, u32[]{:S(2)}) async-start(f32[16,8,128]{2,1,0:T(8,128)} %get-tuple-element.29), calls=%async_computation.2 | async-start | bytes 131072 | tf_op jit(solution)/shard_map/all_to_all | solution.py:770
